TPU v7x, 32 devices: a whole 2x2x4 slice. The times are simulated.
32 devices in a mesh: seq: 16 (over z, x, core), head: 2 (over y).
Axes of the slice: x: 2, y: 2, z: 4, core: 2. Of those that a mesh axis runs over, the one named last changes fastest.
Arguments:
- q_local: bfloat16 [8192, 2048], P('seq', 'head'), may hold values from -130 to 130
- k_local: bfloat16 [8192, 2048], P('seq', 'head'), may hold values from -6 to 6
- nearby_band_contents: bfloat16 [8192, 2048], P('seq', 'head'), may hold values from -6 to 6
- q_stride: bfloat16 [8192, 2048], P('seq', 'head'), may hold values from -130 to 130
- k_stride: bfloat16 [8192, 2048], P('seq', 'head'), may hold values from -6 to 6
- v_stride: bfloat16 [8192, 2048], P('seq', 'head'), may hold values from -6 to 6
- w_local: bfloat16 [2048, 4096], P('head'), may hold values from -0.09375 to 0.09375
- dilated_combiner: bfloat16 [2048, 4096], P('head'), may hold values from -0.09375 to 0.09375
Outputs:
- mixed: bfloat16 [8192, 4096], P(('seq', 'head'))
All inputs are finite; a program needn't handle non-finite values.
Results may differ from a plain program's by a relative error of at most 0.0056.
Values may be sent and summed in bfloat16 or wider, within the bound.
No kernel may reach another device: no remote copies, remote signals or barrier semaphores. Data moves between devices by JAX's collectives and lax.ppermute only.
A program may use at most 128 MiB of HBM per device.

v0:
```python
import jax
import jax.numpy as jnp
from jax import lax
from jax.sharding import PartitionSpec as P

HD = 128
STRIDE = 256
BAND = 256


def extended(block, sides, width):
    for axis, dim in sides:
        count = lax.axis_size(axis)
        forward = [(i, i + 1) for i in range(count - 1)]
        backward = [(target, source) for source, target in forward]
        low = lax.ppermute(
            lax.slice_in_dim(block, block.shape[dim] - width, None, axis=dim), axis, forward
        )
        high = lax.ppermute(lax.slice_in_dim(block, 0, width, axis=dim), axis, backward)
        block = jnp.concatenate([low, block, high], axis=dim)
    return block


def attend(requester_positions, key, value_vectors, valid):
    inverse_root_depth = requester_positions.shape[-1] ** (-0.5)
    similarity_grid = (
        jnp.einsum("suf,iuf->usi", requester_positions, key, preferred_element_type=jnp.float32)
        * inverse_root_depth
    )
    if valid is not None:
        similarity_grid = jnp.where(valid[None, :, :], similarity_grid, jnp.float32(-1e30))
    top = jnp.max(similarity_grid, axis=-1, keepdims=True)
    weight = jnp.exp(similarity_grid - top)
    if valid is not None:
        weight = jnp.where(valid[None, :, :], weight, jnp.float32(0.0))
    total = jnp.sum(weight, axis=-1)
    focus_probabilities = weight.astype(jnp.bfloat16)
    weighted_values = jnp.einsum(
        "xic,cxe->ixe", focus_probabilities, value_vectors, preferred_element_type=jnp.float32
    )
    return (weighted_values / jnp.transpose(total)[:, :, None]).astype(jnp.bfloat16)


def column_attend(parts):
    requester_positions, key, value_vectors = parts
    length, cols, heads, size = requester_positions.shape
    merged = attend(
        requester_positions.reshape(length, cols * heads, size),
        key.reshape(length, cols * heads, size),
        value_vectors.reshape(length, cols * heads, size),
        None,
    )
    return merged.reshape(length, cols, heads, size)


def body(
    q_local, k_local, nearby_band_contents, q_stride, k_stride, v_stride, w_local, dilated_combiner
):
    rows = q_local.shape[0]
    local_heads = q_local.shape[1] // HD
    stride_heads = q_stride.shape[1] // HD
    seqlen = rows * lax.axis_size("seq")
    offset = lax.axis_index("seq") * rows
    piled_together = jnp.stack([k_local, nearby_band_contents])
    padded = extended(piled_together, (("seq", 1),), BAND)
    local_q = q_local.reshape(rows, local_heads, HD)
    wide_k = padded[0].reshape(rows + 2 * BAND, local_heads, HD)
    wide_v = padded[1].reshape(rows + 2 * BAND, local_heads, HD)
    block = min(rows, 512)
    qpos = offset + 0 + jnp.arange(block, dtype=jnp.int32)
    kpos = offset + 0 - BAND + jnp.arange(block + 2 * BAND, dtype=jnp.int32)
    valid = (
        (jnp.abs(qpos[:, None] - kpos[None, :]) <= BAND)
        & (kpos[None, :] >= 0)
        & (kpos[None, :] < seqlen)
    )
    layer_results = attend(local_q, wide_k, wide_v, valid)
    attn_local = layer_results.reshape(rows, local_heads * HD)
    per_column = rows // STRIDE

    def shaped(array):
        return array.reshape(per_column, STRIDE, stride_heads, HD)

    column_out = column_attend(
        (
            lax.all_to_all(shaped(q_stride), "seq", split_axis=1, concat_axis=0, tiled=True),
            lax.all_to_all(shaped(k_stride), "seq", split_axis=1, concat_axis=0, tiled=True),
            lax.all_to_all(shaped(v_stride), "seq", split_axis=1, concat_axis=0, tiled=True),
        )
    )
    columnar_result = lax.all_to_all(column_out, "seq", split_axis=0, concat_axis=1, tiled=True)
    attn_stride = columnar_result.reshape(rows, stride_heads * HD)
    mixed = lax.psum_scatter(
        jnp.dot(attn_local, w_local, preferred_element_type=jnp.float32)
        + jnp.dot(attn_stride, dilated_combiner, preferred_element_type=jnp.float32),
        "head",
        scatter_dimension=0,
        tiled=True,
    )
    return mixed.astype(jnp.bfloat16)


def solution(mesh):
    in_specs = (
        P("seq", "head"),
        P("seq", "head"),
        P("seq", "head"),
        P("seq", "head"),
        P("seq", "head"),
        P("seq", "head"),
        P("head", None),
        P("head", None),
    )
    out_specs = P(("seq", "head"), None)
    return jax.shard_map(body, mesh=mesh, in_specs=in_specs, out_specs=out_specs, check_vma=False)
```

profile of v0, /device:TPU:0, one launch (start us, length us, event | category | flops | bytes accessed | tf_op | source)
XLA Modules:
  0.0 284.0 jit_solution(16026967623933582602)
XLA Ops:
  6.5 1.6 copy.71
  8.1 1.2 copy.52
  9.3 7.4 %all-to-all-start = ((bf16[2,256,8,128]{3,2,0,1:T(8,128)(2,1)}), bf16[2,256,8,128]{3,2,0,1:T(8,128)(2,1)S(1)}, u32[]{:S(2)}, u32[]{:S(2)}) async-start(bf16[2,256,8,128]{3,2,0,1:T(8,128)(2,1)} %copy.52), calls=%async_computation | async-start | bytes 2097152 | tf_op jit(solution)/shard_map/all_to_all | solution.py:86
  16.9 1.2 copy.55
  18.1 21.5 %all-to-all-done = bf16[2,256,8,128]{3,2,0,1:T(8,128)(2,1)S(1)} async-done(((bf16[2,256,8,128]{3,2,0,1:T(8,128)(2,1)}), bf16[2,256,8,128]{3,2,0,1:T(8,128)(2,1)S(1)}, u32[]{:S(2)}, u32[]{:S(2)}) %all-to-all-start) | async-done | bytes 1048608 | tf_op jit(solution)/shard_map/all_to_all | solution.py:86
  39.6 1.0 copy-done.2
  40.6 6.9 %all-to-all-start.1 = ((bf16[2,256,8,128]{3,2,0,1:T(8,128)(2,1)}), bf16[2,256,8,128]{3,2,0,1:T(8,128)(2,1)}, u32[]{:S(2)}, u32[]{:S(2)}) async-start(bf16[2,256,8,128]{3,2,0,1:T(8,128)(2,1)} %copy.55), calls=%async_computation.1 | async-start | bytes 2097152 | tf_op jit(solution)/shard_map/all_to_all | solution.py:87
  48.1 1.5 copy.48
  49.6 1.5 copy.73
  51.1 1.2 copy.58
  52.3 18.2 %all-to-all-done.1 = bf16[2,256,8,128]{3,2,0,1:T(8,128)(2,1)} async-done(((bf16[2,256,8,128]{3,2,0,1:T(8,128)(2,1)}), bf16[2,256,8,128]{3,2,0,1:T(8,128)(2,1)}, u32[]{:S(2)}, u32[]{:S(2)}) %all-to-all-start.1) | async-done | bytes 1048608 | tf_op jit(solution)/shard_map/all_to_all | solution.py:87
  70.5 6.9 %all-to-all-start.2 = ((bf16[2,256,8,128]{3,2,0,1:T(8,128)(2,1)}), bf16[2,256,8,128]{3,2,0,1:T(8,128)(2,1)}, u32[]{:S(2)}, u32[]{:S(2)}) async-start(bf16[2,256,8,128]{3,2,0,1:T(8,128)(2,1)} %copy.58), calls=%async_computation.2 | async-start | bytes 2097152 | tf_op jit(solution)/shard_map/all_to_all | solution.py:88
  77.4 1.4 fusion.18
  78.9 3.3 %collective-permute-start = (bf16[2,256,1024]{1,2,0:T(8,128)(2,1)}, bf16[2,256,1024]{1,2,0:T(8,128)(2,1)}, u32[]{:S(2)}, u32[]{:S(2)}) collective-permute-start(bf16[2,256,1024]{1,2,0:T(8,128)(2,1)} %get-tuple-element.7), channel_id=1, source_target_pairs={{0,2},{2,4},{4,6},{6,8},{8,10},{10,12},{12,14},{14,16},{16,18},{18... | collective-permute-start | bytes 3145736 | tf_op jit(solution)/shard_map/ppermute | solution.py:16
  82.1 1.3 collective-permute-start.1
  83.5 1.7 fusion.10
  85.1 2.0 collective-permute-done.1
  87.2 1.8 pad_maximum_fusion
  89.0 2.5 fusion.39
  91.5 1.0 copy.54
  92.6 2.3 copy.57
  94.8 5.6 %all-to-all-done.2 = bf16[2,256,8,128]{3,2,0,1:T(8,128)(2,1)} async-done(((bf16[2,256,8,128]{3,2,0,1:T(8,128)(2,1)}), bf16[2,256,8,128]{3,2,0,1:T(8,128)(2,1)}, u32[]{:S(2)}, u32[]{:S(2)}) %all-to-all-start.2) | async-done | bytes 1048608 | tf_op jit(solution)/shard_map/all_to_all | solution.py:88
  100.5 2.3 copy.60
  104.1 1.2 fusion.7
  105.4 1.4 copy.62
  106.7 26.8 %all-to-all-start.3 = ((bf16[32,16,8,128]{3,2,1,0:T(8,128)(2,1)}), bf16[32,16,8,128]{3,2,1,0:T(8,128)(2,1)S(1)}, u32[]{:S(2)}, u32[]{:S(2)}) async-start(bf16[32,16,8,128]{3,2,1,0:T(8,128)(2,1)} %copy.62), calls=%async_computation.3 | async-start | bytes 2097152 | tf_op jit(solution)/shard_map/all_to_all | solution.py:91
  133.8 11.9 %fusion.40 = (f32[8,512]{1,0:T(8,128)S(1)}, bf16[8,512,1024]{1,2,0:T(8,128)(2,1)}) fusion(pred[512,1024]{0,1:T(8,128)(4,1)S(1)} %copy-done.6, bf16[1024,8,128]{0,2,1:T(8,128)(2,1)} %bitcast.100, bf16[512,1024]{1,0:T(8,128)(2,1)S(1)} %copy-done), kind=kOutput, calls=%fused_computation.44 | convolution fusion | flops 1098908672 | bytes 12075008 | tf_op jit(solution)/shard_map/sub | solution.py:33
  145.6 5.3 %fusion.8 = bf16[512,8,128]{0,2,1:T(8,128)(2,1)S(1)} fusion(bf16[1024,8,128]{0,2,1:T(8,128)(2,1)} %bitcast.99, bf16[8,512,1024]{1,2,0:T(8,128)(2,1)} %get-tuple-element.10, f32[512,8]{0,1:T(8,128)S(1)} %bitcast.108), kind=kOutput, calls=%fused_computation.16 | convolution fusion | flops 1074790400 | bytes 11550720 | tf_op jit(solution)/shard_map/xic,cxe->ixe/dot_general | solution.py:38
  150.9 10.2 %fusion.45 = f32[512,4096]{1,0:T(8,128)} fusion(bf16[512,1024]{0,1:T(8,128)(2,1)S(1)} %bitcast.101, bf16[1024,4096]{1,0:T(8,128)(2,1)} %param.14), kind=kOutput, calls=%fused_computation.45 | convolution fusion | flops 4294967296 | bytes 17825792 | tf_op jit(solution)/shard_map/dot_general | solution.py:94
  161.2 11.4 %convolution_add_fusion = f32[512,4096]{1,0:T(8,128)} fusion(f32[512,4096]{1,0:T(8,128)} %fusion.45, bf16[1024,4096]{1,0:T(8,128)(2,1)} %param.15, bf16[64,8,8,128]{3,2,1,0:T(8,128)(2,1)S(1)} %bitcast.91), kind=kOutput, calls=%fused_computation.9 | convolution fusion | flops 4297064448 | bytes 26214400 | tf_op jit(solution)/shard_map/dot_general | solution.py:95
  172.6 100.7 %reduce-scatter.2.cloned.1.call-done = f32[256,4096]{1,0:T(8,128)} async-done(((f32[512,4096]{1,0:T(8,128)}), f32[256,4096]{1,0:T(8,128)}) %reduce-scatter.2.cloned.1.call-update) | async-done | bytes 4194320 | tf_op jit(solution)/shard_map/reduce_scatter | solution.py:93
  273.4 3.8 %convert_element_type.19 = bf16[256,4096]{1,0:T(8,128)(2,1)} convert(f32[256,4096]{1,0:T(8,128)} %reduce-scatter.2.cloned.1.call-done) | non-fusion elementwise | flops 1048576 | bytes 6291456 | tf_op jit(solution)/shard_map/convert_element_type | solution.py:100
  (25 shorter events, 2.5 us)
Async XLA Ops:
  6.5 127.2 %copy-start = (bf16[512,1024]{1,0:T(8,128)(2,1)S(1)}, bf16[512,1024]{1,0:T(8,128)(2,1)}, u32[]{:S(2)}) copy-start(bf16[512,1024]{1,0:T(8,128)(2,1)} %param.8) | copy-start | bytes 3145732
  8.1 8.5 %copy-start.4 = (bf16[512,1024]{1,0:T(8,128)(2,1)S(1)}, bf16[512,1024]{1,0:T(8,128)(2,1)}, u32[]{:S(2)}) copy-start(bf16[512,1024]{1,0:T(8,128)(2,1)} %param.12) | copy-start | bytes 3145732
  9.3 30.3 %all-to-all-start = ((bf16[2,256,8,128]{3,2,0,1:T(8,128)(2,1)}), bf16[2,256,8,128]{3,2,0,1:T(8,128)(2,1)S(1)}, u32[]{:S(2)}, u32[]{:S(2)}) async-start(bf16[2,256,8,128]{3,2,0,1:T(8,128)(2,1)} %copy.52), calls=%async_computation | async-start | bytes 2097152 | tf_op jit(solution)/shard_map/all_to_all | solution.py:86
  16.9 30.6 %copy-start.5 = (bf16[512,1024]{1,0:T(8,128)(2,1)S(1)}, bf16[512,1024]{1,0:T(8,128)(2,1)}, u32[]{:S(2)}) copy-start(bf16[512,1024]{1,0:T(8,128)(2,1)} %param.9) | copy-start | bytes 3145732
  39.6 1.0 copy-start.2
  40.6 29.9 %all-to-all-start.1 = ((bf16[2,256,8,128]{3,2,0,1:T(8,128)(2,1)}), bf16[2,256,8,128]{3,2,0,1:T(8,128)(2,1)}, u32[]{:S(2)}, u32[]{:S(2)}) async-start(bf16[2,256,8,128]{3,2,0,1:T(8,128)(2,1)} %copy.55), calls=%async_computation.1 | async-start | bytes 2097152 | tf_op jit(solution)/shard_map/all_to_all | solution.py:87
  70.5 30.0 %all-to-all-start.2 = ((bf16[2,256,8,128]{3,2,0,1:T(8,128)(2,1)}), bf16[2,256,8,128]{3,2,0,1:T(8,128)(2,1)}, u32[]{:S(2)}, u32[]{:S(2)}) async-start(bf16[2,256,8,128]{3,2,0,1:T(8,128)(2,1)} %copy.58), calls=%async_computation.2 | async-start | bytes 2097152 | tf_op jit(solution)/shard_map/all_to_all | solution.py:88
  78.9 6.3 %collective-permute-start = (bf16[2,256,1024]{1,2,0:T(8,128)(2,1)}, bf16[2,256,1024]{1,2,0:T(8,128)(2,1)}, u32[]{:S(2)}, u32[]{:S(2)}) collective-permute-start(bf16[2,256,1024]{1,2,0:T(8,128)(2,1)} %get-tuple-element.7), channel_id=1, source_target_pairs={{0,2},{2,4},{4,6},{6,8},{8,10},{10,12},{12,14},{14,16},{16,18},{18... | collective-permute-start | bytes 3145736 | tf_op jit(solution)/shard_map/ppermute | solution.py:16
  82.1 5.0 %collective-permute-start.1 = (bf16[2,256,1024]{1,2,0:T(8,128)(2,1)}, bf16[2,256,1024]{1,2,0:T(8,128)(2,1)}, u32[]{:S(2)}, u32[]{:S(2)}) collective-permute-start(bf16[2,256,1024]{1,2,0:T(8,128)(2,1)} %get-tuple-element.8), channel_id=1, source_target_pairs={{2,0},{4,2},{6,4},{8,6},{10,8},{12,10},{14,12},{16,14},{18,16},{20... | collective-permute-start | bytes 3145736 | tf_op jit(solution)/shard_map/ppermute | solution.py:19
  89.0 2.5 copy-start.3
  105.3 28.4 %copy-start.6 = (pred[512,1024]{0,1:T(8,128)(4,1)S(1)}, pred[512,1024]{0,1:T(8,128)(4,1)}, u32[]{:S(2)}) copy-start(pred[512,1024]{0,1:T(8,128)(4,1)} %fusion.10) | copy-start | bytes 1572868
  106.7 54.4 %all-to-all-start.3 = ((bf16[32,16,8,128]{3,2,1,0:T(8,128)(2,1)}), bf16[32,16,8,128]{3,2,1,0:T(8,128)(2,1)S(1)}, u32[]{:S(2)}, u32[]{:S(2)}) async-start(bf16[32,16,8,128]{3,2,1,0:T(8,128)(2,1)} %copy.62), calls=%async_computation.3 | async-start | bytes 2097152 | tf_op jit(solution)/shard_map/all_to_all | solution.py:91
  133.5 139.8 %reduce-scatter.2.cloned.1.call-start = ((), (), s32[]{:S(2)}) async-start(), calls=%async_computation.5 | async-start | bytes 12582912 | tf_op jit(solution)/shard_map/reduce_scatter | solution.py:93
  172.6 104.5 %copy-start.1 = (bf16[512,1024]{1,0:T(8,128)(2,1)S(1)}, bf16[512,1024]{1,0:T(8,128)(2,1)}, u32[]{:S(2)}) copy-start(bf16[512,1024]{1,0:T(8,128)(2,1)} %param.8) | copy-start | bytes 3145732
Sparse Core Ops, SparseCore 0:
  172.7 100.5 reduce-scatter.1
where the time goes:
time: 285 us; the launch traced here: 284 us
  waiting for transfers between devices  148 us (52%)
  starting transfers between devices  52.7 us (18%)
  matrix products  40.6 us (14%)
  local copies, waits for them, and re-layouts  19.5 us (7%)
  between operations  13.6 us (5%)
  other arithmetic  9.45 us (3%)
    reduce_scatter x1, waiting for transfers between devices, body(): lax.psum_scatter(jnp.dot(attn_local, w_local, preferred_element_type=jnp....  101 us
    all_to_all x1, starting transfers between devices, body(): lax.all_to_all(column_out, 'seq', split_axis=0, concat_axis=1, tiled=True)  26.8 us
    all_to_all x1, waiting for transfers between devices, body(): lax.all_to_all(shaped(q_stride), 'seq', split_axis=1, concat_axis=0, tile...  21.5 us
    all_to_all x1, waiting for transfers between devices, body(): lax.all_to_all(shaped(k_stride), 'seq', split_axis=1, concat_axis=0, tile...  18.2 us
    sub x1, matrix products, attend(): weight = jnp.exp(similarity_grid - top)  11.9 us
    dot_general x1, matrix products, body(): jnp.dot(attn_stride, dilated_combiner, preferred_element_type=jnp.float32)  11.4 us
    dot_general x1, matrix products, body(): jnp.dot(attn_local, w_local, preferred_element_type=jnp.float32)  10.2 us
    all_to_all x1, starting transfers between devices, body(): lax.all_to_all(shaped(q_stride), 'seq', split_axis=1, concat_axis=0, tile...  7.36 us
  transfers between devices with their start and end apart: 7, of which 5 were waited for; matrix products, arithmetic and copies ran while one was open for 16% of the time, Pallas kernels for 0%

commit v1 on v0

v1 whole, which is shorter than its diff:
```python
import functools

import jax
import jax.numpy as jnp
from jax import lax
from jax.experimental import pallas as pl
from jax.experimental.pallas import tpu as pltpu
from jax.sharding import PartitionSpec as P

HD = 128
STRIDE = 256
BAND = 256
PLANE = 4
TILE = 16
OFF = -1e30
SCALE = HD**-0.5
MIB = 1 << 20

VMEM = pl.BlockSpec(memory_space=pltpu.VMEM)
SMEM = pl.BlockSpec(memory_space=pltpu.SMEM)


def swap(array, axis, mask):
    count = lax.axis_size(axis)
    return lax.ppermute(array, axis, [(i, i ^ mask) for i in range(count)])


def scores(q, k):
    return lax.dot_general(q, k, (((1,), (1,)), ((), ())), preferred_element_type=jnp.float32)


def softmax_sum(score, v):
    top = jnp.max(score, axis=-1, keepdims=True)
    weight = jnp.exp(score - top)
    total = jnp.sum(weight, axis=-1, keepdims=True)
    out = jnp.dot(weight.astype(jnp.bfloat16), v, preferred_element_type=jnp.float32)
    return (out / total).astype(jnp.bfloat16)


def band_kernel(place_ref, q_ref, k_ref, v_ref, lows_ref, highs_ref, out_ref, k_all, v_all, bias):
    rows = q_ref.shape[0]
    step = BAND
    blocks = rows // step

    @pl.when(pl.program_id(0) == 0)
    def _():
        query = lax.broadcasted_iota(jnp.int32, (step, 3 * BAND), 0)
        key = lax.broadcasted_iota(jnp.int32, (step, 3 * BAND), 1)
        inside = (key >= query) & (key <= query + 2 * BAND)
        for b in range(blocks):
            there = inside
            if b == 0:
                there = there & ((key >= BAND) | (place_ref[0] > 0))
            if b == blocks - 1:
                there = there & ((key < 2 * BAND) | (place_ref[0] < place_ref[1] - 1))
            bias[b] = jnp.where(there, 0.0, OFF)

    for held, low, own, high in (
        (k_all, lows_ref.at[0], k_ref, highs_ref.at[0]),
        (v_all, lows_ref.at[1], v_ref, highs_ref.at[1]),
    ):
        held[:BAND] = low[...]
        held[BAND : BAND + rows] = own[...]
        held[BAND + rows :] = high[...]
    for b in range(blocks):
        at = slice(b * step, b * step + step)
        near = slice(b * step, b * step + 3 * BAND)
        score = scores(q_ref[at], k_all[near]) * SCALE + bias[b]
        out_ref[at] = softmax_sum(score, v_all[near])


def band_attention(place, q, k, v, lows, highs):
    rows, width = q.shape
    own = pl.BlockSpec((rows, HD), lambda h: (0, h))
    side = pl.BlockSpec((2, BAND, HD), lambda h: (0, 0, h))
    return pl.pallas_call(
        band_kernel,
        grid=(width // HD,),
        in_specs=[SMEM, own, own, own, side, side],
        out_specs=own,
        out_shape=jax.ShapeDtypeStruct(q.shape, q.dtype),
        scratch_shapes=[
            pltpu.VMEM((rows + 2 * BAND, HD), jnp.bfloat16),
            pltpu.VMEM((rows + 2 * BAND, HD), jnp.bfloat16),
            pltpu.VMEM((rows // BAND, BAND, 3 * BAND), jnp.float32),
        ],
        compiler_params=pltpu.CompilerParams(vmem_limit_bytes=24 * MIB),
        cost_estimate=pl.CostEstimate(
            flops=4 * rows * 3 * BAND * width,
            bytes_accessed=10 * rows * width,
            transcendentals=rows * 3 * BAND * width // HD,
        ),
        name="band_attention",
    )(place, q, k, v, lows, highs)


def column_kernel(planes, *refs):
    ins, outs = refs[:planes], refs[planes : 2 * planes]
    held, bias, result = refs[2 * planes :]
    length = held.shape[1]
    block = bias.shape[0]
    pieces = [(d, a, b, j) for d in range(planes) for a in (0, 1) for b in (0, 1) for j in (0, 1)]
    for i, (d, a, b, j) in enumerate(pieces):
        for t in range(3):
            held[t, i * TILE : (i + 1) * TILE] = ins[d][a, b, t, j]
    query = lax.broadcasted_iota(jnp.int32, bias.shape, 0)
    key = lax.broadcasted_iota(jnp.int32, bias.shape, 1)
    bias[...] = jnp.where((query & (TILE - 1)) == (key & (TILE - 1)), 0.0, OFF)

    @pl.loop(0, length // block)
    def _(step):
        at = pl.ds(pl.multiple_of(step * block, block), block)
        for h in range(held.shape[2] // HD):
            lanes = slice(h * HD, h * HD + HD)
            score = scores(held[0, at, lanes], held[1, :, lanes]) * SCALE + bias[...]
            result[at, lanes] = softmax_sum(score, held[2, :, lanes])

    for i, (d, a, b, j) in enumerate(pieces):
        outs[d][a, b, j] = result[i * TILE : (i + 1) * TILE]


def column_attention(slots):
    planes = len(slots)
    lanes = slots[0].shape[-1]
    length = planes * 8 * TILE
    block = min(length, 256)
    shape = jax.ShapeDtypeStruct((2, 2, 2, TILE, lanes), jnp.bfloat16)
    return pl.pallas_call(
        functools.partial(column_kernel, planes),
        in_specs=[VMEM] * planes,
        out_specs=[VMEM] * planes,
        out_shape=[shape] * planes,
        scratch_shapes=[
            pltpu.VMEM((3, length, lanes), jnp.bfloat16),
            pltpu.VMEM((block, length), jnp.float32),
            pltpu.VMEM((length, lanes), jnp.bfloat16),
        ],
        compiler_params=pltpu.CompilerParams(vmem_limit_bytes=40 * MIB),
        cost_estimate=pl.CostEstimate(
            flops=4 * length * length * lanes,
            bytes_accessed=8 * length * lanes,
            transcendentals=length * length * lanes // HD,
        ),
        name="column_attention",
    )(*slots)


def project_kernel(planes, place_ref, own_ref, got_ref, w_ref, local_ref, keep_ref, send_ref, rows_ref, sum_ref):
    lanes = own_ref.shape[-1]
    chunk = planes * TILE

    @pl.when(pl.program_id(0) == 0)
    def _():
        for c, held in enumerate((own_ref, got_ref)):
            for a in (0, 1):
                lane = ((place_ref[4] ^ c) * 2 + (place_ref[3] ^ a)) * lanes
                at = pl.ds(pl.multiple_of(lane, lanes), lanes)
                for d in range(planes):
                    for j in (0, 1):
                        row = j * chunk + (place_ref[2] ^ d) * TILE
                        rows_ref[pl.ds(pl.multiple_of(row, TILE), TILE), at] = held[a, d, j]

    total = jnp.dot(rows_ref[...], w_ref[...], preferred_element_type=jnp.float32)
    sum_ref[...] = total.reshape(sum_ref.shape) + local_ref[...]
    mine = place_ref[5]
    keep_ref[...] = sum_ref[mine]
    send_ref[...] = sum_ref[1 - mine].astype(jnp.bfloat16)


def project(place, own, got, w, local, index):
    planes = own.shape[1]
    chunk = planes * TILE
    depth, width = w.shape
    step = 512
    return pl.pallas_call(
        functools.partial(project_kernel, planes),
        grid=(width // step,),
        in_specs=[
            SMEM,
            pl.BlockSpec(own.shape, lambda n: (0,) * 5),
            pl.BlockSpec(own.shape, lambda n: (0,) * 5),
            pl.BlockSpec((depth, step), lambda n: (0, n)),
            pl.BlockSpec((2, chunk, step), lambda n: (0, index, n)),
        ],
        out_specs=[pl.BlockSpec((chunk, step), lambda n: (0, n))] * 2,
        out_shape=[
            jax.ShapeDtypeStruct((chunk, width), jnp.float32),
            jax.ShapeDtypeStruct((chunk, width), jnp.bfloat16),
        ],
        scratch_shapes=[
            pltpu.VMEM((2 * chunk, depth), jnp.bfloat16),
            pltpu.VMEM((2, chunk, step), jnp.float32),
        ],
        compiler_params=pltpu.CompilerParams(vmem_limit_bytes=24 * MIB),
        cost_estimate=pl.CostEstimate(
            flops=4 * chunk * depth * width,
            bytes_accessed=2 * depth * width + 14 * chunk * width,
            transcendentals=0,
        ),
        name="project",
    )(place, own, got, w, local)


def body(
    q_local, k_local, nearby_band_contents, q_stride, k_stride, v_stride, w_local, dilated_combiner
):
    rows, width = q_stride.shape
    per_column = rows // STRIDE
    count = lax.axis_size("seq")
    planes = count // PLANE
    s = lax.axis_index("seq")
    z, x, core = s // PLANE, (s // 2) % 2, s % 2
    mine = lax.axis_index("head")
    place = jnp.stack([s, jnp.int32(count), z, x, core, mine]).astype(jnp.int32)
    half, lanes = width // 2, width // PLANE
    chunk = TILE * planes
    chunks = STRIDE // chunk

    given = [lax.dynamic_slice_in_dim(a, (1 - core) * half, half, 1) for a in (q_stride, k_stride, v_stride)]
    held = [lax.dynamic_slice_in_dim(a, core * half, half, 1) for a in (q_stride, k_stride, v_stride)]
    got = swap(jnp.stack(given), "seq", 1)
    held = jnp.stack([jnp.stack(held), got]).reshape(2, 3, per_column, STRIDE, half)

    ends = jnp.stack([k_local, nearby_band_contents])
    lows = lax.ppermute(ends[:, rows - BAND :], "seq", [(i, i + 1) for i in range(count - 1)])
    highs = lax.ppermute(ends[:, :BAND], "seq", [(i + 1, i) for i in range(count - 1)])

    def over_x(i):
        part = held[:, :, :, i * chunk : (i + 1) * chunk]
        keep = lax.dynamic_slice_in_dim(part, x * lanes, lanes, 4)
        give = lax.dynamic_slice_in_dim(part, (1 - x) * lanes, lanes, 4)
        both = jnp.stack([keep, swap(give, "seq", 2)])
        return both.reshape(2, 2, 3, per_column, planes, TILE, lanes)

    def over_z(both):
        slots = []
        for d in range(planes):
            block = lax.dynamic_index_in_dim(both, z ^ d, 4, keepdims=False)
            slots.append(swap(block, "seq", d * PLANE) if d else block)
        return slots

    def back(outs):
        outs = [swap(o, "seq", d * PLANE) if d else o for d, o in enumerate(outs)]
        outs = jnp.stack(outs)
        outs = jnp.stack([outs[:, 0], swap(outs[:, 1], "seq", 2)])
        own, give = outs[:, :, 0], outs[:, :, 1]
        return own, swap(give, "seq", 1)

    attn_local = band_attention(place, q_local, k_local, nearby_band_contents, lows, highs)
    part_local = jnp.dot(attn_local, w_local, preferred_element_type=jnp.float32)
    part_local = part_local.reshape(per_column, STRIDE, -1)
    results = []
    for i in range(chunks):
        own, got = back(column_attention(over_z(over_x(i))))
        keep, send = project(place, own, got, dilated_combiner, part_local, i)
        results.append((keep + swap(send, "head", 1).astype(jnp.float32)).astype(jnp.bfloat16))
    return jnp.concatenate(results, 0)


def solution(mesh):
    in_specs = (
        P("seq", "head"),
        P("seq", "head"),
        P("seq", "head"),
        P("seq", "head"),
        P("seq", "head"),
        P("seq", "head"),
        P("head", None),
        P("head", None),
    )
    out_specs = P(("seq", "head"), None)
    return jax.shard_map(body, mesh=mesh, in_specs=in_specs, out_specs=out_specs, check_vma=False)
```

time: 285 us -> 215 us (0.75)
  waiting for transfers between devices: 148 us -> 64.4 us
  Pallas kernels: 0 us -> 34.8 us
  starting transfers between devices: 52.7 us -> 87 us
  matrix products: 40.6 us -> 6.89 us
  between operations: 13.6 us -> 0.37 us
  local copies, waits for them, and re-layouts: 19.5 us -> 10.3 us
    reduce_scatter x1 -> x0, waiting for transfers between devices: 101 us -> none  [body(): lax.psum_scatter(jnp.dot(attn_local, w_local, preferred_element_type=jnp....]
    ppermute x2 -> x43, starting transfers between devices: 4.54 us -> 87 us  [the longest x41 81.6 us: swap(): return lax.ppermute(array, axis, [(i, i ^ mask) for i in range(count)])]
    ppermute x2 -> x43, waiting for transfers between devices: 2.02 us -> 64.4 us  [the longest x41 64.4 us: swap(): return lax.ppermute(array, axis, [(i, i ^ mask) for i in range(count)])]
    all_to_all x4 -> x0, starting transfers between devices: 48 us -> none  [the longest x1 26.8 us: body(): lax.all_to_all(column_out, 'seq', split_axis=0, concat_axis=1, tiled=True)]
    all_to_all x4 -> x0, waiting for transfers between devices: 45.3 us -> none  [the longest x1 21.5 us: body(): lax.all_to_all(shaped(q_stride), 'seq', split_axis=1, concat_axis=0, tile...]
    pallas_call x0 -> x9, Pallas kernels: none -> 34.8 us  [the longest x4 17.5 us: project(): pl.pallas_call(functools.partial(project_kernel, planes), grid=(width //...]
    dot_general x4 -> x0, matrix products: 18.6 us -> none  [the longest x1 11.4 us: body(): jnp.dot(attn_stride, dilated_combiner, preferred_element_type=jnp.float32)]
    sub x1 -> x0, matrix products: 11.9 us -> none  [attend(): weight = jnp.exp(similarity_grid - top)]
  transfers between devices with their start and end apart: 7 -> 43, of which waited for: 5 -> 10; matrix products, arithmetic and copies ran while one was open for 16% -> 9% of each run, Pallas kernels for 0% -> 16%
where the time goes in v1:
time: 215 us; the launch traced here: 214 us
  starting transfers between devices  87 us (40%)
  waiting for transfers between devices  64.4 us (30%)
  Pallas kernels  34.8 us (16%)
  other arithmetic  10.6 us (5%)
  local copies, waits for them, and re-layouts  10.3 us (5%)
  matrix products  6.89 us (3%)
    ppermute x41, starting transfers between devices, swap(): return lax.ppermute(array, axis, [(i, i ^ mask) for i in range(count)])  81.6 us
    ppermute x41, waiting for transfers between devices, swap(): return lax.ppermute(array, axis, [(i, i ^ mask) for i in range(count)])  64.4 us
    pallas_call x4, Pallas kernels, project(): pl.pallas_call(functools.partial(project_kernel, planes), grid=(width //...  17.5 us
    pallas_call x1, Pallas kernels, band_attention(): pl.pallas_call(band_kernel, grid=(width // HD,), in_specs=[SMEM, own, own...  10.8 us
    dot_general x1, matrix products, body(): jnp.dot(attn_local, w_local, preferred_element_type=jnp.float32)  6.89 us
    pallas_call x4, Pallas kernels, column_attention(): pl.pallas_call(functools.partial(column_kernel, planes), in_specs=[VMEM]...  6.54 us
    dynamic_slice x2, local copies, waits for them, and re-layouts, body(): lax.dynamic_slice_in_dim(a, core * half, half, 1)  4.84 us
  transfers between devices with their start and end apart: 43, of which 10 were waited for; matrix products, arithmetic and copies ran while one was open for 9% of the time, Pallas kernels for 16%

profile of v1, /device:TPU:0, one launch (start us, length us, event | category | flops | bytes accessed | tf_op | source)
XLA Modules:
  0.0 214.3 jit_solution(10441249620993525096)
XLA Ops:
  0.0 2.1 constant_dynamic-slice_fusion.10
  2.1 2.8 %constant_dynamic-slice_fusion.8 = (bf16[512,512]{1,0:T(8,128)(2,1)}, bf16[1,512,512]{2,1,0:T(8,128)(2,1)S(1)}, bf16[1,512,512]{2,1,0:T(8,128)(2,1)S(1)}, bf16[512,512]{1,0:T(8,128)(2,1)}) fusion(bf16[512,1024]{1,0:T(8,128)(2,1)} %param.13, s32[]{:T(128)S(6)} %select_n.69, s32[]{:T(128)S(6)} %select_n.70, bf16[512,1024]{1,0:T(8,128)(2,1)} %param.12), kind=kLoop, calls=%fused_computation.122 | loop fusion | bytes 4194312 | tf_op jit(solution)/shard_map/dynamic_slice | solution.py:220
  9.5 4.1 %collective-permute-start.10 = (bf16[2,256,1024]{2,1,0:T(8,128)(2,1)}, bf16[2,256,1024]{2,1,0:T(8,128)(2,1)}, u32[]{:S(2)}, u32[]{:S(2)}) collective-permute-start(bf16[2,256,1024]{2,1,0:T(8,128)(2,1)} %get-tuple-element.58), channel_id=1, source_target_pairs={{0,2},{2,4},{4,6},{6,8},{8,10},{10,12},{12,14},{14,16},{16,18},{18... | collective-permute-start | bytes 3145736 | tf_op jit(solution)/shard_map/ppermute | solution.py:225
  13.5 2.0 pad_maximum_fusion
  24.4 12.2 %collective-permute-done.1 = bf16[2,3,2,64,256]{4,3,2,1,0:T(8,128)(2,1)} collective-permute-done((bf16[2,3,2,64,256]{4,3,2,1,0:T(8,128)(2,1)}, bf16[2,3,2,64,256]{4,3,2,1,0:T(8,128)(2,1)}, u32[]{:S(2)}, u32[]{:S(2)}) %collective-permute-start.1) | collective-permute-done | bytes 393248 | tf_op jit(solution)/shard_map/ppermute | solution.py:25
  38.5 6.6 %collective-permute-done.33 = bf16[2,3,2,64,256]{4,3,2,1,0:T(8,128)(2,1)} collective-permute-done((bf16[2,3,2,64,256]{4,3,2,1,0:T(8,128)(2,1)}, bf16[2,3,2,64,256]{4,3,2,1,0:T(8,128)(2,1)}, u32[]{:S(2)}, u32[]{:S(2)}) %collective-permute-start.33) | collective-permute-done | bytes 393248 | tf_op jit(solution)/shard_map/ppermute | solution.py:25
  45.0 20.4 %collective-permute-start.4 = (bf16[2,2,3,2,16,256]{5,4,3,2,1,0:T(8,128)(2,1)S(1)}, bf16[2,2,3,2,16,256]{5,4,3,2,1,0:T(8,128)(2,1)S(1)}, u32[]{:S(2)}, u32[]{:S(2)}) collective-permute-start(bf16[2,2,3,2,16,256]{5,4,3,2,1,0:T(8,128)(2,1)S(1)} %get-tuple-element.65), channel_id=1, source_target_pairs={{0,24},{2,26},{4,28},{6,30},{8,16},{10,18},{12,20},{14,22},{16,8},... | collective-permute-start | bytes 589832 | tf_op jit(solution)/shard_map/ppermute | solution.py:25
  65.4 3.2 %collective-permute-start.2 = (bf16[2,2,3,2,16,256]{5,4,3,2,1,0:T(8,128)(2,1)S(1)}, bf16[2,2,3,2,16,256]{5,4,3,2,1,0:T(8,128)(2,1)S(1)}, u32[]{:S(2)}, u32[]{:S(2)}) collective-permute-start(bf16[2,2,3,2,16,256]{5,4,3,2,1,0:T(8,128)(2,1)S(1)} %get-tuple-element.67), channel_id=1, source_target_pairs={{0,8},{2,10},{4,12},{6,14},{8,0},{10,2},{12,4},{14,6},{16,24},{18,... | collective-permute-start | bytes 589832 | tf_op jit(solution)/shard_map/ppermute | solution.py:25
  70.8 2.7 %collective-permute-start.3 = (bf16[2,2,3,2,16,256]{5,4,3,2,1,0:T(8,128)(2,1)S(1)}, bf16[2,2,3,2,16,256]{5,4,3,2,1,0:T(8,128)(2,1)S(1)}, u32[]{:S(2)}, u32[]{:S(2)}) collective-permute-start(bf16[2,2,3,2,16,256]{5,4,3,2,1,0:T(8,128)(2,1)S(1)} %get-tuple-element.68), channel_id=1, source_target_pairs={{0,16},{2,18},{4,20},{6,22},{8,24},{10,26},{12,28},{14,30},{16,0},... | collective-permute-start | bytes 589832 | tf_op jit(solution)/shard_map/ppermute | solution.py:25
  74.4 3.5 %collective-permute-start.35 = (bf16[2,2,3,2,16,256]{5,4,3,2,1,0:T(8,128)(2,1)S(1)}, bf16[2,2,3,2,16,256]{5,4,3,2,1,0:T(8,128)(2,1)S(1)}, u32[]{:S(2)}, u32[]{:S(2)}) collective-permute-start(bf16[2,2,3,2,16,256]{5,4,3,2,1,0:T(8,128)(2,1)S(1)} %get-tuple-element.86), channel_id=1, source_target_pairs={{0,16},{2,18},{4,20},{6,22},{8,24},{10,26},{12,28},{14,30},{16,0},... | collective-permute-start | bytes 589832 | tf_op jit(solution)/shard_map/ppermute | solution.py:25
  78.0 10.8 %band_attention.1 = bf16[512,1024]{1,0:T(8,128)(2,1)S(1)} custom-call(s32[6]{0:T(128)S(1)} %stack.183.place_ref, bf16[512,1024]{1,0:T(8,128)(2,1)S(1)} %copy-done.2, bf16[512,1024]{1,0:T(8,128)(2,1)S(1)} %copy-done, bf16[512,1024]{1,0:T(8,128)(2,1)S(1)} %copy-done.1, bf16[2,256,1024]{2,1,0:T(8,128)(2,1)} %collective-permute-done.10.lows_ref, ...), custom_call_target="tpu_custom_call" | custom-call | flops 1610612736 | bytes 5242880 | tf_op jit(solution)/shard_map/band_attention/pallas_call | solution.py:76
  89.5 12.1 %collective-permute-start.25 = (bf16[2,2,3,2,16,256]{5,4,3,2,1,0:T(8,128)(2,1)S(1)}, bf16[2,2,3,2,16,256]{5,4,3,2,1,0:T(8,128)(2,1)S(1)}, u32[]{:S(2)}, u32[]{:S(2)}) collective-permute-start(bf16[2,2,3,2,16,256]{5,4,3,2,1,0:T(8,128)(2,1)S(1)} %get-tuple-element.80), channel_id=1, source_target_pairs={{0,16},{2,18},{4,20},{6,22},{8,24},{10,26},{12,28},{14,30},{16,0},... | collective-permute-start | bytes 589832 | tf_op jit(solution)/shard_map/ppermute | solution.py:25
  101.6 1.8 collective-permute-start.16
  103.4 9.7 %collective-permute-done.35.refs_2_ = bf16[2,2,3,2,16,256]{5,4,3,2,1,0:T(8,128)(2,1)S(1)} collective-permute-done((bf16[2,2,3,2,16,256]{5,4,3,2,1,0:T(8,128)(2,1)S(1)}, bf16[2,2,3,2,16,256]{5,4,3,2,1,0:T(8,128)(2,1)S(1)}, u32[]{:S(2)}, u32[]{:S(2)}) %collective-permute-start.35) | collective-permute-done | bytes 196640 | tf_op jit(solution)/shard_map/ppermute | solution.py:25
  113.2 5.3 %collective-permute-start.15 = (bf16[2,2,3,2,16,256]{5,4,3,2,1,0:T(8,128)(2,1)S(1)}, bf16[2,2,3,2,16,256]{5,4,3,2,1,0:T(8,128)(2,1)S(1)}, u32[]{:S(2)}, u32[]{:S(2)}) collective-permute-start(bf16[2,2,3,2,16,256]{5,4,3,2,1,0:T(8,128)(2,1)S(1)} %get-tuple-element.74), channel_id=1, source_target_pairs={{0,16},{2,18},{4,20},{6,22},{8,24},{10,26},{12,28},{14,30},{16,0},... | collective-permute-start | bytes 589832 | tf_op jit(solution)/shard_map/ppermute | solution.py:25
  118.4 6.9 %fusion.46 = f32[512,4096]{1,0:T(8,128)S(1)} fusion(bf16[512,1024]{1,0:T(8,128)(2,1)S(1)} %band_attention.1, bf16[1024,4096]{1,0:T(8,128)(2,1)} %param.14), kind=kOutput, calls=%fused_computation.126 | convolution fusion | flops 4294967296 | bytes 17825792 | tf_op jit(solution)/shard_map/dot_general | solution.py:250
  127.1 2.4 %collective-permute-start.6 = (bf16[2,2,2,16,256]{4,3,2,1,0:T(8,128)(2,1)S(1)}, bf16[2,2,2,16,256]{4,3,2,1,0:T(8,128)(2,1)S(1)}, u32[]{:S(2)}, u32[]{:S(2)}) collective-permute-start(bf16[2,2,2,16,256]{4,3,2,1,0:T(8,128)(2,1)S(1)} %get-tuple-element.31), channel_id=1, source_target_pairs={{0,16},{2,18},{4,20},{6,22},{8,24},{10,26},{12,28},{14,30},{16,0},... | collective-permute-start | bytes 196616 | tf_op jit(solution)/shard_map/ppermute | solution.py:25
  129.5 2.0 collective-permute-start.7
  138.9 2.1 collective-permute-start.39
  143.4 2.1 collective-permute-start.29
  146.0 2.2 %collective-permute-start.18 = (bf16[2,2,2,16,256]{4,3,2,1,0:T(8,128)(2,1)S(1)}, bf16[2,2,2,16,256]{4,3,2,1,0:T(8,128)(2,1)S(1)}, u32[]{:S(2)}, u32[]{:S(2)}) collective-permute-start(bf16[2,2,2,16,256]{4,3,2,1,0:T(8,128)(2,1)S(1)} %get-tuple-element.37), channel_id=1, source_target_pairs={{0,16},{2,18},{4,20},{6,22},{8,24},{10,26},{12,28},{14,30},{16,0},... | collective-permute-start | bytes 196616 | tf_op jit(solution)/shard_map/ppermute | solution.py:25
  148.2 2.7 %collective-permute-start.19 = (bf16[2,2,2,16,256]{4,3,2,1,0:T(8,128)(2,1)S(1)}, bf16[2,2,2,16,256]{4,3,2,1,0:T(8,128)(2,1)S(1)}, u32[]{:S(2)}, u32[]{:S(2)}) collective-permute-start(bf16[2,2,2,16,256]{4,3,2,1,0:T(8,128)(2,1)S(1)} %get-tuple-element.38), channel_id=1, source_target_pairs={{0,24},{2,26},{4,28},{6,30},{8,16},{10,18},{12,20},{14,22},{16,8},... | collective-permute-start | bytes 196616 | tf_op jit(solution)/shard_map/ppermute | solution.py:25
  151.9 2.0 collective-permute-start.40
  155.4 2.8 %collective-permute-done.40 = bf16[4,2,2,16,256]{4,3,2,0,1:T(8,128)(2,1)S(1)} collective-permute-done((bf16[4,2,2,16,256]{4,3,2,0,1:T(8,128)(2,1)S(1)}, bf16[4,2,2,16,256]{4,3,2,0,1:T(8,128)(2,1)S(1)}, u32[]{:S(2)}, u32[]{:S(2)}) %collective-permute-start.40) | collective-permute-done | bytes 131104 | tf_op jit(solution)/shard_map/ppermute | solution.py:25
  158.4 1.7 collective-permute-start.20
  160.4 4.4 %project.7 = (f32[64,4096]{1,0:T(8,128)S(1)}, bf16[64,4096]{1,0:T(8,128)(2,1)S(1)}) custom-call(s32[6]{0:T(128)S(1)} %stack.183.place_ref, bf16[2,4,2,16,256]{4,3,2,1,0:T(8,128)(2,1)S(1)} %get-tuple-element.102.own_ref, bf16[2,4,2,16,256]{4,3,2,1,0:T(8,128)(2,1)S(1)} %collective-permute-done.41.got_ref, bf16[1024,4096]{1,0:T(8,128)(2,1)S(1)} %bitcast.121, ...), custom_call_target="tpu_custom_call" | custom-call | flops 1073741824 | bytes 12058624 | tf_op jit(solution)/shard_map/project/pallas_call | solution.py:175
  167.1 4.4 %project.6 = (f32[64,4096]{1,0:T(8,128)S(1)}, bf16[64,4096]{1,0:T(8,128)(2,1)S(1)}) custom-call(s32[6]{0:T(128)S(1)} %stack.183.place_ref, bf16[2,4,2,16,256]{4,3,2,1,0:T(8,128)(2,1)S(1)} %get-tuple-element.98.own_ref, bf16[2,4,2,16,256]{4,3,2,1,0:T(8,128)(2,1)S(1)} %collective-permute-done.31.got_ref, bf16[1024,4096]{1,0:T(8,128)(2,1)S(1)} %bitcast.121, ...), custom_call_target="tpu_custom_call" | custom-call | flops 1073741824 | bytes 12058624 | tf_op jit(solution)/shard_map/project/pallas_call | solution.py:175
  172.0 4.4 %project.5 = (f32[64,4096]{1,0:T(8,128)S(1)}, bf16[64,4096]{1,0:T(8,128)(2,1)S(1)}) custom-call(s32[6]{0:T(128)S(1)} %stack.183.place_ref, bf16[2,4,2,16,256]{4,3,2,1,0:T(8,128)(2,1)S(1)} %get-tuple-element.94.own_ref, bf16[2,4,2,16,256]{4,3,2,1,0:T(8,128)(2,1)S(1)} %collective-permute-done.21.got_ref, bf16[1024,4096]{1,0:T(8,128)(2,1)S(1)} %bitcast.121, ...), custom_call_target="tpu_custom_call" | custom-call | flops 1073741824 | bytes 12058624 | tf_op jit(solution)/shard_map/project/pallas_call | solution.py:175
  178.0 4.4 %project.4 = (f32[64,4096]{1,0:T(8,128)S(1)}, bf16[64,4096]{1,0:T(8,128)(2,1)S(1)}) custom-call(s32[6]{0:T(128)S(1)} %stack.183.place_ref, bf16[2,4,2,16,256]{4,3,2,1,0:T(8,128)(2,1)S(1)} %get-tuple-element.90.own_ref, bf16[2,4,2,16,256]{4,3,2,1,0:T(8,128)(2,1)S(1)} %collective-permute-done.9.got_ref, bf16[1024,4096]{1,0:T(8,128)(2,1)S(1)} %bitcast.121, ...), custom_call_target="tpu_custom_call" | custom-call | flops 1073741824 | bytes 12058624 | tf_op jit(solution)/shard_map/project/pallas_call | solution.py:175
  183.0 7.8 %collective-permute-done.32 = bf16[64,4096]{1,0:T(8,128)(2,1)S(1)} collective-permute-done((bf16[64,4096]{1,0:T(8,128)(2,1)S(1)}, bf16[64,4096]{1,0:T(8,128)(2,1)S(1)}, u32[]{:S(2)}, u32[]{:S(2)}) %collective-permute-start.32) | collective-permute-done | bytes 524320 | tf_op jit(solution)/shard_map/ppermute | solution.py:25
  190.9 11.1 %collective-permute-done.22 = bf16[64,4096]{1,0:T(8,128)(2,1)S(1)} collective-permute-done((bf16[64,4096]{1,0:T(8,128)(2,1)S(1)}, bf16[64,4096]{1,0:T(8,128)(2,1)S(1)}, u32[]{:S(2)}, u32[]{:S(2)}) %collective-permute-start.22) | collective-permute-done | bytes 524320 | tf_op jit(solution)/shard_map/ppermute | solution.py:25
  202.2 10.5 %collective-permute-done.12 = bf16[64,4096]{1,0:T(8,128)(2,1)S(1)} collective-permute-done((bf16[64,4096]{1,0:T(8,128)(2,1)S(1)}, bf16[64,4096]{1,0:T(8,128)(2,1)S(1)}, u32[]{:S(2)}, u32[]{:S(2)}) %collective-permute-start.12) | collective-permute-done | bytes 524320 | tf_op jit(solution)/shard_map/ppermute | solution.py:25
  (109 shorter events, 41.2 us)
Async XLA Ops:
  8.2 62.7 %collective-permute-start.11 = (bf16[2,256,1024]{2,1,0:T(8,128)(2,1)}, bf16[2,256,1024]{2,1,0:T(8,128)(2,1)S(1)}, u32[]{:S(2)}, u32[]{:S(2)}) collective-permute-start(bf16[2,256,1024]{2,1,0:T(8,128)(2,1)} %get-tuple-element.57), channel_id=1, source_target_pairs={{2,0},{4,2},{6,4},{8,6},{10,8},{12,10},{14,12},{16,14},{18,16},{20... | collective-permute-start | bytes 3145736 | tf_op jit(solution)/shard_map/ppermute | solution.py:226
  9.5 64.0 %collective-permute-start.10 = (bf16[2,256,1024]{2,1,0:T(8,128)(2,1)}, bf16[2,256,1024]{2,1,0:T(8,128)(2,1)}, u32[]{:S(2)}, u32[]{:S(2)}) collective-permute-start(bf16[2,256,1024]{2,1,0:T(8,128)(2,1)} %get-tuple-element.58), channel_id=1, source_target_pairs={{0,2},{2,4},{4,6},{6,8},{8,10},{10,12},{12,14},{14,16},{16,18},{18... | collective-permute-start | bytes 3145736 | tf_op jit(solution)/shard_map/ppermute | solution.py:225
  17.7 18.9 %collective-permute-start.1 = (bf16[2,3,2,64,256]{4,3,2,1,0:T(8,128)(2,1)}, bf16[2,3,2,64,256]{4,3,2,1,0:T(8,128)(2,1)}, u32[]{:S(2)}, u32[]{:S(2)}) collective-permute-start(bf16[2,3,2,64,256]{4,3,2,1,0:T(8,128)(2,1)} %get-tuple-element.69), channel_id=1, source_target_pairs={{0,4},{2,6},{4,0},{6,2},{8,12},{10,14},{12,8},{14,10},{16,20},{18,... | collective-permute-start | bytes 1179656 | tf_op jit(solution)/shard_map/ppermute | solution.py:25
  20.1 25.0 %collective-permute-start.33 = (bf16[2,3,2,64,256]{4,3,2,1,0:T(8,128)(2,1)}, bf16[2,3,2,64,256]{4,3,2,1,0:T(8,128)(2,1)}, u32[]{:S(2)}, u32[]{:S(2)}) collective-permute-start(bf16[2,3,2,64,256]{4,3,2,1,0:T(8,128)(2,1)} %get-tuple-element.87), channel_id=1, source_target_pairs={{0,4},{2,6},{4,0},{6,2},{8,12},{10,14},{12,8},{14,10},{16,20},{18,... | collective-permute-start | bytes 1179656 | tf_op jit(solution)/shard_map/ppermute | solution.py:25
  21.5 43.9 %collective-permute-start.23 = (bf16[2,3,2,64,256]{4,3,2,1,0:T(8,128)(2,1)}, bf16[2,3,2,64,256]{4,3,2,1,0:T(8,128)(2,1)}, u32[]{:S(2)}, u32[]{:S(2)}) collective-permute-start(bf16[2,3,2,64,256]{4,3,2,1,0:T(8,128)(2,1)} %get-tuple-element.81), channel_id=1, source_target_pairs={{0,4},{2,6},{4,0},{6,2},{8,12},{10,14},{12,8},{14,10},{16,20},{18,... | collective-permute-start | bytes 1179656 | tf_op jit(solution)/shard_map/ppermute | solution.py:25
  36.6 36.9 %collective-permute-start.13 = (bf16[2,3,2,64,256]{4,3,2,1,0:T(8,128)(2,1)S(1)}, bf16[2,3,2,64,256]{4,3,2,1,0:T(8,128)(2,1)S(1)}, u32[]{:S(2)}, u32[]{:S(2)}) collective-permute-start(bf16[2,3,2,64,256]{4,3,2,1,0:T(8,128)(2,1)S(1)} %get-tuple-element.75), channel_id=1, source_target_pairs={{0,4},{2,6},{4,0},{6,2},{8,12},{10,14},{12,8},{14,10},{16,20},{18,... | collective-permute-start | bytes 1179656 | tf_op jit(solution)/shard_map/ppermute | solution.py:25
  45.0 29.4 %collective-permute-start.4 = (bf16[2,2,3,2,16,256]{5,4,3,2,1,0:T(8,128)(2,1)S(1)}, bf16[2,2,3,2,16,256]{5,4,3,2,1,0:T(8,128)(2,1)S(1)}, u32[]{:S(2)}, u32[]{:S(2)}) collective-permute-start(bf16[2,2,3,2,16,256]{5,4,3,2,1,0:T(8,128)(2,1)S(1)} %get-tuple-element.65), channel_id=1, source_target_pairs={{0,24},{2,26},{4,28},{6,30},{8,16},{10,18},{12,20},{14,22},{16,8},... | collective-permute-start | bytes 589832 | tf_op jit(solution)/shard_map/ppermute | solution.py:25
  65.4 12.5 %collective-permute-start.2 = (bf16[2,2,3,2,16,256]{5,4,3,2,1,0:T(8,128)(2,1)S(1)}, bf16[2,2,3,2,16,256]{5,4,3,2,1,0:T(8,128)(2,1)S(1)}, u32[]{:S(2)}, u32[]{:S(2)}) collective-permute-start(bf16[2,2,3,2,16,256]{5,4,3,2,1,0:T(8,128)(2,1)S(1)} %get-tuple-element.67), channel_id=1, source_target_pairs={{0,8},{2,10},{4,12},{6,14},{8,0},{10,2},{12,4},{14,6},{16,24},{18,... | collective-permute-start | bytes 589832 | tf_op jit(solution)/shard_map/ppermute | solution.py:25
  70.8 18.0 %collective-permute-start.3 = (bf16[2,2,3,2,16,256]{5,4,3,2,1,0:T(8,128)(2,1)S(1)}, bf16[2,2,3,2,16,256]{5,4,3,2,1,0:T(8,128)(2,1)S(1)}, u32[]{:S(2)}, u32[]{:S(2)}) collective-permute-start(bf16[2,2,3,2,16,256]{5,4,3,2,1,0:T(8,128)(2,1)S(1)} %get-tuple-element.68), channel_id=1, source_target_pairs={{0,16},{2,18},{4,20},{6,22},{8,24},{10,26},{12,28},{14,30},{16,0},... | collective-permute-start | bytes 589832 | tf_op jit(solution)/shard_map/ppermute | solution.py:25
  73.5 16.0 %collective-permute-start.36 = (bf16[2,2,3,2,16,256]{5,4,3,2,1,0:T(8,128)(2,1)S(1)}, bf16[2,2,3,2,16,256]{5,4,3,2,1,0:T(8,128)(2,1)S(1)}, u32[]{:S(2)}, u32[]{:S(2)}) collective-permute-start(bf16[2,2,3,2,16,256]{5,4,3,2,1,0:T(8,128)(2,1)S(1)} %get-tuple-element.83), channel_id=1, source_target_pairs={{0,24},{2,26},{4,28},{6,30},{8,16},{10,18},{12,20},{14,22},{16,8},... | collective-permute-start | bytes 589832 | tf_op jit(solution)/shard_map/ppermute | solution.py:25
  73.5 28.1 %collective-permute-start.34 = (bf16[2,2,3,2,16,256]{5,4,3,2,1,0:T(8,128)(2,1)S(1)}, bf16[2,2,3,2,16,256]{5,4,3,2,1,0:T(8,128)(2,1)S(1)}, u32[]{:S(2)}, u32[]{:S(2)}) collective-permute-start(bf16[2,2,3,2,16,256]{5,4,3,2,1,0:T(8,128)(2,1)S(1)} %get-tuple-element.85), channel_id=1, source_target_pairs={{0,8},{2,10},{4,12},{6,14},{8,0},{10,2},{12,4},{14,6},{16,24},{18,... | collective-permute-start | bytes 589832 | tf_op jit(solution)/shard_map/ppermute | solution.py:25
  74.4 38.7 %collective-permute-start.35 = (bf16[2,2,3,2,16,256]{5,4,3,2,1,0:T(8,128)(2,1)S(1)}, bf16[2,2,3,2,16,256]{5,4,3,2,1,0:T(8,128)(2,1)S(1)}, u32[]{:S(2)}, u32[]{:S(2)}) collective-permute-start(bf16[2,2,3,2,16,256]{5,4,3,2,1,0:T(8,128)(2,1)S(1)} %get-tuple-element.86), channel_id=1, source_target_pairs={{0,16},{2,18},{4,20},{6,22},{8,24},{10,26},{12,28},{14,30},{16,0},... | collective-permute-start | bytes 589832 | tf_op jit(solution)/shard_map/ppermute | solution.py:25
  77.9 35.2 %collective-permute-start.26 = (bf16[2,2,3,2,16,256]{5,4,3,2,1,0:T(8,128)(2,1)S(1)}, bf16[2,2,3,2,16,256]{5,4,3,2,1,0:T(8,128)(2,1)S(1)}, u32[]{:S(2)}, u32[]{:S(2)}) collective-permute-start(bf16[2,2,3,2,16,256]{5,4,3,2,1,0:T(8,128)(2,1)S(1)} %get-tuple-element.77), channel_id=1, source_target_pairs={{0,24},{2,26},{4,28},{6,30},{8,16},{10,18},{12,20},{14,22},{16,8},... | collective-permute-start | bytes 589832 | tf_op jit(solution)/shard_map/ppermute | solution.py:25
  88.9 38.1 %collective-permute-start.24 = (bf16[2,2,3,2,16,256]{5,4,3,2,1,0:T(8,128)(2,1)S(1)}, bf16[2,2,3,2,16,256]{5,4,3,2,1,0:T(8,128)(2,1)S(1)}, u32[]{:S(2)}, u32[]{:S(2)}) collective-permute-start(bf16[2,2,3,2,16,256]{5,4,3,2,1,0:T(8,128)(2,1)S(1)} %get-tuple-element.79), channel_id=1, source_target_pairs={{0,8},{2,10},{4,12},{6,14},{8,0},{10,2},{12,4},{14,6},{16,24},{18,... | collective-permute-start | bytes 589832 | tf_op jit(solution)/shard_map/ppermute | solution.py:25
  89.5 37.6 %collective-permute-start.25 = (bf16[2,2,3,2,16,256]{5,4,3,2,1,0:T(8,128)(2,1)S(1)}, bf16[2,2,3,2,16,256]{5,4,3,2,1,0:T(8,128)(2,1)S(1)}, u32[]{:S(2)}, u32[]{:S(2)}) collective-permute-start(bf16[2,2,3,2,16,256]{5,4,3,2,1,0:T(8,128)(2,1)S(1)} %get-tuple-element.80), channel_id=1, source_target_pairs={{0,16},{2,18},{4,20},{6,22},{8,24},{10,26},{12,28},{14,30},{16,0},... | collective-permute-start | bytes 589832 | tf_op jit(solution)/shard_map/ppermute | solution.py:25
  101.6 27.9 %collective-permute-start.16 = (bf16[2,2,3,2,16,256]{5,4,3,2,1,0:T(8,128)(2,1)S(1)}, bf16[2,2,3,2,16,256]{5,4,3,2,1,0:T(8,128)(2,1)S(1)}, u32[]{:S(2)}, u32[]{:S(2)}) collective-permute-start(bf16[2,2,3,2,16,256]{5,4,3,2,1,0:T(8,128)(2,1)S(1)} %get-tuple-element.71), channel_id=1, source_target_pairs={{0,24},{2,26},{4,28},{6,30},{8,16},{10,18},{12,20},{14,22},{16,8},... | collective-permute-start | bytes 589832 | tf_op jit(solution)/shard_map/ppermute | solution.py:25
  113.1 21.6 %collective-permute-start.14 = (bf16[2,2,3,2,16,256]{5,4,3,2,1,0:T(8,128)(2,1)S(1)}, bf16[2,2,3,2,16,256]{5,4,3,2,1,0:T(8,128)(2,1)S(1)}, u32[]{:S(2)}, u32[]{:S(2)}) collective-permute-start(bf16[2,2,3,2,16,256]{5,4,3,2,1,0:T(8,128)(2,1)S(1)} %get-tuple-element.73), channel_id=1, source_target_pairs={{0,8},{2,10},{4,12},{6,14},{8,0},{10,2},{12,4},{14,6},{16,24},{18,... | collective-permute-start | bytes 589832 | tf_op jit(solution)/shard_map/ppermute | solution.py:25
  113.2 23.9 %collective-permute-start.15 = (bf16[2,2,3,2,16,256]{5,4,3,2,1,0:T(8,128)(2,1)S(1)}, bf16[2,2,3,2,16,256]{5,4,3,2,1,0:T(8,128)(2,1)S(1)}, u32[]{:S(2)}, u32[]{:S(2)}) collective-permute-start(bf16[2,2,3,2,16,256]{5,4,3,2,1,0:T(8,128)(2,1)S(1)} %get-tuple-element.74), channel_id=1, source_target_pairs={{0,16},{2,18},{4,20},{6,22},{8,24},{10,26},{12,28},{14,30},{16,0},... | collective-permute-start | bytes 589832 | tf_op jit(solution)/shard_map/ppermute | solution.py:25
  127.0 11.9 %collective-permute-start.5 = (bf16[2,2,2,16,256]{4,3,2,1,0:T(8,128)(2,1)S(1)}, bf16[2,2,2,16,256]{4,3,2,1,0:T(8,128)(2,1)S(1)}, u32[]{:S(2)}, u32[]{:S(2)}) collective-permute-start(bf16[2,2,2,16,256]{4,3,2,1,0:T(8,128)(2,1)S(1)} %get-tuple-element.30), channel_id=1, source_target_pairs={{0,8},{2,10},{4,12},{6,14},{8,0},{10,2},{12,4},{14,6},{16,24},{18,... | collective-permute-start | bytes 196616 | tf_op jit(solution)/shard_map/ppermute | solution.py:25
  127.1 13.8 %collective-permute-start.6 = (bf16[2,2,2,16,256]{4,3,2,1,0:T(8,128)(2,1)S(1)}, bf16[2,2,2,16,256]{4,3,2,1,0:T(8,128)(2,1)S(1)}, u32[]{:S(2)}, u32[]{:S(2)}) collective-permute-start(bf16[2,2,2,16,256]{4,3,2,1,0:T(8,128)(2,1)S(1)} %get-tuple-element.31), channel_id=1, source_target_pairs={{0,16},{2,18},{4,20},{6,22},{8,24},{10,26},{12,28},{14,30},{16,0},... | collective-permute-start | bytes 196616 | tf_op jit(solution)/shard_map/ppermute | solution.py:25
  129.5 12.8 %collective-permute-start.7 = (bf16[2,2,2,16,256]{4,3,2,1,0:T(8,128)(2,1)S(1)}, bf16[2,2,2,16,256]{4,3,2,1,0:T(8,128)(2,1)S(1)}, u32[]{:S(2)}, u32[]{:S(2)}) collective-permute-start(bf16[2,2,2,16,256]{4,3,2,1,0:T(8,128)(2,1)S(1)} %get-tuple-element.32), channel_id=1, source_target_pairs={{0,24},{2,26},{4,28},{6,30},{8,16},{10,18},{12,20},{14,22},{16,8},... | collective-permute-start | bytes 196616 | tf_op jit(solution)/shard_map/ppermute | solution.py:25
  134.8 8.6 %collective-permute-start.37 = (bf16[2,2,2,16,256]{4,3,2,1,0:T(8,128)(2,1)S(1)}, bf16[2,2,2,16,256]{4,3,2,1,0:T(8,128)(2,1)S(1)}, u32[]{:S(2)}, u32[]{:S(2)}) collective-permute-start(bf16[2,2,2,16,256]{4,3,2,1,0:T(8,128)(2,1)S(1)} %get-tuple-element.48), channel_id=1, source_target_pairs={{0,8},{2,10},{4,12},{6,14},{8,0},{10,2},{12,4},{14,6},{16,24},{18,... | collective-permute-start | bytes 196616 | tf_op jit(solution)/shard_map/ppermute | solution.py:25
  142.3 9.6 %collective-permute-start.28 = (bf16[2,2,2,16,256]{4,3,2,1,0:T(8,128)(2,1)S(1)}, bf16[2,2,2,16,256]{4,3,2,1,0:T(8,128)(2,1)S(1)}, u32[]{:S(2)}, u32[]{:S(2)}) collective-permute-start(bf16[2,2,2,16,256]{4,3,2,1,0:T(8,128)(2,1)S(1)} %get-tuple-element.43), channel_id=1, source_target_pairs={{0,16},{2,18},{4,20},{6,22},{8,24},{10,26},{12,28},{14,30},{16,0},... | collective-permute-start | bytes 196616 | tf_op jit(solution)/shard_map/ppermute | solution.py:25
  143.4 8.5 %collective-permute-start.29 = (bf16[2,2,2,16,256]{4,3,2,1,0:T(8,128)(2,1)S(1)}, bf16[2,2,2,16,256]{4,3,2,1,0:T(8,128)(2,1)S(1)}, u32[]{:S(2)}, u32[]{:S(2)}) collective-permute-start(bf16[2,2,2,16,256]{4,3,2,1,0:T(8,128)(2,1)S(1)} %get-tuple-element.44), channel_id=1, source_target_pairs={{0,24},{2,26},{4,28},{6,30},{8,16},{10,18},{12,20},{14,22},{16,8},... | collective-permute-start | bytes 196616 | tf_op jit(solution)/shard_map/ppermute | solution.py:25
  145.5 8.5 %collective-permute-start.17 = (bf16[2,2,2,16,256]{4,3,2,1,0:T(8,128)(2,1)S(1)}, bf16[2,2,2,16,256]{4,3,2,1,0:T(8,128)(2,1)S(1)}, u32[]{:S(2)}, u32[]{:S(2)}) collective-permute-start(bf16[2,2,2,16,256]{4,3,2,1,0:T(8,128)(2,1)S(1)} %get-tuple-element.36), channel_id=1, source_target_pairs={{0,8},{2,10},{4,12},{6,14},{8,0},{10,2},{12,4},{14,6},{16,24},{18,... | collective-permute-start | bytes 196616 | tf_op jit(solution)/shard_map/ppermute | solution.py:25
  146.0 9.4 %collective-permute-start.18 = (bf16[2,2,2,16,256]{4,3,2,1,0:T(8,128)(2,1)S(1)}, bf16[2,2,2,16,256]{4,3,2,1,0:T(8,128)(2,1)S(1)}, u32[]{:S(2)}, u32[]{:S(2)}) collective-permute-start(bf16[2,2,2,16,256]{4,3,2,1,0:T(8,128)(2,1)S(1)} %get-tuple-element.37), channel_id=1, source_target_pairs={{0,16},{2,18},{4,20},{6,22},{8,24},{10,26},{12,28},{14,30},{16,0},... | collective-permute-start | bytes 196616 | tf_op jit(solution)/shard_map/ppermute | solution.py:25
  151.9 14.6 %collective-permute-start.8 = (bf16[4,2,2,16,256]{4,3,2,0,1:T(8,128)(2,1)S(1)}, bf16[4,2,2,16,256]{4,3,2,0,1:T(8,128)(2,1)S(1)}, u32[]{:S(2)}, u32[]{:S(2)}) collective-permute-start(bf16[4,2,2,16,256]{4,3,2,0,1:T(8,128)(2,1)S(1)} %get-tuple-element.91), channel_id=1, source_target_pairs={{0,4},{2,6},{4,0},{6,2},{8,12},{10,14},{12,8},{14,10},{16,20},{18,... | collective-permute-start | bytes 393224 | tf_op jit(solution)/shard_map/ppermute | solution.py:25
  164.8 18.1 %collective-permute-start.42 = (bf16[64,4096]{1,0:T(8,128)(2,1)S(1)}, bf16[64,4096]{1,0:T(8,128)(2,1)S(1)}, u32[]{:S(2)}, u32[]{:S(2)}) collective-permute-start(bf16[64,4096]{1,0:T(8,128)(2,1)S(1)} %get-tuple-element.52), channel_id=1, source_target_pairs={{0,1},{1,0},{2,3},{3,2},{4,5},{5,4},{6,7},{7,6},{8,9},{9,8},{10,11... | collective-permute-start | bytes 1572872 | tf_op jit(solution)/shard_map/ppermute | solution.py:25
  166.5 11.5 %collective-permute-start.9 = (bf16[2,4,2,16,256]{4,3,2,1,0:T(8,128)(2,1)S(1)}, bf16[2,4,2,16,256]{4,3,2,1,0:T(8,128)(2,1)S(1)}, u32[]{:S(2)}, u32[]{:S(2)}) collective-permute-start(bf16[2,4,2,16,256]{4,3,2,1,0:T(8,128)(2,1)S(1)} %get-tuple-element.89), channel_id=1, source_target_pairs={{0,2},{2,0},{4,6},{6,4},{8,10},{10,8},{12,14},{14,12},{16,18},{18,... | collective-permute-start | bytes 393224 | tf_op jit(solution)/shard_map/ppermute | solution.py:25
  171.5 19.4 %collective-permute-start.32 = (bf16[64,4096]{1,0:T(8,128)(2,1)S(1)}, bf16[64,4096]{1,0:T(8,128)(2,1)S(1)}, u32[]{:S(2)}, u32[]{:S(2)}) collective-permute-start(bf16[64,4096]{1,0:T(8,128)(2,1)S(1)} %get-tuple-element.46), channel_id=1, source_target_pairs={{0,1},{1,0},{2,3},{3,2},{4,5},{5,4},{6,7},{7,6},{8,9},{9,8},{10,11... | collective-permute-start | bytes 1572872 | tf_op jit(solution)/shard_map/ppermute | solution.py:25
  176.4 25.7 %collective-permute-start.22 = (bf16[64,4096]{1,0:T(8,128)(2,1)S(1)}, bf16[64,4096]{1,0:T(8,128)(2,1)S(1)}, u32[]{:S(2)}, u32[]{:S(2)}) collective-permute-start(bf16[64,4096]{1,0:T(8,128)(2,1)S(1)} %get-tuple-element.40), channel_id=1, source_target_pairs={{0,1},{1,0},{2,3},{3,2},{4,5},{5,4},{6,7},{7,6},{8,9},{9,8},{10,11... | collective-permute-start | bytes 1572872 | tf_op jit(solution)/shard_map/ppermute | solution.py:25
  182.4 30.3 %collective-permute-start.12 = (bf16[64,4096]{1,0:T(8,128)(2,1)S(1)}, bf16[64,4096]{1,0:T(8,128)(2,1)S(1)}, u32[]{:S(2)}, u32[]{:S(2)}) collective-permute-start(bf16[64,4096]{1,0:T(8,128)(2,1)S(1)} %get-tuple-element.34), channel_id=1, source_target_pairs={{0,1},{1,0},{2,3},{3,2},{4,5},{5,4},{6,7},{7,6},{8,9},{9,8},{10,11... | collective-permute-start | bytes 1572872 | tf_op jit(solution)/shard_map/ppermute | solution.py:25
  (17 other events, 277.4 us)

commit v2 on v1

v2 whole, which is shorter than its diff:
```python
import functools

import jax
import jax.numpy as jnp
from jax import lax
from jax.experimental import pallas as pl
from jax.experimental.pallas import tpu as pltpu
from jax.sharding import PartitionSpec as P

HD = 128
STRIDE = 256
BAND = 256
PLANE = 4
TILE = 16
OFF = -1e30
SCALE = HD**-0.5
LOG2E = 1.4426950408889634
MIB = 1 << 20
FREE = pl.CostEstimate(flops=0, bytes_accessed=0, transcendentals=0)

VMEM = pl.BlockSpec(memory_space=pltpu.VMEM)
SMEM = pl.BlockSpec(memory_space=pltpu.SMEM)
ANY = pl.BlockSpec(memory_space=pl.ANY)


def swap(array, axis, mask):
    count = lax.axis_size(axis)
    return lax.ppermute(array, axis, [(i, i ^ mask) for i in range(count)])


def scores(q, k):
    return lax.dot_general(q, k, (((1,), (1,)), ((), ())), preferred_element_type=jnp.float32)


def softmax_sum(score, v):
    top = jnp.max(score, axis=-1, keepdims=True)
    weight = jnp.exp2((score - top) * (SCALE * LOG2E))
    total = jnp.sum(weight, axis=-1, keepdims=True)
    out = jnp.dot(weight.astype(jnp.bfloat16), v, preferred_element_type=jnp.float32)
    return (out / total).astype(jnp.bfloat16)


def band_kernel(place_ref, q_ref, k_ref, v_ref, lows_ref, highs_ref, *refs):
    out_ref, k_all, v_all, bias = refs[-4:]
    rows = q_ref.shape[0]
    step = BAND
    blocks = rows // step

    @pl.when(pl.program_id(0) == 0)
    def _():
        query = lax.broadcasted_iota(jnp.int32, (step, BAND), 0)
        key = lax.broadcasted_iota(jnp.int32, (step, BAND), 1)
        for b in range(blocks):
            before = key >= query
            after = key <= query
            if b == 0:
                before = before & (place_ref[0] > 0)
            if b == blocks - 1:
                after = after & (place_ref[0] < place_ref[1] - 1)
            bias[b, 0] = jnp.where(before, 0.0, OFF)
            bias[b, 1] = jnp.where(after, 0.0, OFF)

    for held, low, own, high in (
        (k_all, lows_ref.at[0], k_ref, highs_ref.at[0]),
        (v_all, lows_ref.at[1], v_ref, highs_ref.at[1]),
    ):
        held[:BAND] = low[...]
        held[BAND : BAND + rows] = own[...]
        held[BAND + rows :] = high[...]
    for b in range(blocks):
        at = slice(b * step, b * step + step)
        near = slice(b * step, b * step + 3 * BAND)
        score = scores(q_ref[at], k_all[near])
        score = jnp.concatenate(
            [
                score[:, :BAND] + bias[b, 0],
                score[:, BAND : 2 * BAND],
                score[:, 2 * BAND :] + bias[b, 1],
            ],
            axis=1,
        )
        out_ref[at] = softmax_sum(score, v_all[near])


def band_attention(place, q, k, v, lows, highs, after=()):
    rows, width = q.shape
    own = pl.BlockSpec((rows, HD), lambda h: (0, h))
    side = pl.BlockSpec((2, BAND, HD), lambda h: (0, 0, h))
    return pl.pallas_call(
        band_kernel,
        grid=(width // HD,),
        in_specs=[SMEM, own, own, own, side, side] + [ANY] * len(after),
        out_specs=own,
        out_shape=jax.ShapeDtypeStruct(q.shape, q.dtype),
        scratch_shapes=[
            pltpu.VMEM((rows + 2 * BAND, HD), jnp.bfloat16),
            pltpu.VMEM((rows + 2 * BAND, HD), jnp.bfloat16),
            pltpu.VMEM((rows // BAND, 2, BAND, BAND), jnp.float32),
        ],
        compiler_params=pltpu.CompilerParams(vmem_limit_bytes=62 * MIB),
        cost_estimate=FREE,
        name="band_attention",
    )(place, q, k, v, lows, highs, *after)


def add_kernel(keep_ref, got_ref, *refs):
    refs[-1][...] = (keep_ref[...] + got_ref[...].astype(jnp.float32)).astype(jnp.bfloat16)


def add_into(out, keep, got, first, rows, after=()):
    chunk, width = keep.shape
    step = width
    spec = pl.BlockSpec((chunk, step), lambda n: (0, n))
    held = () if out is None else (out,)
    return pl.pallas_call(
        add_kernel,
        grid=(width // step,),
        in_specs=[spec, spec] + [ANY] * (len(held) + len(after)),
        out_specs=pl.BlockSpec((chunk, step), lambda n: (first // chunk, n)),
        out_shape=jax.ShapeDtypeStruct((rows, width), jnp.bfloat16),
        input_output_aliases={2: 0} if held else {},
        compiler_params=pltpu.CompilerParams(vmem_limit_bytes=62 * MIB),
        cost_estimate=FREE,
        name="add_into",
    )(keep, got, *held, *after)


def ends_kernel(k_ref, v_ref, *refs):
    lows_ref, highs_ref = refs[-2:]
    for t, held in enumerate((k_ref, v_ref)):
        highs_ref[t] = held[:BAND]
        lows_ref[t] = held[held.shape[0] - BAND :]


def ends(k, v, after=()):
    shape = jax.ShapeDtypeStruct((2, BAND, k.shape[1]), k.dtype)
    return pl.pallas_call(
        ends_kernel,
        grid=(1,),
        in_specs=[pl.BlockSpec(k.shape, lambda n: (0, 0))] * 2 + [ANY] * len(after),
        out_specs=[pl.BlockSpec(shape.shape, lambda n: (0, 0, 0))] * 2,
        out_shape=[shape] * 2,
        compiler_params=pltpu.CompilerParams(vmem_limit_bytes=62 * MIB),
        cost_estimate=FREE,
        name="ends",
    )(k, v, *after)


def pack_kernel(q_ref, k_ref, v_ref, *refs):
    out_ref = refs[-1]
    per_column, tile, _ = q_ref.shape
    lanes = out_ref.shape[-1]
    ahead = out_ref.shape[1] - 3 * per_column * tile
    for p in range(PLANE):
        for t, held in enumerate((q_ref, k_ref, v_ref)):
            for j in range(per_column):
                at = ahead + (t * per_column + j) * tile
                out_ref[p, at : at + tile] = held[j, :, p * lanes : (p + 1) * lanes]


def pack(arrays, first, tile, ahead, planes, after=()):
    rows, width = arrays[0].shape
    per_column = rows // STRIDE
    lanes = width // PLANE
    views = [a.reshape(per_column, STRIDE, width) for a in arrays]
    spec = pl.BlockSpec((per_column, tile, width), lambda n: (0, first // tile + n, 0))
    shape = (planes * PLANE, ahead + 3 * per_column * tile, lanes)
    return pl.pallas_call(
        pack_kernel,
        grid=(planes,),
        in_specs=[spec] * 3 + [ANY] * len(after),
        out_specs=pl.BlockSpec((PLANE,) + shape[1:], lambda n: (n, 0, 0)),
        out_shape=jax.ShapeDtypeStruct(shape, jnp.bfloat16),
        compiler_params=pltpu.CompilerParams(vmem_limit_bytes=62 * MIB),
        cost_estimate=FREE,
        name="pack",
    )(*views, *after)


def column_kernel(tile, ahead, in_ref, *refs):
    out_ref, held, bias, result = refs[-4:]
    count = in_ref.shape[0]
    per_column = out_ref.shape[1] // tile
    length = held.shape[1]
    block = bias.shape[0]

    @pl.when(pl.program_id(0) == 0)
    def _():
        query = lax.broadcasted_iota(jnp.int32, bias.shape, 0)
        key = lax.broadcasted_iota(jnp.int32, bias.shape, 1)
        bias[...] = jnp.where((query & (TILE - 1)) == (key & (TILE - 1)), 0.0, OFF)

    for part in range(tile // TILE):
        for s in range(count):
            for j in range(per_column):
                at = (s * per_column + j) * TILE
                for t in range(3):
                    row = ahead + (t * per_column + j) * tile + part * TILE
                    held[t, at : at + TILE] = in_ref[s, row : row + TILE]

        @pl.loop(0, length // block)
        def _(step):
            at = pl.ds(pl.multiple_of(step * block, block), block)
            score = scores(held[0, at], held[1]) + bias[...]
            result[at] = softmax_sum(score, held[2])

        for s in range(count):
            for j in range(per_column):
                at = (s * per_column + j) * TILE
                row = j * tile + part * TILE
                out_ref[s, row : row + TILE] = result[at : at + TILE]


def column_attention(got, ahead, tile, per_column, into, after=()):
    count, rows, lanes = got.shape
    length = count * per_column * TILE
    block = min(length, 256)
    held = () if into is None else (into,)
    shape = (count, per_column * tile, lanes) if into is None else into.shape
    return pl.pallas_call(
        functools.partial(column_kernel, tile, ahead),
        grid=(lanes // HD,),
        in_specs=[pl.BlockSpec((count, rows, HD), lambda h: (0, 0, h))]
        + [ANY] * (len(held) + len(after)),
        out_specs=pl.BlockSpec((count, per_column * tile, HD), lambda h: (0, 0, h)),
        out_shape=jax.ShapeDtypeStruct(shape, jnp.bfloat16),
        input_output_aliases={1: 0} if held else {},
        scratch_shapes=[
            pltpu.VMEM((3, length, HD), jnp.bfloat16),
            pltpu.VMEM((block, length), jnp.float32),
            pltpu.VMEM((length, HD), jnp.bfloat16),
        ],
        compiler_params=pltpu.CompilerParams(vmem_limit_bytes=62 * MIB),
        cost_estimate=FREE,
        name="column_attention",
    )(got, *held, *after)


def stream(step, w_ref, held, sems):
    width = held.shape[2]

    def block(n):
        columns = pl.ds(n * width, width)
        return pltpu.make_async_copy(w_ref.at[:, columns], held.at[n], sems.at[n])

    @pl.when(step == 0)
    def _():
        for n in range(held.shape[0]):
            block(n).start()

    for n in range(held.shape[0]):

        @pl.when(step == n)
        def _():
            block(n).wait()


def stream_scratch(depth, width, step):
    return [
        pltpu.VMEM((width // step, depth, step), jnp.bfloat16),
        pltpu.SemaphoreType.DMA((width // step,)),
    ]


def project_kernel(tile, mine_ref, w_ref, local_ref, in_ref, *refs):
    keep_ref, send_ref, rows_ref, sum_ref, held, sems = refs[-6:]
    stream(pl.program_id(0), w_ref, held, sems)

    @pl.when(pl.program_id(0) == 0)
    def _():
        count, rows, lanes = in_ref.shape
        chunk = tile * (count // PLANE)
        for s in range(count):
            lane = s % PLANE * lanes
            for j in range(rows // tile):
                row = j * chunk + s // PLANE * tile
                part = in_ref[s, j * tile : (j + 1) * tile]
                rows_ref[row : row + tile, lane : lane + lanes] = part

    w = held[pl.program_id(0)]
    total = jnp.dot(rows_ref[...], w, preferred_element_type=jnp.float32)
    sum_ref[...] = total.reshape(sum_ref.shape) + local_ref[...]
    mine = mine_ref[0]
    keep_ref[...] = sum_ref[mine]
    send_ref[...] = sum_ref[1 - mine].astype(jnp.bfloat16)


def project(mine, got, w, local, first, tile, chunk, after=()):
    depth, width = w.shape
    count, _, lanes = got.shape
    per_column = local.shape[0]
    step = 1024
    return pl.pallas_call(
        functools.partial(project_kernel, tile),
        grid=(width // step,),
        in_specs=[
            SMEM,
            ANY,
            pl.BlockSpec((per_column, chunk, step), lambda n: (0, first // chunk, n)),
            pl.BlockSpec((count, per_column * tile, lanes), lambda n: (0, 0, 0)),
        ]
        + [ANY] * len(after),
        out_specs=[pl.BlockSpec((chunk, step), lambda n: (0, n))] * 2,
        out_shape=[
            jax.ShapeDtypeStruct((chunk, width), jnp.float32),
            jax.ShapeDtypeStruct((chunk, width), jnp.bfloat16),
        ],
        scratch_shapes=[
            pltpu.VMEM((2 * chunk, depth), jnp.bfloat16),
            pltpu.VMEM((2, chunk, step), jnp.float32),
            *stream_scratch(depth, width, step),
        ],
        compiler_params=pltpu.CompilerParams(vmem_limit_bytes=62 * MIB),
        cost_estimate=FREE,
        name="project",
    )(mine, w, local, got, *after)


def local_kernel(a_ref, w_ref, *refs):
    out_ref, held, sems = refs[-3:]
    stream(pl.program_id(0), w_ref, held, sems)
    w = held[pl.program_id(0)]
    out_ref[...] = jnp.dot(a_ref[...], w, preferred_element_type=jnp.float32)


def project_local(a, w, after=()):
    rows, depth = a.shape
    width = w.shape[1]
    step = 1024
    return pl.pallas_call(
        local_kernel,
        grid=(width // step,),
        in_specs=[
            pl.BlockSpec((rows, depth), lambda n: (0, 0)),
            ANY,
        ]
        + [ANY] * len(after),
        out_specs=pl.BlockSpec((rows, step), lambda n: (0, n)),
        out_shape=jax.ShapeDtypeStruct((rows, width), jnp.float32),
        scratch_shapes=stream_scratch(depth, width, step),
        compiler_params=pltpu.CompilerParams(vmem_limit_bytes=62 * MIB),
        cost_estimate=FREE,
        name="project_local",
    )(a, w, *after)


def column_chunks(planes):
    tiles = STRIDE // (planes * TILE)
    if tiles == 4:
        return ((0, 2 * TILE), (2 * TILE * planes, TILE), (3 * TILE * planes, TILE))
    return tuple((i * TILE * planes, TILE) for i in range(tiles))


def body(
    q_local, k_local, nearby_band_contents, q_stride, k_stride, v_stride, w_local, dilated_combiner
):
    rows, width = q_stride.shape
    per_column = rows // STRIDE
    count = lax.axis_size("seq")
    planes = count // PLANE
    place = jnp.stack([lax.axis_index("seq"), jnp.int32(count)]).astype(jnp.int32)
    mine = lax.axis_index("head").astype(jnp.int32).reshape(1)
    chunks = column_chunks(planes)
    last = len(chunks) - 1

    def exchange(a):
        return lax.all_to_all(a, "seq", split_axis=0, concat_axis=0, tiled=True)

    stride = (q_stride, k_stride, v_stride)
    ahead = [0] + [per_column * t for _, t in chunks[:-1]]
    packed, token = [], ()
    for i, (first, tile) in enumerate(chunks):
        packed.append(pack(stride, first, tile, ahead[i], planes, token))
        if i == 0:
            lows, highs = ends(k_local, nearby_band_contents, tuple(packed))
            token = (lows,)
    packed.append(None)
    lows = lax.ppermute(lows, "seq", [(i, i + 1) for i in range(count - 1)])
    highs = lax.ppermute(highs, "seq", [(i + 1, i) for i in range(count - 1)])

    results, after = [], (lows, highs)
    got = exchange(packed[0])
    for i, (first, tile) in enumerate(chunks):
        if i == min(1, last):
            attn_local = band_attention(
                place, q_local, k_local, nearby_band_contents, lows, highs, after
            )
            part_local = project_local(attn_local, w_local, (attn_local,))
            part_local = part_local.reshape(per_column, STRIDE, -1)
            after = (part_local,)
        outs = column_attention(got, ahead[i], tile, per_column, packed[i + 1], after)
        after = (outs,)
        back, got = got, exchange(outs)
        for j in range(i - 1, i + (i == last)):
            if j < 0:
                continue
            start, tile = chunks[j]
            keep, send = project(
                mine,
                back if j < i else got,
                dilated_combiner,
                part_local,
                start,
                tile,
                tile * planes,
                after,
            )
            after = (send,)
            results.append((keep, swap(send, "head", 1), start))
    out = None
    for keep, other, start in results:
        out = add_into(out, keep, other, start, rows // 2, after if out is None else ())
    return out


def solution(mesh):
    in_specs = (
        P("seq", "head"),
        P("seq", "head"),
        P("seq", "head"),
        P("seq", "head"),
        P("seq", "head"),
        P("seq", "head"),
        P("head", None),
        P("head", None),
    )
    out_specs = P(("seq", "head"), None)
    return jax.shard_map(body, mesh=mesh, in_specs=in_specs, out_specs=out_specs, check_vma=False)
```

time: 215 us -> 182 us (0.85)
  Pallas kernels: 34.8 us -> 76 us
  starting transfers between devices: 87 us -> 52.3 us
  waiting for transfers between devices: 64.4 us -> 45.8 us
  other arithmetic: 10.6 us -> 0.61 us
  matrix products: 6.89 us -> 0 us
  local copies, waits for them, and re-layouts: 10.3 us -> 5.53 us
    ppermute x41 -> x3, starting transfers between devices: 81.6 us -> 4.75 us  [swap(): return lax.ppermute(array, axis, [(i, i ^ mask) for i in range(count)])]
    ppermute x41 -> x3, waiting for transfers between devices: 64.4 us -> 7.42 us  [swap(): return lax.ppermute(array, axis, [(i, i ^ mask) for i in range(count)])]
    all_to_all x0 -> x4, starting transfers between devices: none -> 42.2 us  [exchange(): return lax.all_to_all(a, 'seq', split_axis=0, concat_axis=0, tiled=True)]
    pallas_call x8 -> x14, Pallas kernels: 24 us -> 65.1 us  [the longest x3 21.8 us: project(): pl.pallas_call(functools.partial(project_kernel, tile), grid=(width // st...]
    all_to_all x0 -> x4, waiting for transfers between devices: none -> 38.4 us  [exchange(): return lax.all_to_all(a, 'seq', split_axis=0, concat_axis=0, tiled=True)]
    dynamic_slice x6 -> x0, local copies, waits for them, and re-layouts: 8.87 us -> none  [the longest x2 4.84 us: body(): lax.dynamic_slice_in_dim(a, core * half, half, 1)]
    dot_general x1 -> x0, matrix products: 6.89 us -> none  [body(): jnp.dot(attn_local, w_local, preferred_element_type=jnp.float32)]
    unnamed x12, local copies, waits for them, and re-layouts: 0.02 us -> 5.53 us
  transfers between devices with their start and end apart: 43 -> 9, of which waited for: 10 -> 5; matrix products, arithmetic and copies ran while one was open for 9% -> 0% of each run, Pallas kernels for 16% -> 34%
where the time goes in v2:
time: 182 us; the launch traced here: 180 us
  Pallas kernels  76 us (42%)
  starting transfers between devices  52.3 us (29%)
  waiting for transfers between devices  45.8 us (25%)
  local copies, waits for them, and re-layouts  5.53 us (3%)
    all_to_all x4, starting transfers between devices, exchange(): return lax.all_to_all(a, 'seq', split_axis=0, concat_axis=0, tiled=True)  42.2 us
    all_to_all x4, waiting for transfers between devices, exchange(): return lax.all_to_all(a, 'seq', split_axis=0, concat_axis=0, tiled=True)  38.4 us
    pallas_call x3, Pallas kernels, project(): pl.pallas_call(functools.partial(project_kernel, tile), grid=(width // st...  21.8 us
    pallas_call x3, Pallas kernels, column_attention(): pl.pallas_call(functools.partial(column_kernel, tile, ahead), grid=(lanes...  13.2 us
    pallas_call x1, Pallas kernels, band_attention(): pl.pallas_call(band_kernel, grid=(width // HD,), in_specs=[SMEM, own, own...  10.9 us
    pallas_call x3, Pallas kernels, pack(): pl.pallas_call(pack_kernel, grid=(planes,), in_specs=[spec] * 3 + [ANY] *...  10.2 us
    pallas_call x1, Pallas kernels, project_local(): pl.pallas_call(local_kernel, grid=(width // step,), in_specs=[pl.BlockSpe...  9.43 us
    pallas_call x3, Pallas kernels, add_into(): pl.pallas_call(add_kernel, grid=(width // step,), in_specs=[spec, spec] +...  7.47 us
  transfers between devices with their start and end apart: 9, of which 5 were waited for; matrix products, arithmetic and copies ran while one was open for 0% of the time, Pallas kernels for 34%

profile of v2, /device:TPU:0, one launch (start us, length us, event | category | flops | bytes accessed | tf_op | source)
XLA Modules:
  0.0 180.4 jit_solution(5696267794975780191)
XLA Ops:
  0.0 3.6 %pack.3.refs_0_ = bf16[16,192,256]{2,1,0:T(8,128)(2,1)} custom-call(bf16[2,256,1024]{2,1,0:T(8,128)(2,1)} %bitcast.10, bf16[2,256,1024]{2,1,0:T(8,128)(2,1)} %bitcast.13, bf16[2,256,1024]{2,1,0:T(8,128)(2,1)} %bitcast.16), custom_call_target="tpu_custom_call" | custom-call | tf_op jit(solution)/shard_map/pack/pallas_call | solution.py:168
  3.6 7.4 %all-to-all-start = ((bf16[16,192,256]{2,1,0:T(8,128)(2,1)}), bf16[16,192,256]{2,1,0:T(8,128)(2,1)S(1)}, u32[]{:S(2)}, u32[]{:S(2)}) async-start(bf16[16,192,256]{2,1,0:T(8,128)(2,1)} %pack.3.refs_0_), calls=%async_computation | async-start | bytes 3145728 | tf_op jit(solution)/shard_map/all_to_all | solution.py:367
  11.0 3.0 %ends.1 = (bf16[2,256,1024]{2,1,0:T(8,128)(2,1)}, bf16[2,256,1024]{2,1,0:T(8,128)(2,1)}) custom-call(bf16[512,1024]{1,0:T(8,128)(2,1)} %k_ref.3, bf16[512,1024]{1,0:T(8,128)(2,1)} %v_ref.3, bf16[16,192,256]{2,1,0:T(8,128)(2,1)} %pack.3.refs_0_), custom_call_target="tpu_custom_call" | custom-call | tf_op jit(solution)/shard_map/ends/pallas_call | solution.py:137
  14.0 1.3 collective-permute-start.1
  15.3 4.0 %collective-permute-start = (bf16[2,256,1024]{2,1,0:T(8,128)(2,1)}, bf16[2,256,1024]{2,1,0:T(8,128)(2,1)}, u32[]{:S(2)}, u32[]{:S(2)}) collective-permute-start(bf16[2,256,1024]{2,1,0:T(8,128)(2,1)} %get-tuple-element.13.refs_0_), channel_id=1, source_target_pairs={{0,2},{2,4},{4,6},{6,8},{8,10},{10,12},{12,14},{14,16},{16,18},{18... | collective-permute-start | bytes 3145736 | tf_op jit(solution)/shard_map/ppermute | solution.py:378
  19.3 3.3 %pack.4.refs_0_ = bf16[16,160,256]{2,1,0:T(8,128)(2,1)} custom-call(bf16[2,256,1024]{2,1,0:T(8,128)(2,1)} %bitcast.11, bf16[2,256,1024]{2,1,0:T(8,128)(2,1)} %bitcast.14, bf16[2,256,1024]{2,1,0:T(8,128)(2,1)} %bitcast.17, bf16[2,256,1024]{2,1,0:T(8,128)(2,1)} %get-tuple-element.13.refs_0_), custom_call_target="tpu_custom_call" | custom-call | tf_op jit(solution)/shard_map/pack/pallas_call | solution.py:168
  22.6 20.4 %all-to-all-done.in_ref = bf16[16,192,256]{2,1,0:T(8,128)(2,1)S(1)} async-done(((bf16[16,192,256]{2,1,0:T(8,128)(2,1)}), bf16[16,192,256]{2,1,0:T(8,128)(2,1)S(1)}, u32[]{:S(2)}, u32[]{:S(2)}) %all-to-all-start) | async-done | bytes 1572896 | tf_op jit(solution)/shard_map/all_to_all | solution.py:367
  43.1 1.1 copy-done.2
  44.2 5.8 %column_attention.3.refs_0_ = bf16[16,160,256]{2,1,0:T(8,128)(2,1)} custom-call(bf16[16,192,256]{2,1,0:T(8,128)(2,1)} %copy-done.2, bf16[16,160,256]{2,1,0:T(8,128)(2,1)} %pack.4.refs_0_, bf16[2,256,1024]{2,1,0:T(8,128)(2,1)} %collective-permute-done.refs_1_.lows_ref, ...), custom_call_target="tpu_custom_call", output_to_operand_aliasing={{}: (1, {})} | custom-call | tf_op jit(solution)/shard_map/column_attention/pallas_call | solution.py:220
  50.0 20.0 %all-to-all-start.1 = ((bf16[16,160,256]{2,1,0:T(8,128)(2,1)}), bf16[16,160,256]{2,1,0:T(8,128)(2,1)S(1)}, u32[]{:S(2)}, u32[]{:S(2)}) async-start(bf16[16,160,256]{2,1,0:T(8,128)(2,1)} %column_attention.3.refs_0_), calls=%async_computation.1 | async-start | bytes 2621440 | tf_op jit(solution)/shard_map/all_to_all | solution.py:367
  70.0 3.3 %pack.5.refs_0_ = bf16[16,128,256]{2,1,0:T(8,128)(2,1)} custom-call(bf16[2,256,1024]{2,1,0:T(8,128)(2,1)} %bitcast.12, bf16[2,256,1024]{2,1,0:T(8,128)(2,1)} %bitcast.15, bf16[2,256,1024]{2,1,0:T(8,128)(2,1)} %bitcast.18, bf16[2,256,1024]{2,1,0:T(8,128)(2,1)} %get-tuple-element.13.refs_0_), custom_call_target="tpu_custom_call" | custom-call | tf_op jit(solution)/shard_map/pack/pallas_call | solution.py:168
  73.9 10.9 %band_attention.1.a_ref.refs_0_ = bf16[512,1024]{1,0:T(8,128)(2,1)} custom-call(s32[2]{0:T(128)} %pad_add_fusion.place_ref, bf16[512,1024]{1,0:T(8,128)(2,1)} %q_ref.1, bf16[512,1024]{1,0:T(8,128)(2,1)} %k_ref.3, bf16[512,1024]{1,0:T(8,128)(2,1)} %v_ref.3, bf16[2,256,1024]{2,1,0:T(8,128)(2,1)} %collective-permute-done.refs_1_.lows_ref, ...), custom_call_target="tpu_custom_call" | custom-call | tf_op jit(solution)/shard_map/band_attention/pallas_call | solution.py:89
  84.8 9.4 %project_local.1 = f32[512,4096]{1,0:T(8,128)} custom-call(bf16[512,1024]{1,0:T(8,128)(2,1)} %band_attention.1.a_ref.refs_0_, bf16[1024,4096]{1,0:T(8,128)(2,1)} %w_ref.4, bf16[512,1024]{1,0:T(8,128)(2,1)} %band_attention.1.a_ref.refs_0_), custom_call_target="tpu_custom_call" | custom-call | tf_op jit(solution)/shard_map/project_local/pallas_call | solution.py:330
  94.2 3.2 %all-to-all-done.1.in_ref = bf16[16,160,256]{2,1,0:T(8,128)(2,1)S(1)} async-done(((bf16[16,160,256]{2,1,0:T(8,128)(2,1)}), bf16[16,160,256]{2,1,0:T(8,128)(2,1)S(1)}, u32[]{:S(2)}, u32[]{:S(2)}) %all-to-all-start.1) | async-done | bytes 1310752 | tf_op jit(solution)/shard_map/all_to_all | solution.py:367
  97.4 1.1 copy-done
  98.4 3.8 %column_attention.4.refs_0_ = bf16[16,128,256]{2,1,0:T(8,128)(2,1)} custom-call(bf16[16,160,256]{2,1,0:T(8,128)(2,1)} %copy-done, bf16[16,128,256]{2,1,0:T(8,128)(2,1)} %pack.5.refs_0_, f32[2,256,4096]{2,1,0:T(8,128)} %bitcast.6), custom_call_target="tpu_custom_call", output_to_operand_aliasing={{}: (1, {})} | custom-call | tf_op jit(solution)/shard_map/column_attention/pallas_call | solution.py:220
  102.2 8.0 %all-to-all-start.2 = ((bf16[16,128,256]{2,1,0:T(8,128)(2,1)}), bf16[16,128,256]{2,1,0:T(8,128)(2,1)S(1)}, u32[]{:S(2)}, u32[]{:S(2)}) async-start(bf16[16,128,256]{2,1,0:T(8,128)(2,1)} %column_attention.4.refs_0_), calls=%async_computation.2 | async-start | bytes 2097152 | tf_op jit(solution)/shard_map/all_to_all | solution.py:367
  110.2 8.1 %project.3 = (f32[128,4096]{1,0:T(8,128)}, bf16[128,4096]{1,0:T(8,128)(2,1)}) custom-call(s32[1]{0:T(128)} %bitcast.mine_ref, bf16[1024,4096]{1,0:T(8,128)(2,1)} %w_ref.7, f32[2,256,4096]{2,1,0:T(8,128)} %bitcast.7, bf16[16,160,256]{2,1,0:T(8,128)(2,1)} %copy-done, bf16[16,128,256]{2,1,0:T(8,128)(2,1)} %column_attention.4.refs_0_), custom_call_target="tpu_custom_call" | custom-call | tf_op jit(solution)/shard_map/project/pallas_call | solution.py:293
  118.4 1.6 collective-permute-start.4
  119.9 13.2 %all-to-all-done.2.in_ref = bf16[16,128,256]{2,1,0:T(8,128)(2,1)S(1)} async-done(((bf16[16,128,256]{2,1,0:T(8,128)(2,1)}), bf16[16,128,256]{2,1,0:T(8,128)(2,1)S(1)}, u32[]{:S(2)}, u32[]{:S(2)}) %all-to-all-start.2) | async-done | bytes 1048608 | tf_op jit(solution)/shard_map/all_to_all | solution.py:367
  133.2 1.0 copy-done.1
  134.1 3.7 %column_attention.5.refs_0_ = bf16[16,32,256]{2,1,0:T(8,128)(2,1)} custom-call(bf16[16,128,256]{2,1,0:T(8,128)(2,1)} %copy-done.1, bf16[128,4096]{1,0:T(8,128)(2,1)} %get-tuple-element.15.refs_0_), custom_call_target="tpu_custom_call" | custom-call | tf_op jit(solution)/shard_map/column_attention/pallas_call | solution.py:220
  137.8 6.9 %all-to-all-start.3 = ((bf16[16,32,256]{2,1,0:T(8,128)(2,1)}), bf16[16,32,256]{2,1,0:T(8,128)(2,1)S(1)}, u32[]{:S(2)}, u32[]{:S(2)}) async-start(bf16[16,32,256]{2,1,0:T(8,128)(2,1)} %column_attention.5.refs_0_), calls=%async_computation.3 | async-start | bytes 524288 | tf_op jit(solution)/shard_map/all_to_all | solution.py:367
  144.7 6.9 %project.4 = (f32[64,4096]{1,0:T(8,128)}, bf16[64,4096]{1,0:T(8,128)(2,1)}) custom-call(s32[1]{0:T(128)} %bitcast.mine_ref, bf16[1024,4096]{1,0:T(8,128)(2,1)} %w_ref.7, f32[2,256,4096]{2,1,0:T(8,128)} %bitcast.8, bf16[16,128,256]{2,1,0:T(8,128)(2,1)} %copy-done.1, bf16[16,32,256]{2,1,0:T(8,128)(2,1)} %column_attention.5.refs_0_), custom_call_target="tpu_custom_call" | custom-call | tf_op jit(solution)/shard_map/project/pallas_call | solution.py:293
  151.6 1.6 collective-permute-start.3
  153.1 1.6 all-to-all-done.3.in_ref
  155.4 6.8 %project.5 = (f32[64,4096]{1,0:T(8,128)}, bf16[64,4096]{1,0:T(8,128)(2,1)}) custom-call(s32[1]{0:T(128)} %bitcast.mine_ref, bf16[1024,4096]{1,0:T(8,128)(2,1)} %w_ref.7, f32[2,256,4096]{2,1,0:T(8,128)} %bitcast.9, bf16[16,32,256]{2,1,0:T(8,128)(2,1)} %copy-done.3, bf16[64,4096]{1,0:T(8,128)(2,1)} %get-tuple-element.16.refs_0_), custom_call_target="tpu_custom_call" | custom-call | tf_op jit(solution)/shard_map/project/pallas_call | solution.py:293
  162.2 1.6 collective-permute-start.2
  163.8 3.0 %add_into.3.refs_0_ = bf16[256,4096]{1,0:T(8,128)(2,1)} custom-call(f32[128,4096]{1,0:T(8,128)} %get-tuple-element.20.keep_ref, bf16[128,4096]{1,0:T(8,128)(2,1)} %collective-permute-done.4.got_ref, bf16[64,4096]{1,0:T(8,128)(2,1)} %get-tuple-element.18.refs_0_), custom_call_target="tpu_custom_call" | custom-call | tf_op jit(solution)/shard_map/add_into/pallas_call | solution.py:115
  167.7 2.2 %add_into.4.refs_0_ = bf16[256,4096]{1,0:T(8,128)(2,1)} custom-call(f32[64,4096]{1,0:T(8,128)} %get-tuple-element.19.keep_ref, bf16[64,4096]{1,0:T(8,128)(2,1)} %copy-done.4, bf16[256,4096]{1,0:T(8,128)(2,1)} %add_into.3.refs_0_), custom_call_target="tpu_custom_call", output_to_operand_aliasing={{}: (2, {})} | custom-call | tf_op jit(solution)/shard_map/add_into/pallas_call | solution.py:115
  169.9 7.4 %collective-permute-done.2.got_ref = bf16[64,4096]{1,0:T(8,128)(2,1)S(1)} collective-permute-done((bf16[64,4096]{1,0:T(8,128)(2,1)}, bf16[64,4096]{1,0:T(8,128)(2,1)S(1)}, u32[]{:S(2)}, u32[]{:S(2)}) %collective-permute-start.2) | collective-permute-done | bytes 524320 | tf_op jit(solution)/shard_map/ppermute | solution.py:28
  178.1 2.2 %add_into.5 = bf16[256,4096]{1,0:T(8,128)(2,1)} custom-call(f32[64,4096]{1,0:T(8,128)} %get-tuple-element.17.keep_ref, bf16[64,4096]{1,0:T(8,128)(2,1)} %copy-done.5, bf16[256,4096]{1,0:T(8,128)(2,1)} %add_into.4.refs_0_), custom_call_target="tpu_custom_call", output_to_operand_aliasing={{}: (2, {})} | custom-call | tf_op jit(solution)/shard_map/add_into/pallas_call | solution.py:115
  (14 shorter events, 3.0 us)
Async XLA Ops:
  3.6 39.4 %all-to-all-start = ((bf16[16,192,256]{2,1,0:T(8,128)(2,1)}), bf16[16,192,256]{2,1,0:T(8,128)(2,1)S(1)}, u32[]{:S(2)}, u32[]{:S(2)}) async-start(bf16[16,192,256]{2,1,0:T(8,128)(2,1)} %pack.3.refs_0_), calls=%async_computation | async-start | bytes 3145728 | tf_op jit(solution)/shard_map/all_to_all | solution.py:367
  14.0 8.7 %collective-permute-start.1 = (bf16[2,256,1024]{2,1,0:T(8,128)(2,1)}, bf16[2,256,1024]{2,1,0:T(8,128)(2,1)}, u32[]{:S(2)}, u32[]{:S(2)}) collective-permute-start(bf16[2,256,1024]{2,1,0:T(8,128)(2,1)} %get-tuple-element.14), channel_id=1, source_target_pairs={{2,0},{4,2},{6,4},{8,6},{10,8},{12,10},{14,12},{16,14},{18,16},{20... | collective-permute-start | bytes 3145736 | tf_op jit(solution)/shard_map/ppermute | solution.py:379
  15.3 7.4 %collective-permute-start = (bf16[2,256,1024]{2,1,0:T(8,128)(2,1)}, bf16[2,256,1024]{2,1,0:T(8,128)(2,1)}, u32[]{:S(2)}, u32[]{:S(2)}) collective-permute-start(bf16[2,256,1024]{2,1,0:T(8,128)(2,1)} %get-tuple-element.13.refs_0_), channel_id=1, source_target_pairs={{0,2},{2,4},{4,6},{6,8},{8,10},{10,12},{12,14},{14,16},{16,18},{18... | collective-permute-start | bytes 3145736 | tf_op jit(solution)/shard_map/ppermute | solution.py:378
  43.1 1.1 copy-start.2
  50.0 47.4 %all-to-all-start.1 = ((bf16[16,160,256]{2,1,0:T(8,128)(2,1)}), bf16[16,160,256]{2,1,0:T(8,128)(2,1)S(1)}, u32[]{:S(2)}, u32[]{:S(2)}) async-start(bf16[16,160,256]{2,1,0:T(8,128)(2,1)} %column_attention.3.refs_0_), calls=%async_computation.1 | async-start | bytes 2621440 | tf_op jit(solution)/shard_map/all_to_all | solution.py:367
  97.4 1.1 copy-start
  102.2 31.0 %all-to-all-start.2 = ((bf16[16,128,256]{2,1,0:T(8,128)(2,1)}), bf16[16,128,256]{2,1,0:T(8,128)(2,1)S(1)}, u32[]{:S(2)}, u32[]{:S(2)}) async-start(bf16[16,128,256]{2,1,0:T(8,128)(2,1)} %column_attention.4.refs_0_), calls=%async_computation.2 | async-start | bytes 2097152 | tf_op jit(solution)/shard_map/all_to_all | solution.py:367
  118.4 45.5 %collective-permute-start.4 = (bf16[128,4096]{1,0:T(8,128)(2,1)}, bf16[128,4096]{1,0:T(8,128)(2,1)}, u32[]{:S(2)}, u32[]{:S(2)}) collective-permute-start(bf16[128,4096]{1,0:T(8,128)(2,1)} %get-tuple-element.15.refs_0_), channel_id=1, source_target_pairs={{0,1},{1,0},{2,3},{3,2},{4,5},{5,4},{6,7},{7,6},{8,9},{9,8},{10,11... | collective-permute-start | bytes 3145736 | tf_op jit(solution)/shard_map/ppermute | solution.py:28
  133.2 1.0 copy-start.1
  137.8 16.9 %all-to-all-start.3 = ((bf16[16,32,256]{2,1,0:T(8,128)(2,1)}), bf16[16,32,256]{2,1,0:T(8,128)(2,1)S(1)}, u32[]{:S(2)}, u32[]{:S(2)}) async-start(bf16[16,32,256]{2,1,0:T(8,128)(2,1)} %column_attention.5.refs_0_), calls=%async_computation.3 | async-start | bytes 524288 | tf_op jit(solution)/shard_map/all_to_all | solution.py:367
  151.6 15.3 %collective-permute-start.3 = (bf16[64,4096]{1,0:T(8,128)(2,1)}, bf16[64,4096]{1,0:T(8,128)(2,1)S(1)}, u32[]{:S(2)}, u32[]{:S(2)}) collective-permute-start(bf16[64,4096]{1,0:T(8,128)(2,1)} %get-tuple-element.16.refs_0_), channel_id=1, source_target_pairs={{0,1},{1,0},{2,3},{3,2},{4,5},{5,4},{6,7},{7,6},{8,9},{9,8},{10,11... | collective-permute-start | bytes 1572872 | tf_op jit(solution)/shard_map/ppermute | solution.py:28
  154.7 0.7 copy-start.3
  162.2 15.1 %collective-permute-start.2 = (bf16[64,4096]{1,0:T(8,128)(2,1)}, bf16[64,4096]{1,0:T(8,128)(2,1)S(1)}, u32[]{:S(2)}, u32[]{:S(2)}) collective-permute-start(bf16[64,4096]{1,0:T(8,128)(2,1)} %get-tuple-element.18.refs_0_), channel_id=1, source_target_pairs={{0,1},{1,0},{2,3},{3,2},{4,5},{5,4},{6,7},{7,6},{8,9},{9,8},{10,11... | collective-permute-start | bytes 1572872 | tf_op jit(solution)/shard_map/ppermute | solution.py:28
  166.8 0.9 copy-start.4
  177.3 0.8 copy-start.5

commit v3 on v2

v3 whole, which is shorter than its diff:
```python
import functools

import jax
import jax.numpy as jnp
from jax import lax
from jax.experimental import pallas as pl
from jax.experimental.pallas import tpu as pltpu
from jax.sharding import PartitionSpec as P

HD = 128
STRIDE = 256
BAND = 256
PLANE = 4
TILE = 8
PIECE = 16
ROUNDS = ((0, 4), (128, 2), (192, 2))
OFF = -1e30
SCALE = HD**-0.5
LOG2E = 1.4426950408889634
MIB = 1 << 20
FREE = pl.CostEstimate(flops=0, bytes_accessed=0, transcendentals=0)

VMEM = pl.BlockSpec(memory_space=pltpu.VMEM)
SMEM = pl.BlockSpec(memory_space=pltpu.SMEM)
ANY = pl.BlockSpec(memory_space=pl.ANY)


def swap(array, axis, mask):
    count = lax.axis_size(axis)
    return lax.ppermute(array, axis, [(i, i ^ mask) for i in range(count)])


def scores(q, k):
    return lax.dot_general(q, k, (((1,), (1,)), ((), ())), preferred_element_type=jnp.float32)


def softmax_sum(score, v):
    top = jnp.max(score, axis=-1, keepdims=True)
    weight = jnp.exp2((score - top) * (SCALE * LOG2E))
    total = jnp.sum(weight, axis=-1, keepdims=True)
    out = jnp.dot(weight.astype(jnp.bfloat16), v, preferred_element_type=jnp.float32)
    return (out / total).astype(jnp.bfloat16)


def band_kernel(place_ref, q_ref, k_ref, v_ref, lows_ref, highs_ref, *refs):
    out_ref, k_all, v_all, bias = refs[-4:]
    rows = q_ref.shape[0]
    step = BAND
    blocks = rows // step

    @pl.when(pl.program_id(0) == 0)
    def _():
        query = lax.broadcasted_iota(jnp.int32, (step, BAND), 0)
        key = lax.broadcasted_iota(jnp.int32, (step, BAND), 1)
        for b in range(blocks):
            before = key >= query
            after = key <= query
            if b == 0:
                before = before & (place_ref[0] > 0)
            if b == blocks - 1:
                after = after & (place_ref[0] < place_ref[1] - 1)
            bias[b, 0] = jnp.where(before, 0.0, OFF)
            bias[b, 1] = jnp.where(after, 0.0, OFF)

    for held, low, own, high in (
        (k_all, lows_ref.at[0], k_ref, highs_ref.at[0]),
        (v_all, lows_ref.at[1], v_ref, highs_ref.at[1]),
    ):
        held[:BAND] = low[...]
        held[BAND : BAND + rows] = own[...]
        held[BAND + rows :] = high[...]
    for b in range(blocks):
        at = slice(b * step, b * step + step)
        near = slice(b * step, b * step + 3 * BAND)
        score = scores(q_ref[at], k_all[near])
        score = jnp.concatenate(
            [
                score[:, :BAND] + bias[b, 0],
                score[:, BAND : 2 * BAND],
                score[:, 2 * BAND :] + bias[b, 1],
            ],
            axis=1,
        )
        out_ref[at] = softmax_sum(score, v_all[near])


def band_attention(place, q, k, v, lows, highs, after=()):
    rows, width = q.shape
    own = pl.BlockSpec((rows, HD), lambda h: (0, h))
    side = pl.BlockSpec((2, BAND, HD), lambda h: (0, 0, h))
    return pl.pallas_call(
        band_kernel,
        grid=(width // HD,),
        in_specs=[SMEM, own, own, own, side, side] + [ANY] * len(after),
        out_specs=own,
        out_shape=jax.ShapeDtypeStruct(q.shape, q.dtype),
        scratch_shapes=[
            pltpu.VMEM((rows + 2 * BAND, HD), jnp.bfloat16),
            pltpu.VMEM((rows + 2 * BAND, HD), jnp.bfloat16),
            pltpu.VMEM((rows // BAND, 2, BAND, BAND), jnp.float32),
        ],
        compiler_params=pltpu.CompilerParams(vmem_limit_bytes=60 * MIB),
        cost_estimate=FREE,
        name="band_attention",
    )(place, q, k, v, lows, highs, *after)


def add_kernel(keep_ref, got_ref, *refs):
    refs[-1][...] = (keep_ref[...] + got_ref[...].astype(jnp.float32)).astype(jnp.bfloat16)


def add_into(out, keep, got, first, part, parts, rows, after=()):
    chunk, width = keep.shape
    step = width
    spec = pl.BlockSpec((chunk, step), lambda n: (0, n))
    held = () if out is None else (out,)
    return pl.pallas_call(
        add_kernel,
        grid=(width // step,),
        in_specs=[spec, spec] + [ANY] * (len(held) + len(after)),
        out_specs=pl.BlockSpec((chunk, step), lambda n: (first // chunk, part)),
        out_shape=jax.ShapeDtypeStruct((rows, parts * width), jnp.bfloat16),
        input_output_aliases={2: 0} if held else {},
        compiler_params=pltpu.CompilerParams(vmem_limit_bytes=16 * MIB),
        cost_estimate=FREE,
        name="add_into",
    )(keep, got, *held, *after)


def ends_kernel(k_ref, v_ref, *refs):
    lows_ref, highs_ref = refs[-2:]
    for t, held in enumerate((k_ref, v_ref)):
        highs_ref[t] = held[:BAND]
        lows_ref[t] = held[held.shape[0] - BAND :]


def ends(k, v, after=()):
    shape = jax.ShapeDtypeStruct((2, BAND, k.shape[1]), k.dtype)
    return pl.pallas_call(
        ends_kernel,
        grid=(1,),
        in_specs=[pl.BlockSpec(k.shape, lambda n: (0, 0))] * 2 + [ANY] * len(after),
        out_specs=[pl.BlockSpec(shape.shape, lambda n: (0, 0, 0))] * 2,
        out_shape=[shape] * 2,
        compiler_params=pltpu.CompilerParams(vmem_limit_bytes=60 * MIB),
        cost_estimate=FREE,
        name="ends",
    )(k, v, *after)


def pack_kernel(planes, ahead, q_ref, k_ref, v_ref, *refs):
    out_ref = refs[-1]
    lanes = out_ref.shape[-1]
    per_column, columns, _ = q_ref.shape
    unit = pl.program_id(0)
    for t, held in enumerate((q_ref, k_ref, v_ref)):
        rows = [held[j].astype(jnp.float32) for j in range(per_column)]
        at = pl.ds(pl.multiple_of(ahead + (unit * 3 + t) * PIECE, PIECE), PIECE)
        for z in range(planes):
            piece = jnp.concatenate([r[z * TILE : (z + 1) * TILE] for r in rows])
            piece = piece.astype(jnp.bfloat16)
            for p in range(PLANE):
                out_ref[z * PLANE + p, at] = piece[:, p * lanes : (p + 1) * lanes]


def pack(arrays, first, units, ahead, planes, after=()):
    rows, width = arrays[0].shape
    per_column = rows // STRIDE
    lanes = width // PLANE
    columns = planes * TILE
    views = [a.reshape(per_column, STRIDE, width) for a in arrays]
    spec = pl.BlockSpec((per_column, columns, width), lambda n: (0, first // columns + n, 0))
    shape = (planes * PLANE, ahead + 3 * PIECE * units, lanes)
    return pl.pallas_call(
        functools.partial(pack_kernel, planes, ahead),
        grid=(units,),
        in_specs=[spec] * 3 + [ANY] * len(after),
        out_specs=pl.BlockSpec(shape, lambda n: (0, 0, 0)),
        out_shape=jax.ShapeDtypeStruct(shape, jnp.bfloat16),
        compiler_params=pltpu.CompilerParams(vmem_limit_bytes=60 * MIB),
        cost_estimate=FREE,
        name="pack",
    )(*views, *after)


def column_kernel(lo, units, ahead, in_ref, *refs):
    out_ref, held, result, bias, in_sems, out_sems = refs[-6:]
    count, lanes = held.shape[2], held.shape[4]
    length = count * PIECE
    block = bias.shape[0]

    def arrival(u, t):
        rows = pl.ds(ahead + ((lo + u) * 3 + t) * PIECE, PIECE)
        return pltpu.make_async_copy(in_ref.at[:, rows], held.at[u, t], in_sems.at[u, t])

    def departure(u):
        rows = pl.ds((lo + u) * PIECE, PIECE)
        return pltpu.make_async_copy(result.at[u], out_ref.at[:, rows], out_sems.at[u])

    for u in range(units):
        for t in range(3):
            arrival(u, t).start()
    query = lax.broadcasted_iota(jnp.int32, bias.shape, 0)
    key = lax.broadcasted_iota(jnp.int32, bias.shape, 1)
    bias[...] = jnp.where((query & (TILE - 1)) == (key & (TILE - 1)), 0.0, OFF)
    for u in range(units):
        for t in range(3):
            arrival(u, t).wait()
        for h in range(lanes // HD):
            head = slice(h * HD, h * HD + HD)
            k = held[u, 1, :, :, head].reshape(length, HD)
            v = held[u, 2, :, :, head].reshape(length, HD)
            for s in range(0, count, block // PIECE):
                part = slice(s, s + block // PIECE)
                q = held[u, 0, part, :, head].reshape(block, HD)
                out = softmax_sum(scores(q, k) + bias[...], v)
                result[u, part, :, head] = out.reshape(block // PIECE, PIECE, HD)
        departure(u).start()
    for u in range(units):
        departure(u).wait()


def column_attention(got, ahead, lo, units, into, after=()):
    count, _, lanes = got.shape
    length = count * PIECE
    block = min(length, 256)
    held = () if into is None else (into,)
    shape = (count, units * PIECE, lanes) if into is None else into.shape
    return pl.pallas_call(
        functools.partial(column_kernel, lo, units, ahead),
        in_specs=[ANY] * (1 + len(held) + len(after)),
        out_specs=ANY,
        out_shape=jax.ShapeDtypeStruct(shape, jnp.bfloat16),
        input_output_aliases={1: 0} if held else {},
        scratch_shapes=[
            pltpu.VMEM((units, 3, count, PIECE, lanes), jnp.bfloat16),
            pltpu.VMEM((units, count, PIECE, lanes), jnp.bfloat16),
            pltpu.VMEM((block, length), jnp.float32),
            pltpu.SemaphoreType.DMA((units, 3)),
            pltpu.SemaphoreType.DMA((units,)),
        ],
        compiler_params=pltpu.CompilerParams(vmem_limit_bytes=52 * MIB),
        cost_estimate=FREE,
        name="column_attention",
    )(got, *held, *after)


def stream(step, w_ref, held, sems, start=0):
    width = held.shape[2]

    def block(n):
        columns = pl.ds(start + n * width, width)
        return pltpu.make_async_copy(w_ref.at[:, columns], held.at[n], sems.at[n])

    @pl.when(step == 0)
    def _():
        for n in range(held.shape[0]):
            block(n).start()

    for n in range(held.shape[0]):

        @pl.when(step == n)
        def _():
            block(n).wait()


def stream_scratch(depth, width, step):
    return [
        pltpu.VMEM((width // step, depth, step), jnp.bfloat16),
        pltpu.SemaphoreType.DMA((width // step,)),
    ]


def project_kernel(units, begin, mine_ref, w_ref, local_ref, in_ref, *refs):
    keep_ref, send_ref, rows_ref, sum_ref, held, sems = refs[-6:]
    stream(pl.program_id(0), w_ref, held, sems, begin)

    @pl.when(pl.program_id(0) == 0)
    def _():
        count, _, lanes = in_ref.shape
        planes = count // PLANE
        columns = planes * TILE
        chunk = units * columns
        for u in range(units):
            for p in range(PLANE):
                pieces = [
                    in_ref[z * PLANE + p, u * PIECE : (u + 1) * PIECE].astype(jnp.float32)
                    for z in range(planes)
                ]
                for j in range(PIECE // TILE):
                    part = jnp.concatenate([x[j * TILE : (j + 1) * TILE] for x in pieces])
                    row = j * chunk + u * columns
                    lane = slice(p * lanes, (p + 1) * lanes)
                    rows_ref[row : row + columns, lane] = part.astype(jnp.bfloat16)

    w = held[pl.program_id(0)]
    total = jnp.dot(rows_ref[...], w, preferred_element_type=jnp.float32)
    sum_ref[...] = total.reshape(sum_ref.shape) + local_ref[...]
    mine = mine_ref[0]
    keep_ref[...] = sum_ref[mine]
    send_ref[...] = sum_ref[1 - mine].astype(jnp.bfloat16)


def project(mine, got, w, local, first, units, chunk, part, parts, after=()):
    depth = w.shape[0]
    width = w.shape[1] // parts
    count, _, lanes = got.shape
    per_column = local.shape[0]
    step = 1024
    steps = width // step
    return pl.pallas_call(
        functools.partial(project_kernel, units, part * width),
        grid=(width // step,),
        in_specs=[
            SMEM,
            ANY,
            pl.BlockSpec((per_column, chunk, step), lambda n: (0, first // chunk, part * steps + n)),
            pl.BlockSpec((count, units * PIECE, lanes), lambda n: (0, 0, 0)),
        ]
        + [ANY] * len(after),
        out_specs=[pl.BlockSpec((chunk, step), lambda n: (0, n))] * 2,
        out_shape=[
            jax.ShapeDtypeStruct((chunk, width), jnp.float32),
            jax.ShapeDtypeStruct((chunk, width), jnp.bfloat16),
        ],
        scratch_shapes=[
            pltpu.VMEM((2 * chunk, depth), jnp.bfloat16),
            pltpu.VMEM((2, chunk, step), jnp.float32),
            *stream_scratch(depth, width, step),
        ],
        compiler_params=pltpu.CompilerParams(vmem_limit_bytes=58 * MIB),
        cost_estimate=FREE,
        name="project",
    )(mine, w, local, got, *after)


def local_kernel(a_ref, w_ref, *refs):
    out_ref, held, sems = refs[-3:]
    stream(pl.program_id(0), w_ref, held, sems)
    w = held[pl.program_id(0)]
    out_ref[...] = jnp.dot(a_ref[...], w, preferred_element_type=jnp.float32)


def project_local(a, w, after=()):
    rows, depth = a.shape
    width = w.shape[1]
    step = 1024
    return pl.pallas_call(
        local_kernel,
        grid=(width // step,),
        in_specs=[
            pl.BlockSpec((rows, depth), lambda n: (0, 0)),
            ANY,
        ]
        + [ANY] * len(after),
        out_specs=pl.BlockSpec((rows, step), lambda n: (0, n)),
        out_shape=jax.ShapeDtypeStruct((rows, width), jnp.float32),
        scratch_shapes=stream_scratch(depth, width, step),
        compiler_params=pltpu.CompilerParams(vmem_limit_bytes=60 * MIB),
        cost_estimate=FREE,
        name="project_local",
    )(a, w, *after)


def column_chunks(planes):
    units = STRIDE // (planes * TILE)
    if units == 8:
        return ROUNDS
    return ((0, units),)


def body(
    q_local, k_local, nearby_band_contents, q_stride, k_stride, v_stride, w_local, dilated_combiner
):
    rows, width = q_stride.shape
    per_column = rows // STRIDE
    count = lax.axis_size("seq")
    planes = count // PLANE
    place = jnp.stack([lax.axis_index("seq"), jnp.int32(count)]).astype(jnp.int32)
    mine = lax.axis_index("head").astype(jnp.int32).reshape(1)
    chunks = column_chunks(planes)
    last = len(chunks) - 1

    def exchange(a):
        return lax.all_to_all(a, "seq", split_axis=0, concat_axis=0, tiled=True)

    stride = (q_stride, k_stride, v_stride)
    ahead = [0] + [PIECE * units for _, units in chunks[:-1]]
    packed, token = [], ()
    for i, (first, units) in enumerate(chunks):
        packed.append(pack(stride, first, units, ahead[i], planes, token))
        if i == 0:
            lows, highs = ends(k_local, nearby_band_contents, tuple(packed))
            token = (lows,)
    packed.append(None)
    lows = lax.ppermute(lows, "seq", [(i, i + 1) for i in range(count - 1)])
    highs = lax.ppermute(highs, "seq", [(i + 1, i) for i in range(count - 1)])

    results, after = [], (lows, highs)
    got = exchange(packed[0])
    for i, (first, units) in enumerate(chunks):
        if i == min(1, last):
            attn_local = band_attention(
                place, q_local, k_local, nearby_band_contents, lows, highs, after
            )
            part_local = project_local(attn_local, w_local, (attn_local,))
            part_local = part_local.reshape(per_column, STRIDE, -1)
            after = (part_local,)
        if i == 0 and i < last:
            early = units // 2
            outs = column_attention(got, ahead[i], 0, early, packed[i + 1])
            outs = column_attention(got, ahead[i], early, units - early, outs, after)
        else:
            outs = column_attention(got, ahead[i], 0, units, packed[i + 1], after)
        after = (outs,)
        back, got = got, exchange(outs)
        for j in range(i - 1, i + (i == last)):
            if j < 0:
                continue
            start, size = chunks[j]
            parts = 2 if j == last else 1
            for part in range(parts):
                keep, send = project(
                    mine,
                    back if j < i else got,
                    dilated_combiner,
                    part_local,
                    start,
                    size,
                    size * planes * TILE,
                    part,
                    parts,
                    after,
                )
                after = (send,)
                results.append((keep, swap(send, "head", 1), start, part, parts))
    out = None
    for keep, other, start, part, parts in results:
        out = add_into(out, keep, other, start, part, parts, rows // 2, after if out is None else ())
    return out


def solution(mesh):
    in_specs = (
        P("seq", "head"),
        P("seq", "head"),
        P("seq", "head"),
        P("seq", "head"),
        P("seq", "head"),
        P("seq", "head"),
        P("head", None),
        P("head", None),
    )
    out_specs = P(("seq", "head"), None)
    return jax.shard_map(body, mesh=mesh, in_specs=in_specs, out_specs=out_specs, check_vma=False)
```

time: 182 us -> 172 us (0.945)
  Pallas kernels: 76 us -> 69.7 us
  starting transfers between devices: 52.3 us -> 46 us
  waiting for transfers between devices: 45.8 us -> 47.7 us
    all_to_all x4, starting transfers between devices: 42.2 us -> 36.2 us  [exchange(): return lax.all_to_all(a, 'seq', split_axis=0, concat_axis=0, tiled=True)]
    pallas_call x3 -> x4, Pallas kernels: 7.47 us -> 3.52 us  [add_into(): pl.pallas_call(add_kernel, grid=(width // step,), in_specs=[spec, spec] +...]
    all_to_all x4, waiting for transfers between devices: 38.4 us -> 41.5 us  [exchange(): return lax.all_to_all(a, 'seq', split_axis=0, concat_axis=0, tiled=True)]
    pallas_call x9 -> x11, Pallas kernels: 45.2 us -> 42.9 us  [the longest x4 24.2 us: project(): pl.pallas_call(functools.partial(project_kernel, units, part * width), gr...]
    unnamed x12 -> x24, local copies, waits for them, and re-layouts: 5.53 us -> 6.79 us
    ppermute x3 -> x4, waiting for transfers between devices: 7.42 us -> 6.21 us  [swap(): return lax.ppermute(array, axis, [(i, i ^ mask) for i in range(count)])]
    ppermute x3 -> x4, starting transfers between devices: 4.75 us -> 5.38 us  [swap(): return lax.ppermute(array, axis, [(i, i ^ mask) for i in range(count)])]
  transfers between devices with their start and end apart: 9 -> 10, of which waited for: 5 -> 6; matrix products, arithmetic and copies ran while one was open for 0% -> 0% of each run, Pallas kernels for 34% -> 35%
where the time goes in v3:
time: 172 us; the launch traced here: 171 us
  Pallas kernels  69.7 us (41%)
  waiting for transfers between devices  47.7 us (28%)
  starting transfers between devices  46 us (27%)
  local copies, waits for them, and re-layouts  6.79 us (4%)
    all_to_all x4, waiting for transfers between devices, exchange(): return lax.all_to_all(a, 'seq', split_axis=0, concat_axis=0, tiled=True)  41.5 us
    all_to_all x4, starting transfers between devices, exchange(): return lax.all_to_all(a, 'seq', split_axis=0, concat_axis=0, tiled=True)  36.2 us
    pallas_call x4, Pallas kernels, project(): pl.pallas_call(functools.partial(project_kernel, units, part * width), gr...  24.2 us
    pallas_call x1, Pallas kernels, band_attention(): pl.pallas_call(band_kernel, grid=(width // HD,), in_specs=[SMEM, own, own...  10.9 us
    pallas_call x4, Pallas kernels, column_attention(): pl.pallas_call(functools.partial(column_kernel, lo, units, ahead), in_spe...  10.7 us
    pallas_call x1, Pallas kernels, project_local(): pl.pallas_call(local_kernel, grid=(width // step,), in_specs=[pl.BlockSpe...  9.43 us
    pallas_call x3, Pallas kernels, pack(): pl.pallas_call(functools.partial(pack_kernel, planes, ahead), grid=(units...  8.04 us
    unnamed x24, local copies, waits for them, and re-layouts  6.79 us
  transfers between devices with their start and end apart: 10, of which 6 were waited for; matrix products, arithmetic and copies ran while one was open for 0% of the time, Pallas kernels for 35%

profile of v3, /device:TPU:0, one launch (start us, length us, event | category | flops | bytes accessed | tf_op | source)
XLA Modules:
  0.0 171.0 jit_solution(10894828373018164619)
XLA Ops:
  0.0 3.5 %pack.3.refs_0_ = bf16[16,192,256]{2,1,0:T(8,128)(2,1)} custom-call(bf16[2,256,1024]{2,1,0:T(8,128)(2,1)} %bitcast.11, bf16[2,256,1024]{2,1,0:T(8,128)(2,1)} %bitcast.14, bf16[2,256,1024]{2,1,0:T(8,128)(2,1)} %bitcast.17), custom_call_target="tpu_custom_call" | custom-call | tf_op jit(solution)/shard_map/pack/pallas_call | solution.py:174
  3.5 7.4 %all-to-all-start = ((bf16[16,192,256]{2,1,0:T(8,128)(2,1)}), bf16[16,192,256]{2,1,0:T(8,128)(2,1)S(1)}, u32[]{:S(2)}, u32[]{:S(2)}) async-start(bf16[16,192,256]{2,1,0:T(8,128)(2,1)} %pack.3.refs_0_), calls=%async_computation | async-start | bytes 3145728 | tf_op jit(solution)/shard_map/all_to_all | solution.py:385
  10.8 3.0 %ends.1 = (bf16[2,256,1024]{2,1,0:T(8,128)(2,1)}, bf16[2,256,1024]{2,1,0:T(8,128)(2,1)}) custom-call(bf16[512,1024]{1,0:T(8,128)(2,1)} %k_ref.3, bf16[512,1024]{1,0:T(8,128)(2,1)} %v_ref.3, bf16[16,192,256]{2,1,0:T(8,128)(2,1)} %pack.3.refs_0_), custom_call_target="tpu_custom_call" | custom-call | tf_op jit(solution)/shard_map/ends/pallas_call | solution.py:139
  13.8 1.3 collective-permute-start.1
  15.1 3.1 %collective-permute-start = (bf16[2,256,1024]{2,1,0:T(8,128)(2,1)}, bf16[2,256,1024]{2,1,0:T(8,128)(2,1)S(1)}, u32[]{:S(2)}, u32[]{:S(2)}) collective-permute-start(bf16[2,256,1024]{2,1,0:T(8,128)(2,1)} %get-tuple-element.15.refs_0_), channel_id=1, source_target_pairs={{0,2},{2,4},{4,6},{6,8},{8,10},{10,12},{12,14},{14,16},{16,18},{18... | collective-permute-start | bytes 3145736 | tf_op jit(solution)/shard_map/ppermute | solution.py:396
  18.2 2.4 %pack.4.refs_0_ = bf16[16,160,256]{2,1,0:T(8,128)(2,1)} custom-call(bf16[2,256,1024]{2,1,0:T(8,128)(2,1)} %bitcast.12, bf16[2,256,1024]{2,1,0:T(8,128)(2,1)} %bitcast.15, bf16[2,256,1024]{2,1,0:T(8,128)(2,1)} %bitcast.18, bf16[2,256,1024]{2,1,0:T(8,128)(2,1)} %get-tuple-element.15.refs_0_), custom_call_target="tpu_custom_call" | custom-call | tf_op jit(solution)/shard_map/pack/pallas_call | solution.py:174
  20.5 22.4 %all-to-all-done.in_ref = bf16[16,192,256]{2,1,0:T(8,128)(2,1)S(1)} async-done(((bf16[16,192,256]{2,1,0:T(8,128)(2,1)}), bf16[16,192,256]{2,1,0:T(8,128)(2,1)S(1)}, u32[]{:S(2)}, u32[]{:S(2)}) %all-to-all-start) | async-done | bytes 1572896 | tf_op jit(solution)/shard_map/all_to_all | solution.py:385
  42.9 1.1 copy-done.9
  44.0 1.3 copy-done
  45.4 2.3 %column_attention.4.refs_0_ = bf16[16,160,256]{2,1,0:T(8,128)(2,1)S(1)} custom-call(bf16[16,192,256]{2,1,0:T(8,128)(2,1)} %copy-done.9, bf16[16,160,256]{2,1,0:T(8,128)(2,1)S(1)} %copy-done), custom_call_target="tpu_custom_call", output_to_operand_aliasing={{}: (1, {})} | custom-call | tf_op jit(solution)/shard_map/column_attention/pallas_call | solution.py:229
  48.8 3.3 %column_attention.5.refs_0_ = bf16[16,160,256]{2,1,0:T(8,128)(2,1)} custom-call(bf16[16,192,256]{2,1,0:T(8,128)(2,1)} %copy-done.9, bf16[16,160,256]{2,1,0:T(8,128)(2,1)} %copy-done.1, bf16[2,256,1024]{2,1,0:T(8,128)(2,1)S(1)} %collective-permute-done.refs_1_.lows_ref, ...), custom_call_target="tpu_custom_call", output_to_operand_aliasing={{}: (1, {})} | custom-call | tf_op jit(solution)/shard_map/column_attention/pallas_call | solution.py:229
  52.2 14.0 %all-to-all-start.1 = ((bf16[16,160,256]{2,1,0:T(8,128)(2,1)}), bf16[16,160,256]{2,1,0:T(8,128)(2,1)S(1)}, u32[]{:S(2)}, u32[]{:S(2)}) async-start(bf16[16,160,256]{2,1,0:T(8,128)(2,1)} %column_attention.5.refs_0_), calls=%async_computation.1 | async-start | bytes 2621440 | tf_op jit(solution)/shard_map/all_to_all | solution.py:385
  66.1 2.2 %pack.5.refs_0_ = bf16[16,128,256]{2,1,0:T(8,128)(2,1)} custom-call(bf16[2,256,1024]{2,1,0:T(8,128)(2,1)} %bitcast.13, bf16[2,256,1024]{2,1,0:T(8,128)(2,1)} %bitcast.16, bf16[2,256,1024]{2,1,0:T(8,128)(2,1)} %bitcast.19, bf16[2,256,1024]{2,1,0:T(8,128)(2,1)} %get-tuple-element.15.refs_0_), custom_call_target="tpu_custom_call" | custom-call | tf_op jit(solution)/shard_map/pack/pallas_call | solution.py:174
  69.0 10.9 %band_attention.1.a_ref.refs_0_ = bf16[512,1024]{1,0:T(8,128)(2,1)} custom-call(s32[2]{0:T(128)} %pad_add_fusion.place_ref, bf16[512,1024]{1,0:T(8,128)(2,1)} %q_ref.1, bf16[512,1024]{1,0:T(8,128)(2,1)} %k_ref.3, bf16[512,1024]{1,0:T(8,128)(2,1)} %v_ref.3, bf16[2,256,1024]{2,1,0:T(8,128)(2,1)} %copy-done.3, ...), custom_call_target="tpu_custom_call" | custom-call | tf_op jit(solution)/shard_map/band_attention/pallas_call | solution.py:91
  79.9 9.4 %project_local.1 = f32[512,4096]{1,0:T(8,128)} custom-call(bf16[512,1024]{1,0:T(8,128)(2,1)} %band_attention.1.a_ref.refs_0_, bf16[1024,4096]{1,0:T(8,128)(2,1)} %w_ref.5, bf16[512,1024]{1,0:T(8,128)(2,1)} %band_attention.1.a_ref.refs_0_), custom_call_target="tpu_custom_call" | custom-call | tf_op jit(solution)/shard_map/project_local/pallas_call | solution.py:348
  89.3 4.2 %all-to-all-done.1.in_ref = bf16[16,160,256]{2,1,0:T(8,128)(2,1)S(1)} async-done(((bf16[16,160,256]{2,1,0:T(8,128)(2,1)}), bf16[16,160,256]{2,1,0:T(8,128)(2,1)S(1)}, u32[]{:S(2)}, u32[]{:S(2)}) %all-to-all-start.1) | async-done | bytes 1310752 | tf_op jit(solution)/shard_map/all_to_all | solution.py:385
  94.7 3.0 %column_attention.6.refs_0_ = bf16[16,128,256]{2,1,0:T(8,128)(2,1)} custom-call(bf16[16,160,256]{2,1,0:T(8,128)(2,1)} %copy-done.10, bf16[16,128,256]{2,1,0:T(8,128)(2,1)} %pack.5.refs_0_, f32[2,256,4096]{2,1,0:T(8,128)} %bitcast.6), custom_call_target="tpu_custom_call", output_to_operand_aliasing={{}: (1, {})} | custom-call | tf_op jit(solution)/shard_map/column_attention/pallas_call | solution.py:229
  97.6 8.0 %all-to-all-start.2 = ((bf16[16,128,256]{2,1,0:T(8,128)(2,1)}), bf16[16,128,256]{2,1,0:T(8,128)(2,1)S(1)}, u32[]{:S(2)}, u32[]{:S(2)}) async-start(bf16[16,128,256]{2,1,0:T(8,128)(2,1)} %column_attention.6.refs_0_), calls=%async_computation.2 | async-start | bytes 2097152 | tf_op jit(solution)/shard_map/all_to_all | solution.py:385
  105.7 8.1 %project.4 = (f32[128,4096]{1,0:T(8,128)}, bf16[128,4096]{1,0:T(8,128)(2,1)}) custom-call(s32[1]{0:T(128)} %bitcast.mine_ref, bf16[1024,4096]{1,0:T(8,128)(2,1)} %w_ref.9, f32[2,256,4096]{2,1,0:T(8,128)} %bitcast.7, bf16[16,160,256]{2,1,0:T(8,128)(2,1)} %copy-done.10, bf16[16,128,256]{2,1,0:T(8,128)(2,1)} %column_attention.6.refs_0_), custom_call_target="tpu_custom_call" | custom-call | tf_op jit(solution)/shard_map/project/pallas_call | solution.py:311
  113.8 1.6 collective-permute-start.5
  115.3 13.3 %all-to-all-done.2.in_ref = bf16[16,128,256]{2,1,0:T(8,128)(2,1)S(1)} async-done(((bf16[16,128,256]{2,1,0:T(8,128)(2,1)}), bf16[16,128,256]{2,1,0:T(8,128)(2,1)S(1)}, u32[]{:S(2)}, u32[]{:S(2)}) %all-to-all-start.2) | async-done | bytes 1048608 | tf_op jit(solution)/shard_map/all_to_all | solution.py:385
  128.6 2.1 %column_attention.7.refs_0_ = bf16[16,32,256]{2,1,0:T(8,128)(2,1)} custom-call(bf16[16,128,256]{2,1,0:T(8,128)(2,1)S(1)} %all-to-all-done.2.in_ref, bf16[128,4096]{1,0:T(8,128)(2,1)} %get-tuple-element.17.refs_0_), custom_call_target="tpu_custom_call" | custom-call | tf_op jit(solution)/shard_map/column_attention/pallas_call | solution.py:229
  130.7 6.9 %all-to-all-start.3 = ((bf16[16,32,256]{2,1,0:T(8,128)(2,1)}), bf16[16,32,256]{2,1,0:T(8,128)(2,1)S(1)}, u32[]{:S(2)}, u32[]{:S(2)}) async-start(bf16[16,32,256]{2,1,0:T(8,128)(2,1)} %column_attention.7.refs_0_), calls=%async_computation.3 | async-start | bytes 524288 | tf_op jit(solution)/shard_map/all_to_all | solution.py:385
  137.6 6.8 %project.5 = (f32[64,4096]{1,0:T(8,128)}, bf16[64,4096]{1,0:T(8,128)(2,1)}) custom-call(s32[1]{0:T(128)} %bitcast.mine_ref, bf16[1024,4096]{1,0:T(8,128)(2,1)} %w_ref.9, f32[2,256,4096]{2,1,0:T(8,128)} %bitcast.8, bf16[16,128,256]{2,1,0:T(8,128)(2,1)} %copy-done.2, bf16[16,32,256]{2,1,0:T(8,128)(2,1)} %column_attention.7.refs_0_), custom_call_target="tpu_custom_call" | custom-call | tf_op jit(solution)/shard_map/project/pallas_call | solution.py:311
  144.4 1.6 collective-permute-start.4
  146.0 1.6 all-to-all-done.3.in_ref
  148.3 4.6 %project.6 = (f32[64,2048]{1,0:T(8,128)}, bf16[64,2048]{1,0:T(8,128)(2,1)}) custom-call(s32[1]{0:T(128)} %bitcast.mine_ref, bf16[1024,4096]{1,0:T(8,128)(2,1)} %w_ref.9, f32[2,256,4096]{2,1,0:T(8,128)} %bitcast.9, bf16[16,32,256]{2,1,0:T(8,128)(2,1)} %copy-done.11, bf16[64,4096]{1,0:T(8,128)(2,1)} %get-tuple-element.18.refs_0_), custom_call_target="tpu_custom_call" | custom-call | tf_op jit(solution)/shard_map/project/pallas_call | solution.py:311
  153.0 1.6 collective-permute-start.3
  154.6 4.6 %project.7 = (f32[64,2048]{1,0:T(8,128)}, bf16[64,2048]{1,0:T(8,128)(2,1)}) custom-call(s32[1]{0:T(128)} %bitcast.mine_ref, bf16[1024,4096]{1,0:T(8,128)(2,1)} %w_ref.9, f32[2,256,4096]{2,1,0:T(8,128)} %bitcast.10, bf16[16,32,256]{2,1,0:T(8,128)(2,1)} %copy-done.11, bf16[64,2048]{1,0:T(8,128)(2,1)} %get-tuple-element.19.refs_0_), custom_call_target="tpu_custom_call" | custom-call | tf_op jit(solution)/shard_map/project/pallas_call | solution.py:311
  160.8 1.1 add_into.4.refs_0_
  163.2 1.8 %collective-permute-done.3.got_ref = bf16[64,2048]{1,0:T(8,128)(2,1)S(1)} collective-permute-done((bf16[64,2048]{1,0:T(8,128)(2,1)}, bf16[64,2048]{1,0:T(8,128)(2,1)S(1)}, u32[]{:S(2)}, u32[]{:S(2)}) %collective-permute-start.3) | collective-permute-done | bytes 262176 | tf_op jit(solution)/shard_map/ppermute | solution.py:30
  165.8 4.4 %collective-permute-done.2.got_ref = bf16[64,2048]{1,0:T(8,128)(2,1)S(1)} collective-permute-done((bf16[64,2048]{1,0:T(8,128)(2,1)}, bf16[64,2048]{1,0:T(8,128)(2,1)S(1)}, u32[]{:S(2)}, u32[]{:S(2)}) %collective-permute-start.2) | collective-permute-done | bytes 262176 | tf_op jit(solution)/shard_map/ppermute | solution.py:30
  (31 shorter events, 8.0 us)
Async XLA Ops:
  3.5 39.4 %all-to-all-start = ((bf16[16,192,256]{2,1,0:T(8,128)(2,1)}), bf16[16,192,256]{2,1,0:T(8,128)(2,1)S(1)}, u32[]{:S(2)}, u32[]{:S(2)}) async-start(bf16[16,192,256]{2,1,0:T(8,128)(2,1)} %pack.3.refs_0_), calls=%async_computation | async-start | bytes 3145728 | tf_op jit(solution)/shard_map/all_to_all | solution.py:385
  13.8 35.0 %collective-permute-start.1 = (bf16[2,256,1024]{2,1,0:T(8,128)(2,1)}, bf16[2,256,1024]{2,1,0:T(8,128)(2,1)}, u32[]{:S(2)}, u32[]{:S(2)}) collective-permute-start(bf16[2,256,1024]{2,1,0:T(8,128)(2,1)} %get-tuple-element.16), channel_id=1, source_target_pairs={{2,0},{4,2},{6,4},{8,6},{10,8},{12,10},{14,12},{16,14},{18,16},{20... | collective-permute-start | bytes 3145736 | tf_op jit(solution)/shard_map/ppermute | solution.py:397
  15.1 33.7 %collective-permute-start = (bf16[2,256,1024]{2,1,0:T(8,128)(2,1)}, bf16[2,256,1024]{2,1,0:T(8,128)(2,1)S(1)}, u32[]{:S(2)}, u32[]{:S(2)}) collective-permute-start(bf16[2,256,1024]{2,1,0:T(8,128)(2,1)} %get-tuple-element.15.refs_0_), channel_id=1, source_target_pairs={{0,2},{2,4},{4,6},{6,8},{8,10},{10,12},{12,14},{14,16},{16,18},{18... | collective-permute-start | bytes 3145736 | tf_op jit(solution)/shard_map/ppermute | solution.py:396
  42.9 1.1 copy-start.9
  44.0 1.3 copy-start
  47.7 1.1 copy-start.1
  48.8 3.3 %copy-start.3 = (bf16[2,256,1024]{2,1,0:T(8,128)(2,1)}, bf16[2,256,1024]{2,1,0:T(8,128)(2,1)S(1)}, u32[]{:S(2)}) copy-start(bf16[2,256,1024]{2,1,0:T(8,128)(2,1)S(1)} %collective-permute-done.refs_1_.lows_ref) | copy-start | bytes 3145732
  52.2 41.4 %all-to-all-start.1 = ((bf16[16,160,256]{2,1,0:T(8,128)(2,1)}), bf16[16,160,256]{2,1,0:T(8,128)(2,1)S(1)}, u32[]{:S(2)}, u32[]{:S(2)}) async-start(bf16[16,160,256]{2,1,0:T(8,128)(2,1)} %column_attention.5.refs_0_), calls=%async_computation.1 | async-start | bytes 2621440 | tf_op jit(solution)/shard_map/all_to_all | solution.py:385
  93.6 1.1 copy-start.10
  97.6 31.0 %all-to-all-start.2 = ((bf16[16,128,256]{2,1,0:T(8,128)(2,1)}), bf16[16,128,256]{2,1,0:T(8,128)(2,1)S(1)}, u32[]{:S(2)}, u32[]{:S(2)}) async-start(bf16[16,128,256]{2,1,0:T(8,128)(2,1)} %column_attention.6.refs_0_), calls=%async_computation.2 | async-start | bytes 2097152 | tf_op jit(solution)/shard_map/all_to_all | solution.py:385
  113.8 46.1 %collective-permute-start.5 = (bf16[128,4096]{1,0:T(8,128)(2,1)}, bf16[128,4096]{1,0:T(8,128)(2,1)S(1)}, u32[]{:S(2)}, u32[]{:S(2)}) collective-permute-start(bf16[128,4096]{1,0:T(8,128)(2,1)} %get-tuple-element.17.refs_0_), channel_id=1, source_target_pairs={{0,1},{1,0},{2,3},{3,2},{4,5},{5,4},{6,7},{7,6},{8,9},{9,8},{10,11... | collective-permute-start | bytes 3145736 | tf_op jit(solution)/shard_map/ppermute | solution.py:30
  128.6 9.0 %copy-start.2 = (bf16[16,128,256]{2,1,0:T(8,128)(2,1)}, bf16[16,128,256]{2,1,0:T(8,128)(2,1)S(1)}, u32[]{:S(2)}) copy-start(bf16[16,128,256]{2,1,0:T(8,128)(2,1)S(1)} %all-to-all-done.2.in_ref) | copy-start | bytes 3145732
  130.7 16.9 %all-to-all-start.3 = ((bf16[16,32,256]{2,1,0:T(8,128)(2,1)}), bf16[16,32,256]{2,1,0:T(8,128)(2,1)S(1)}, u32[]{:S(2)}, u32[]{:S(2)}) async-start(bf16[16,32,256]{2,1,0:T(8,128)(2,1)} %column_attention.7.refs_0_), calls=%async_computation.3 | async-start | bytes 524288 | tf_op jit(solution)/shard_map/all_to_all | solution.py:385
  144.4 17.5 %collective-permute-start.4 = (bf16[64,4096]{1,0:T(8,128)(2,1)}, bf16[64,4096]{1,0:T(8,128)(2,1)S(1)}, u32[]{:S(2)}, u32[]{:S(2)}) collective-permute-start(bf16[64,4096]{1,0:T(8,128)(2,1)} %get-tuple-element.18.refs_0_), channel_id=1, source_target_pairs={{0,1},{1,0},{2,3},{3,2},{4,5},{5,4},{6,7},{7,6},{8,9},{9,8},{10,11... | collective-permute-start | bytes 1572872 | tf_op jit(solution)/shard_map/ppermute | solution.py:30
  147.6 0.7 copy-start.11
  153.0 6.9 %copy-start.4 = (f32[128,4096]{1,0:T(8,128)S(1)}, f32[128,4096]{1,0:T(8,128)}, u32[]{:S(2)}) copy-start(f32[128,4096]{1,0:T(8,128)} %get-tuple-element.24.keep_ref) | copy-start | bytes 6291460
  153.0 12.0 %collective-permute-start.3 = (bf16[64,2048]{1,0:T(8,128)(2,1)}, bf16[64,2048]{1,0:T(8,128)(2,1)S(1)}, u32[]{:S(2)}, u32[]{:S(2)}) collective-permute-start(bf16[64,2048]{1,0:T(8,128)(2,1)} %get-tuple-element.19.refs_0_), channel_id=1, source_target_pairs={{0,1},{1,0},{2,3},{3,2},{4,5},{5,4},{6,7},{7,6},{8,9},{9,8},{10,11... | collective-permute-start | bytes 786440 | tf_op jit(solution)/shard_map/ppermute | solution.py:30
  159.2 11.0 %collective-permute-start.2 = (bf16[64,2048]{1,0:T(8,128)(2,1)}, bf16[64,2048]{1,0:T(8,128)(2,1)S(1)}, u32[]{:S(2)}, u32[]{:S(2)}) collective-permute-start(bf16[64,2048]{1,0:T(8,128)(2,1)} %get-tuple-element.21.refs_0_), channel_id=1, source_target_pairs={{0,1},{1,0},{2,3},{3,2},{4,5},{5,4},{6,7},{7,6},{8,9},{9,8},{10,11... | collective-permute-start | bytes 786440 | tf_op jit(solution)/shard_map/ppermute | solution.py:30
  159.9 1.0 copy-start.8
  160.8 1.5 copy-start.5
  162.4 2.7 %copy-start.7 = (f32[64,2048]{1,0:T(8,128)S(1)}, f32[64,2048]{1,0:T(8,128)}, u32[]{:S(2)}) copy-start(f32[64,2048]{1,0:T(8,128)} %get-tuple-element.22.keep_ref) | copy-start | bytes 1572868
  165.1 5.1 %copy-start.6 = (f32[64,2048]{1,0:T(8,128)S(1)}, f32[64,2048]{1,0:T(8,128)}, u32[]{:S(2)}) copy-start(f32[64,2048]{1,0:T(8,128)} %get-tuple-element.20.keep_ref) | copy-start | bytes 1572868

commit v4 on v3

--- a/solution.py
+++ b/solution.py
@@ -42,7 +42,7 @@
     return (out / total).astype(jnp.bfloat16)
 
 
-def band_kernel(place_ref, q_ref, k_ref, v_ref, lows_ref, highs_ref, *refs):
+def band_kernel(place_ref, q_ref, k_ref, v_ref, k_low, k_high, v_low, v_high, *refs):
     out_ref, k_all, v_all, bias = refs[-4:]
     rows = q_ref.shape[0]
     step = BAND
@@ -63,8 +63,8 @@
             bias[b, 1] = jnp.where(after, 0.0, OFF)
 
     for held, low, own, high in (
-        (k_all, lows_ref.at[0], k_ref, highs_ref.at[0]),
-        (v_all, lows_ref.at[1], v_ref, highs_ref.at[1]),
+        (k_all, k_low, k_ref, k_high),
+        (v_all, v_low, v_ref, v_high),
     ):
         held[:BAND] = low[...]
         held[BAND : BAND + rows] = own[...]
@@ -84,14 +84,14 @@
         out_ref[at] = softmax_sum(score, v_all[near])
 
 
-def band_attention(place, q, k, v, lows, highs, after=()):
+def band_attention(place, q, k, v, halos, after=()):
     rows, width = q.shape
     own = pl.BlockSpec((rows, HD), lambda h: (0, h))
-    side = pl.BlockSpec((2, BAND, HD), lambda h: (0, 0, h))
+    side = pl.BlockSpec((BAND, HD), lambda h: (0, h))
     return pl.pallas_call(
         band_kernel,
         grid=(width // HD,),
-        in_specs=[SMEM, own, own, own, side, side] + [ANY] * len(after),
+        in_specs=[SMEM, own, own, own, side, side, side, side] + [ANY] * len(after),
         out_specs=own,
         out_shape=jax.ShapeDtypeStruct(q.shape, q.dtype),
         scratch_shapes=[
@@ -102,7 +102,24 @@
         compiler_params=pltpu.CompilerParams(vmem_limit_bytes=60 * MIB),
         cost_estimate=FREE,
         name="band_attention",
-    )(place, q, k, v, lows, highs, *after)
+    )(place, q, k, v, *halos, *after)
+
+
+def tie_kernel(*refs):
+    pass
+
+
+def tie(array, *after):
+    return pl.pallas_call(
+        tie_kernel,
+        in_specs=[ANY] * (1 + len(after)),
+        out_specs=ANY,
+        out_shape=jax.ShapeDtypeStruct(array.shape, array.dtype),
+        input_output_aliases={0: 0},
+        compiler_params=pltpu.CompilerParams(vmem_limit_bytes=52 * MIB),
+        cost_estimate=FREE,
+        name="tie",
+    )(array, *after)
 
 
 def add_kernel(keep_ref, got_ref, *refs):
@@ -128,33 +145,44 @@
 
 
 def ends_kernel(k_ref, v_ref, *refs):
-    lows_ref, highs_ref = refs[-2:]
-    for t, held in enumerate((k_ref, v_ref)):
-        highs_ref[t] = held[:BAND]
-        lows_ref[t] = held[held.shape[0] - BAND :]
+    k_low, k_high, v_low, v_high = refs[-4:]
+    for held, low, high in ((k_ref, k_low, k_high), (v_ref, v_low, v_high)):
+        low[...] = held[held.shape[0] - BAND :]
+        high[...] = held[:BAND]
 
 
 def ends(k, v, after=()):
-    shape = jax.ShapeDtypeStruct((2, BAND, k.shape[1]), k.dtype)
+    shape = jax.ShapeDtypeStruct((BAND, k.shape[1]), k.dtype)
     return pl.pallas_call(
         ends_kernel,
         grid=(1,),
         in_specs=[pl.BlockSpec(k.shape, lambda n: (0, 0))] * 2 + [ANY] * len(after),
-        out_specs=[pl.BlockSpec(shape.shape, lambda n: (0, 0, 0))] * 2,
-        out_shape=[shape] * 2,
+        out_specs=[pl.BlockSpec(shape.shape, lambda n: (0, 0))] * 4,
+        out_shape=[shape] * 4,
         compiler_params=pltpu.CompilerParams(vmem_limit_bytes=60 * MIB),
         cost_estimate=FREE,
         name="ends",
     )(k, v, *after)
+
+
+def direct(low, high):
+    count = lax.axis_size("seq")
+    return (
+        lax.ppermute(low, "seq", [(i, i + 1) for i in range(count - 1)]),
+        lax.ppermute(high, "seq", [(i + 1, i) for i in range(count - 1)]),
+    )
 
 
 def pack_kernel(planes, ahead, q_ref, k_ref, v_ref, *refs):
     out_ref = refs[-1]
     lanes = out_ref.shape[-1]
     per_column, columns, _ = q_ref.shape
-    unit = pl.program_id(0)
-    for t, held in enumerate((q_ref, k_ref, v_ref)):
-        rows = [held[j].astype(jnp.float32) for j in range(per_column)]
+    many = columns // (planes * TILE)
+    for i, t in [(i, t) for i in range(many) for t in range(3)]:
+        held = (q_ref, k_ref, v_ref)[t]
+        unit = pl.program_id(0) * many + i
+        group = slice(i * planes * TILE, (i + 1) * planes * TILE)
+        rows = [held[j, group].astype(jnp.float32) for j in range(per_column)]
         at = pl.ds(pl.multiple_of(ahead + (unit * 3 + t) * PIECE, PIECE), PIECE)
         for z in range(planes):
             piece = jnp.concatenate([r[z * TILE : (z + 1) * TILE] for r in rows])
@@ -167,13 +195,13 @@
     rows, width = arrays[0].shape
     per_column = rows // STRIDE
     lanes = width // PLANE
-    columns = planes * TILE
+    columns = 2 * planes * TILE
     views = [a.reshape(per_column, STRIDE, width) for a in arrays]
     spec = pl.BlockSpec((per_column, columns, width), lambda n: (0, first // columns + n, 0))
     shape = (planes * PLANE, ahead + 3 * PIECE * units, lanes)
     return pl.pallas_call(
         functools.partial(pack_kernel, planes, ahead),
-        grid=(units,),
+        grid=(units // 2,),
         in_specs=[spec] * 3 + [ANY] * len(after),
         out_specs=pl.BlockSpec(shape, lambda n: (0, 0, 0)),
         out_shape=jax.ShapeDtypeStruct(shape, jnp.bfloat16),
@@ -390,26 +418,24 @@
     for i, (first, units) in enumerate(chunks):
         packed.append(pack(stride, first, units, ahead[i], planes, token))
         if i == 0:
-            lows, highs = ends(k_local, nearby_band_contents, tuple(packed))
-            token = (lows,)
+            k_low, k_high, v_low, v_high = ends(k_local, nearby_band_contents, tuple(packed))
+            token = (k_low,)
     packed.append(None)
-    lows = lax.ppermute(lows, "seq", [(i, i + 1) for i in range(count - 1)])
-    highs = lax.ppermute(highs, "seq", [(i + 1, i) for i in range(count - 1)])
-
-    results, after = [], (lows, highs)
+    halos = direct(k_low, k_high) + direct(v_low, v_high)
+
+    results, after = [], halos
     got = exchange(packed[0])
     for i, (first, units) in enumerate(chunks):
         if i == min(1, last):
             attn_local = band_attention(
-                place, q_local, k_local, nearby_band_contents, lows, highs, after
+                place, q_local, k_local, nearby_band_contents, halos, after
             )
             part_local = project_local(attn_local, w_local, (attn_local,))
             part_local = part_local.reshape(per_column, STRIDE, -1)
             after = (part_local,)
         if i == 0 and i < last:
-            early = units // 2
-            outs = column_attention(got, ahead[i], 0, early, packed[i + 1])
-            outs = column_attention(got, ahead[i], early, units - early, outs, after)
+            outs = column_attention(got, ahead[i], 0, units, packed[i + 1])
+            outs = tie(outs, *after)
         else:
             outs = column_attention(got, ahead[i], 0, units, packed[i + 1], after)
         after = (outs,)

time: 172 us -> 169 us (0.983)
  waiting for transfers between devices: 47.7 us -> 42.7 us
  starting transfers between devices: 46 us -> 50 us
  Pallas kernels: 69.7 us -> 66.1 us
    ppermute x2 -> x4, starting transfers between devices: 4.38 us -> 9.81 us  [the longest x2 7.24 us: direct(): lax.ppermute(low, 'seq', [(i, i + 1) for i in range(count - 1)])]
    all_to_all x4, waiting for transfers between devices: 41.5 us -> 36.5 us  [exchange(): return lax.all_to_all(a, 'seq', split_axis=0, concat_axis=0, tiled=True)]
    pallas_call x4 -> x3, Pallas kernels: 10.7 us -> 8.44 us  [column_attention(): pl.pallas_call(functools.partial(column_kernel, lo, units, ahead), in_spe...]
    unnamed x24 -> x28, local copies, waits for them, and re-layouts: 6.79 us -> 7.85 us
  transfers between devices with their start and end apart: 10 -> 12, of which waited for: 6 -> 6; matrix products, arithmetic and copies ran while one was open for 0% -> 0% of each run, Pallas kernels for 35% -> 36%
where the time goes in v4:
time: 169 us; the launch traced here: 167 us
  Pallas kernels  66.1 us (39%)
  starting transfers between devices  50 us (30%)
  waiting for transfers between devices  42.7 us (25%)
  local copies, waits for them, and re-layouts  7.85 us (5%)
    all_to_all x4, waiting for transfers between devices, exchange(): return lax.all_to_all(a, 'seq', split_axis=0, concat_axis=0, tiled=True)  36.5 us
    all_to_all x4, starting transfers between devices, exchange(): return lax.all_to_all(a, 'seq', split_axis=0, concat_axis=0, tiled=True)  34.8 us
    pallas_call x4, Pallas kernels, project(): pl.pallas_call(functools.partial(project_kernel, units, part * width), gr...  24.2 us
    pallas_call x1, Pallas kernels, band_attention(): pl.pallas_call(band_kernel, grid=(width // HD,), in_specs=[SMEM, own, own...  10.7 us
    pallas_call x1, Pallas kernels, project_local(): pl.pallas_call(local_kernel, grid=(width // step,), in_specs=[pl.BlockSpe...  9.38 us
    pallas_call x3, Pallas kernels, column_attention(): pl.pallas_call(functools.partial(column_kernel, lo, units, ahead), in_spe...  8.44 us
    unnamed x28, local copies, waits for them, and re-layouts  7.85 us
    ppermute x2, starting transfers between devices, direct(): lax.ppermute(low, 'seq', [(i, i + 1) for i in range(count - 1)])  7.24 us
  transfers between devices with their start and end apart: 12, of which 6 were waited for; matrix products, arithmetic and copies ran while one was open for 0% of the time, Pallas kernels for 36%

profile of v4, /device:TPU:0, one launch (start us, length us, event | category | flops | bytes accessed | tf_op | source)
XLA Modules:
  0.0 167.4 jit_solution(859487209588983663)
XLA Ops:
  0.0 2.5 %pack.3.refs_0_ = bf16[16,192,256]{2,1,0:T(8,128)(2,1)} custom-call(bf16[2,256,1024]{2,1,0:T(8,128)(2,1)} %bitcast.11, bf16[2,256,1024]{2,1,0:T(8,128)(2,1)} %bitcast.14, bf16[2,256,1024]{2,1,0:T(8,128)(2,1)} %bitcast.17), custom_call_target="tpu_custom_call" | custom-call | tf_op jit(solution)/shard_map/pack/pallas_call | solution.py:202
  2.5 7.4 %all-to-all-start = ((bf16[16,192,256]{2,1,0:T(8,128)(2,1)}), bf16[16,192,256]{2,1,0:T(8,128)(2,1)S(1)}, u32[]{:S(2)}, u32[]{:S(2)}) async-start(bf16[16,192,256]{2,1,0:T(8,128)(2,1)} %pack.3.refs_0_), calls=%async_computation | async-start | bytes 3145728 | tf_op jit(solution)/shard_map/all_to_all | solution.py:413
  9.9 2.9 %ends.1 = (bf16[256,1024]{1,0:T(8,128)(2,1)}, bf16[256,1024]{1,0:T(8,128)(2,1)}, bf16[256,1024]{1,0:T(8,128)(2,1)}, bf16[256,1024]{1,0:T(8,128)(2,1)}) custom-call(bf16[512,1024]{1,0:T(8,128)(2,1)} %k_ref.3, bf16[512,1024]{1,0:T(8,128)(2,1)} %v_ref.3, bf16[16,192,256]{2,1,0:T(8,128)(2,1)} %pack.3.refs_0_), custom_call_target="tpu_custom_call" | custom-call | tf_op jit(solution)/shard_map/ends/pallas_call | solution.py:156
  12.8 1.3 collective-permute-start.1
  14.1 3.1 %collective-permute-start.2 = (bf16[256,1024]{1,0:T(8,128)(2,1)}, bf16[256,1024]{1,0:T(8,128)(2,1)S(1)}, u32[]{:S(2)}, u32[]{:S(2)}) collective-permute-start(bf16[256,1024]{1,0:T(8,128)(2,1)} %get-tuple-element.19), channel_id=1, source_target_pairs={{0,2},{2,4},{4,6},{6,8},{8,10},{10,12},{12,14},{14,16},{16,18},{18... | collective-permute-start | bytes 1572872 | tf_op jit(solution)/shard_map/ppermute | solution.py:171
  17.2 1.3 collective-permute-start.3
  18.5 4.2 %collective-permute-start = (bf16[256,1024]{1,0:T(8,128)(2,1)}, bf16[256,1024]{1,0:T(8,128)(2,1)S(1)}, u32[]{:S(2)}, u32[]{:S(2)}) collective-permute-start(bf16[256,1024]{1,0:T(8,128)(2,1)} %get-tuple-element.17.refs_0_), channel_id=1, source_target_pairs={{0,2},{2,4},{4,6},{6,8},{8,10},{10,12},{12,14},{14,16},{16,18},{18... | collective-permute-start | bytes 1572872 | tf_op jit(solution)/shard_map/ppermute | solution.py:171
  22.6 2.2 %pack.4.refs_0_ = bf16[16,160,256]{2,1,0:T(8,128)(2,1)} custom-call(bf16[2,256,1024]{2,1,0:T(8,128)(2,1)} %bitcast.12, bf16[2,256,1024]{2,1,0:T(8,128)(2,1)} %bitcast.15, bf16[2,256,1024]{2,1,0:T(8,128)(2,1)} %bitcast.18, bf16[256,1024]{1,0:T(8,128)(2,1)} %get-tuple-element.17.refs_0_), custom_call_target="tpu_custom_call" | custom-call | tf_op jit(solution)/shard_map/pack/pallas_call | solution.py:202
  24.9 17.1 %all-to-all-done.in_ref = bf16[16,192,256]{2,1,0:T(8,128)(2,1)S(1)} async-done(((bf16[16,192,256]{2,1,0:T(8,128)(2,1)}), bf16[16,192,256]{2,1,0:T(8,128)(2,1)S(1)}, u32[]{:S(2)}, u32[]{:S(2)}) %all-to-all-start) | async-done | bytes 1572896 | tf_op jit(solution)/shard_map/all_to_all | solution.py:413
  43.1 1.3 copy-done
  44.4 3.4 %column_attention.3.refs_0_ = bf16[16,160,256]{2,1,0:T(8,128)(2,1)S(1)} custom-call(bf16[16,192,256]{2,1,0:T(8,128)(2,1)} %copy-done.12, bf16[16,160,256]{2,1,0:T(8,128)(2,1)S(1)} %copy-done), custom_call_target="tpu_custom_call", output_to_operand_aliasing={{}: (1, {})} | custom-call | tf_op jit(solution)/shard_map/column_attention/pallas_call | solution.py:257
  50.1 12.5 %all-to-all-start.1 = ((bf16[16,160,256]{2,1,0:T(8,128)(2,1)}), bf16[16,160,256]{2,1,0:T(8,128)(2,1)S(1)}, u32[]{:S(2)}, u32[]{:S(2)}) async-start(bf16[16,160,256]{2,1,0:T(8,128)(2,1)} %tie.1.refs_0_), calls=%async_computation.1 | async-start | bytes 2621440 | tf_op jit(solution)/shard_map/all_to_all | solution.py:413
  62.7 2.1 %pack.5.refs_0_ = bf16[16,128,256]{2,1,0:T(8,128)(2,1)} custom-call(bf16[2,256,1024]{2,1,0:T(8,128)(2,1)} %bitcast.13, bf16[2,256,1024]{2,1,0:T(8,128)(2,1)} %bitcast.16, bf16[2,256,1024]{2,1,0:T(8,128)(2,1)} %bitcast.19, bf16[256,1024]{1,0:T(8,128)(2,1)} %get-tuple-element.17.refs_0_), custom_call_target="tpu_custom_call" | custom-call | tf_op jit(solution)/shard_map/pack/pallas_call | solution.py:202
  65.4 10.7 %band_attention.1.a_ref.refs_0_ = bf16[512,1024]{1,0:T(8,128)(2,1)} custom-call(s32[2]{0:T(128)} %pad_add_fusion.place_ref, bf16[512,1024]{1,0:T(8,128)(2,1)} %q_ref.1, bf16[512,1024]{1,0:T(8,128)(2,1)} %k_ref.3, bf16[512,1024]{1,0:T(8,128)(2,1)} %v_ref.3, bf16[256,1024]{1,0:T(8,128)(2,1)} %copy-done.6, bf16[256,1024]{1,0:T(8,128)(2,1)} %copy-done.4, ...), custom_call_target="tpu_custom_call" | custom-call | tf_op jit(solution)/shard_map/band_attention/pallas_call | solution.py:91
  76.1 9.4 %project_local.1 = f32[512,4096]{1,0:T(8,128)} custom-call(bf16[512,1024]{1,0:T(8,128)(2,1)} %band_attention.1.a_ref.refs_0_, bf16[1024,4096]{1,0:T(8,128)(2,1)} %w_ref.5, bf16[512,1024]{1,0:T(8,128)(2,1)} %band_attention.1.a_ref.refs_0_), custom_call_target="tpu_custom_call" | custom-call | tf_op jit(solution)/shard_map/project_local/pallas_call | solution.py:376
  85.5 4.5 %all-to-all-done.1.in_ref = bf16[16,160,256]{2,1,0:T(8,128)(2,1)S(1)} async-done(((bf16[16,160,256]{2,1,0:T(8,128)(2,1)}), bf16[16,160,256]{2,1,0:T(8,128)(2,1)S(1)}, u32[]{:S(2)}, u32[]{:S(2)}) %all-to-all-start.1) | async-done | bytes 1310752 | tf_op jit(solution)/shard_map/all_to_all | solution.py:413
  91.2 3.0 %column_attention.4.refs_0_ = bf16[16,128,256]{2,1,0:T(8,128)(2,1)} custom-call(bf16[16,160,256]{2,1,0:T(8,128)(2,1)} %copy-done.11, bf16[16,128,256]{2,1,0:T(8,128)(2,1)} %pack.5.refs_0_, f32[2,256,4096]{2,1,0:T(8,128)} %bitcast.6), custom_call_target="tpu_custom_call", output_to_operand_aliasing={{}: (1, {})} | custom-call | tf_op jit(solution)/shard_map/column_attention/pallas_call | solution.py:257
  94.1 8.0 %all-to-all-start.2 = ((bf16[16,128,256]{2,1,0:T(8,128)(2,1)}), bf16[16,128,256]{2,1,0:T(8,128)(2,1)S(1)}, u32[]{:S(2)}, u32[]{:S(2)}) async-start(bf16[16,128,256]{2,1,0:T(8,128)(2,1)} %column_attention.4.refs_0_), calls=%async_computation.2 | async-start | bytes 2097152 | tf_op jit(solution)/shard_map/all_to_all | solution.py:413
  102.2 8.1 %project.4 = (f32[128,4096]{1,0:T(8,128)}, bf16[128,4096]{1,0:T(8,128)(2,1)}) custom-call(s32[1]{0:T(128)} %bitcast.mine_ref, bf16[1024,4096]{1,0:T(8,128)(2,1)} %w_ref.9, f32[2,256,4096]{2,1,0:T(8,128)} %bitcast.7, bf16[16,160,256]{2,1,0:T(8,128)(2,1)} %copy-done.11, bf16[16,128,256]{2,1,0:T(8,128)(2,1)} %column_attention.4.refs_0_), custom_call_target="tpu_custom_call" | custom-call | tf_op jit(solution)/shard_map/project/pallas_call | solution.py:339
  110.3 1.6 collective-permute-start.7
  111.8 13.3 %all-to-all-done.2.in_ref = bf16[16,128,256]{2,1,0:T(8,128)(2,1)S(1)} async-done(((bf16[16,128,256]{2,1,0:T(8,128)(2,1)}), bf16[16,128,256]{2,1,0:T(8,128)(2,1)S(1)}, u32[]{:S(2)}, u32[]{:S(2)}) %all-to-all-start.2) | async-done | bytes 1048608 | tf_op jit(solution)/shard_map/all_to_all | solution.py:413
  125.1 2.1 %column_attention.5.refs_0_ = bf16[16,32,256]{2,1,0:T(8,128)(2,1)} custom-call(bf16[16,128,256]{2,1,0:T(8,128)(2,1)S(1)} %all-to-all-done.2.in_ref, bf16[128,4096]{1,0:T(8,128)(2,1)} %get-tuple-element.21.refs_0_), custom_call_target="tpu_custom_call" | custom-call | tf_op jit(solution)/shard_map/column_attention/pallas_call | solution.py:257
  127.2 6.9 %all-to-all-start.3 = ((bf16[16,32,256]{2,1,0:T(8,128)(2,1)}), bf16[16,32,256]{2,1,0:T(8,128)(2,1)S(1)}, u32[]{:S(2)}, u32[]{:S(2)}) async-start(bf16[16,32,256]{2,1,0:T(8,128)(2,1)} %column_attention.5.refs_0_), calls=%async_computation.3 | async-start | bytes 524288 | tf_op jit(solution)/shard_map/all_to_all | solution.py:413
  134.1 6.8 %project.5 = (f32[64,4096]{1,0:T(8,128)}, bf16[64,4096]{1,0:T(8,128)(2,1)}) custom-call(s32[1]{0:T(128)} %bitcast.mine_ref, bf16[1024,4096]{1,0:T(8,128)(2,1)} %w_ref.9, f32[2,256,4096]{2,1,0:T(8,128)} %bitcast.8, bf16[16,128,256]{2,1,0:T(8,128)(2,1)} %copy-done.2, bf16[16,32,256]{2,1,0:T(8,128)(2,1)} %column_attention.5.refs_0_), custom_call_target="tpu_custom_call" | custom-call | tf_op jit(solution)/shard_map/project/pallas_call | solution.py:339
  140.9 1.6 collective-permute-start.6
  142.5 1.6 all-to-all-done.3.in_ref
  144.8 4.6 %project.6 = (f32[64,2048]{1,0:T(8,128)}, bf16[64,2048]{1,0:T(8,128)(2,1)}) custom-call(s32[1]{0:T(128)} %bitcast.mine_ref, bf16[1024,4096]{1,0:T(8,128)(2,1)} %w_ref.9, f32[2,256,4096]{2,1,0:T(8,128)} %bitcast.9, bf16[16,32,256]{2,1,0:T(8,128)(2,1)} %copy-done.13, bf16[64,4096]{1,0:T(8,128)(2,1)} %get-tuple-element.22.refs_0_), custom_call_target="tpu_custom_call" | custom-call | tf_op jit(solution)/shard_map/project/pallas_call | solution.py:339
  149.5 1.6 collective-permute-start.5
  151.1 4.6 %project.7 = (f32[64,2048]{1,0:T(8,128)}, bf16[64,2048]{1,0:T(8,128)(2,1)}) custom-call(s32[1]{0:T(128)} %bitcast.mine_ref, bf16[1024,4096]{1,0:T(8,128)(2,1)} %w_ref.9, f32[2,256,4096]{2,1,0:T(8,128)} %bitcast.10, bf16[16,32,256]{2,1,0:T(8,128)(2,1)} %copy-done.13, bf16[64,2048]{1,0:T(8,128)(2,1)} %get-tuple-element.23.refs_0_), custom_call_target="tpu_custom_call" | custom-call | tf_op jit(solution)/shard_map/project/pallas_call | solution.py:339
  157.3 1.1 add_into.4.refs_0_
  159.7 1.8 %collective-permute-done.5.got_ref = bf16[64,2048]{1,0:T(8,128)(2,1)S(1)} collective-permute-done((bf16[64,2048]{1,0:T(8,128)(2,1)}, bf16[64,2048]{1,0:T(8,128)(2,1)S(1)}, u32[]{:S(2)}, u32[]{:S(2)}) %collective-permute-start.5) | collective-permute-done | bytes 262176 | tf_op jit(solution)/shard_map/ppermute | solution.py:30
  162.3 4.4 %collective-permute-done.4.got_ref = bf16[64,2048]{1,0:T(8,128)(2,1)S(1)} collective-permute-done((bf16[64,2048]{1,0:T(8,128)(2,1)}, bf16[64,2048]{1,0:T(8,128)(2,1)S(1)}, u32[]{:S(2)}, u32[]{:S(2)}) %collective-permute-start.4) | collective-permute-done | bytes 262176 | tf_op jit(solution)/shard_map/ppermute | solution.py:30
  (39 shorter events, 10.2 us)
Async XLA Ops:
  2.5 39.4 %all-to-all-start = ((bf16[16,192,256]{2,1,0:T(8,128)(2,1)}), bf16[16,192,256]{2,1,0:T(8,128)(2,1)S(1)}, u32[]{:S(2)}, u32[]{:S(2)}) async-start(bf16[16,192,256]{2,1,0:T(8,128)(2,1)} %pack.3.refs_0_), calls=%async_computation | async-start | bytes 3145728 | tf_op jit(solution)/shard_map/all_to_all | solution.py:413
  12.8 36.1 %collective-permute-start.1 = (bf16[256,1024]{1,0:T(8,128)(2,1)}, bf16[256,1024]{1,0:T(8,128)(2,1)S(1)}, u32[]{:S(2)}, u32[]{:S(2)}) collective-permute-start(bf16[256,1024]{1,0:T(8,128)(2,1)} %get-tuple-element.18), channel_id=1, source_target_pairs={{2,0},{4,2},{6,4},{8,6},{10,8},{12,10},{14,12},{16,14},{18,16},{20... | collective-permute-start | bytes 1572872 | tf_op jit(solution)/shard_map/ppermute | solution.py:172
  14.1 34.9 %collective-permute-start.2 = (bf16[256,1024]{1,0:T(8,128)(2,1)}, bf16[256,1024]{1,0:T(8,128)(2,1)S(1)}, u32[]{:S(2)}, u32[]{:S(2)}) collective-permute-start(bf16[256,1024]{1,0:T(8,128)(2,1)} %get-tuple-element.19), channel_id=1, source_target_pairs={{0,2},{2,4},{4,6},{6,8},{8,10},{10,12},{12,14},{14,16},{16,18},{18... | collective-permute-start | bytes 1572872 | tf_op jit(solution)/shard_map/ppermute | solution.py:171
  17.2 31.8 %collective-permute-start.3 = (bf16[256,1024]{1,0:T(8,128)(2,1)}, bf16[256,1024]{1,0:T(8,128)(2,1)}, u32[]{:S(2)}, u32[]{:S(2)}) collective-permute-start(bf16[256,1024]{1,0:T(8,128)(2,1)} %get-tuple-element.20), channel_id=1, source_target_pairs={{2,0},{4,2},{6,4},{8,6},{10,8},{12,10},{14,12},{16,14},{18,16},{20... | collective-permute-start | bytes 1572872 | tf_op jit(solution)/shard_map/ppermute | solution.py:172
  18.5 30.5 %collective-permute-start = (bf16[256,1024]{1,0:T(8,128)(2,1)}, bf16[256,1024]{1,0:T(8,128)(2,1)S(1)}, u32[]{:S(2)}, u32[]{:S(2)}) collective-permute-start(bf16[256,1024]{1,0:T(8,128)(2,1)} %get-tuple-element.17.refs_0_), channel_id=1, source_target_pairs={{0,2},{2,4},{4,6},{6,8},{8,10},{10,12},{12,14},{14,16},{16,18},{18... | collective-permute-start | bytes 1572872 | tf_op jit(solution)/shard_map/ppermute | solution.py:171
  42.0 1.1 copy-start.12
  43.1 1.3 copy-start
  47.9 1.1 copy-start.1
  48.9 0.8 copy-start.4
  48.9 1.0 copy-start.5
  49.0 1.2 copy-start.6
  50.1 39.9 %all-to-all-start.1 = ((bf16[16,160,256]{2,1,0:T(8,128)(2,1)}), bf16[16,160,256]{2,1,0:T(8,128)(2,1)S(1)}, u32[]{:S(2)}, u32[]{:S(2)}) async-start(bf16[16,160,256]{2,1,0:T(8,128)(2,1)} %tie.1.refs_0_), calls=%async_computation.1 | async-start | bytes 2621440 | tf_op jit(solution)/shard_map/all_to_all | solution.py:413
  90.1 1.1 copy-start.11
  94.1 31.0 %all-to-all-start.2 = ((bf16[16,128,256]{2,1,0:T(8,128)(2,1)}), bf16[16,128,256]{2,1,0:T(8,128)(2,1)S(1)}, u32[]{:S(2)}, u32[]{:S(2)}) async-start(bf16[16,128,256]{2,1,0:T(8,128)(2,1)} %column_attention.4.refs_0_), calls=%async_computation.2 | async-start | bytes 2097152 | tf_op jit(solution)/shard_map/all_to_all | solution.py:413
  110.3 46.1 %collective-permute-start.7 = (bf16[128,4096]{1,0:T(8,128)(2,1)}, bf16[128,4096]{1,0:T(8,128)(2,1)S(1)}, u32[]{:S(2)}, u32[]{:S(2)}) collective-permute-start(bf16[128,4096]{1,0:T(8,128)(2,1)} %get-tuple-element.21.refs_0_), channel_id=1, source_target_pairs={{0,1},{1,0},{2,3},{3,2},{4,5},{5,4},{6,7},{7,6},{8,9},{9,8},{10,11... | collective-permute-start | bytes 3145736 | tf_op jit(solution)/shard_map/ppermute | solution.py:30
  125.1 9.0 %copy-start.2 = (bf16[16,128,256]{2,1,0:T(8,128)(2,1)}, bf16[16,128,256]{2,1,0:T(8,128)(2,1)S(1)}, u32[]{:S(2)}) copy-start(bf16[16,128,256]{2,1,0:T(8,128)(2,1)S(1)} %all-to-all-done.2.in_ref) | copy-start | bytes 3145732
  127.2 16.9 %all-to-all-start.3 = ((bf16[16,32,256]{2,1,0:T(8,128)(2,1)}), bf16[16,32,256]{2,1,0:T(8,128)(2,1)S(1)}, u32[]{:S(2)}, u32[]{:S(2)}) async-start(bf16[16,32,256]{2,1,0:T(8,128)(2,1)} %column_attention.5.refs_0_), calls=%async_computation.3 | async-start | bytes 524288 | tf_op jit(solution)/shard_map/all_to_all | solution.py:413
  140.9 17.6 %collective-permute-start.6 = (bf16[64,4096]{1,0:T(8,128)(2,1)}, bf16[64,4096]{1,0:T(8,128)(2,1)S(1)}, u32[]{:S(2)}, u32[]{:S(2)}) collective-permute-start(bf16[64,4096]{1,0:T(8,128)(2,1)} %get-tuple-element.22.refs_0_), channel_id=1, source_target_pairs={{0,1},{1,0},{2,3},{3,2},{4,5},{5,4},{6,7},{7,6},{8,9},{9,8},{10,11... | collective-permute-start | bytes 1572872 | tf_op jit(solution)/shard_map/ppermute | solution.py:30
  144.1 0.7 copy-start.13
  149.5 6.9 %copy-start.3 = (f32[128,4096]{1,0:T(8,128)S(1)}, f32[128,4096]{1,0:T(8,128)}, u32[]{:S(2)}) copy-start(f32[128,4096]{1,0:T(8,128)} %get-tuple-element.28.keep_ref) | copy-start | bytes 6291460
  149.5 12.0 %collective-permute-start.5 = (bf16[64,2048]{1,0:T(8,128)(2,1)}, bf16[64,2048]{1,0:T(8,128)(2,1)S(1)}, u32[]{:S(2)}, u32[]{:S(2)}) collective-permute-start(bf16[64,2048]{1,0:T(8,128)(2,1)} %get-tuple-element.23.refs_0_), channel_id=1, source_target_pairs={{0,1},{1,0},{2,3},{3,2},{4,5},{5,4},{6,7},{7,6},{8,9},{9,8},{10,11... | collective-permute-start | bytes 786440 | tf_op jit(solution)/shard_map/ppermute | solution.py:30
  155.7 11.0 %collective-permute-start.4 = (bf16[64,2048]{1,0:T(8,128)(2,1)}, bf16[64,2048]{1,0:T(8,128)(2,1)S(1)}, u32[]{:S(2)}, u32[]{:S(2)}) collective-permute-start(bf16[64,2048]{1,0:T(8,128)(2,1)} %get-tuple-element.25.refs_0_), channel_id=1, source_target_pairs={{0,1},{1,0},{2,3},{3,2},{4,5},{5,4},{6,7},{7,6},{8,9},{9,8},{10,11... | collective-permute-start | bytes 786440 | tf_op jit(solution)/shard_map/ppermute | solution.py:30
  156.3 1.0 copy-start.10
  157.3 1.5 copy-start.7
  158.9 2.7 %copy-start.9 = (f32[64,2048]{1,0:T(8,128)S(1)}, f32[64,2048]{1,0:T(8,128)}, u32[]{:S(2)}) copy-start(f32[64,2048]{1,0:T(8,128)} %get-tuple-element.26.keep_ref) | copy-start | bytes 1572868
  161.5 5.1 %copy-start.8 = (f32[64,2048]{1,0:T(8,128)S(1)}, f32[64,2048]{1,0:T(8,128)}, u32[]{:S(2)}) copy-start(f32[64,2048]{1,0:T(8,128)} %get-tuple-element.24.keep_ref) | copy-start | bytes 1572868

commit v5 on v4

--- a/solution.py
+++ b/solution.py
@@ -144,25 +144,24 @@
     )(keep, got, *held, *after)
 
 
-def ends_kernel(k_ref, v_ref, *refs):
-    k_low, k_high, v_low, v_high = refs[-4:]
-    for held, low, high in ((k_ref, k_low, k_high), (v_ref, v_low, v_high)):
-        low[...] = held[held.shape[0] - BAND :]
-        high[...] = held[:BAND]
-
-
-def ends(k, v, after=()):
-    shape = jax.ShapeDtypeStruct((BAND, k.shape[1]), k.dtype)
+def ends_kernel(in_ref, *refs):
+    low, high = refs[-2:]
+    low[...] = in_ref[in_ref.shape[0] - BAND :]
+    high[...] = in_ref[:BAND]
+
+
+def ends(array, after=()):
+    shape = jax.ShapeDtypeStruct((BAND, array.shape[1]), array.dtype)
     return pl.pallas_call(
         ends_kernel,
         grid=(1,),
-        in_specs=[pl.BlockSpec(k.shape, lambda n: (0, 0))] * 2 + [ANY] * len(after),
-        out_specs=[pl.BlockSpec(shape.shape, lambda n: (0, 0))] * 4,
-        out_shape=[shape] * 4,
+        in_specs=[pl.BlockSpec(array.shape, lambda n: (0, 0))] + [ANY] * len(after),
+        out_specs=[pl.BlockSpec(shape.shape, lambda n: (0, 0))] * 2,
+        out_shape=[shape] * 2,
         compiler_params=pltpu.CompilerParams(vmem_limit_bytes=60 * MIB),
         cost_estimate=FREE,
         name="ends",
-    )(k, v, *after)
+    )(array, *after)
 
 
 def direct(low, high):
@@ -418,8 +417,9 @@
     for i, (first, units) in enumerate(chunks):
         packed.append(pack(stride, first, units, ahead[i], planes, token))
         if i == 0:
-            k_low, k_high, v_low, v_high = ends(k_local, nearby_band_contents, tuple(packed))
-            token = (k_low,)
+            k_low, k_high = ends(k_local, tuple(packed))
+            v_low, v_high = ends(nearby_band_contents, (k_low,))
+            token = (v_low,)
     packed.append(None)
     halos = direct(k_low, k_high) + direct(v_low, v_high)
 
@@ -444,7 +444,7 @@
             if j < 0:
                 continue
             start, size = chunks[j]
-            parts = 2 if j == last else 1
+            parts = 2 if j >= last - 1 else 1
             for part in range(parts):
                 keep, send = project(
                     mine,

time: 169 us -> 167 us (0.988)
  waiting for transfers between devices: 42.7 us -> 35.6 us
  Pallas kernels: 66.1 us -> 70.8 us
    ppermute x4 -> x5, waiting for transfers between devices: 6.2 us -> 2.31 us  [swap(): return lax.ppermute(array, axis, [(i, i ^ mask) for i in range(count)])]
    all_to_all x4, waiting for transfers between devices: 36.5 us -> 33.3 us  [exchange(): return lax.all_to_all(a, 'seq', split_axis=0, concat_axis=0, tiled=True)]
    pallas_call x4 -> x5, Pallas kernels: 24.2 us -> 26.7 us  [project(): pl.pallas_call(functools.partial(project_kernel, units, part * width), gr...]
    pallas_call x1 -> x2, Pallas kernels: 2.88 us -> 4.46 us  [ends(): pl.pallas_call(ends_kernel, grid=(1,), in_specs=[pl.BlockSpec(array.shape...]
    pallas_call x4 -> x5, Pallas kernels: 3.52 us -> 4.13 us  [add_into(): pl.pallas_call(add_kernel, grid=(width // step,), in_specs=[spec, spec] +...]
    ppermute x4 -> x5, starting transfers between devices: 5.38 us -> 5.95 us  [swap(): return lax.ppermute(array, axis, [(i, i ^ mask) for i in range(count)])]
    unnamed x28 -> x30, local copies, waits for them, and re-layouts: 7.85 us -> 8.18 us
  transfers between devices with their start and end apart: 12 -> 13, of which waited for: 6 -> 4; matrix products, arithmetic and copies ran while one was open for 0% -> 0% of each run, Pallas kernels for 36% -> 39%
where the time goes in v5:
time: 167 us; the launch traced here: 166 us
  Pallas kernels  70.8 us (42%)
  starting transfers between devices  50.6 us (30%)
  waiting for transfers between devices  35.6 us (21%)
  local copies, waits for them, and re-layouts  8.18 us (5%)
    all_to_all x4, starting transfers between devices, exchange(): return lax.all_to_all(a, 'seq', split_axis=0, concat_axis=0, tiled=True)  34.8 us
    all_to_all x4, waiting for transfers between devices, exchange(): return lax.all_to_all(a, 'seq', split_axis=0, concat_axis=0, tiled=True)  33.3 us
    pallas_call x5, Pallas kernels, project(): pl.pallas_call(functools.partial(project_kernel, units, part * width), gr...  26.7 us
    pallas_call x1, Pallas kernels, band_attention(): pl.pallas_call(band_kernel, grid=(width // HD,), in_specs=[SMEM, own, own...  10.7 us
    pallas_call x1, Pallas kernels, project_local(): pl.pallas_call(local_kernel, grid=(width // step,), in_specs=[pl.BlockSpe...  9.43 us
    pallas_call x3, Pallas kernels, column_attention(): pl.pallas_call(functools.partial(column_kernel, lo, units, ahead), in_spe...  8.46 us
    unnamed x30, local copies, waits for them, and re-layouts  8.18 us
    ppermute x2, starting transfers between devices, direct(): lax.ppermute(low, 'seq', [(i, i + 1) for i in range(count - 1)])  7.24 us
  transfers between devices with their start and end apart: 13, of which 4 were waited for; matrix products, arithmetic and copies ran while one was open for 0% of the time, Pallas kernels for 39%

profile of v5, /device:TPU:0, one launch (start us, length us, event | category | flops | bytes accessed | tf_op | source)
XLA Modules:
  0.0 166.0 jit_solution(3038972474141616546)
XLA Ops:
  0.0 2.5 %pack.3.refs_0_ = bf16[16,192,256]{2,1,0:T(8,128)(2,1)} custom-call(bf16[2,256,1024]{2,1,0:T(8,128)(2,1)} %bitcast.12, bf16[2,256,1024]{2,1,0:T(8,128)(2,1)} %bitcast.15, bf16[2,256,1024]{2,1,0:T(8,128)(2,1)} %bitcast.18), custom_call_target="tpu_custom_call" | custom-call | tf_op jit(solution)/shard_map/pack/pallas_call | solution.py:201
  2.5 7.4 %all-to-all-start = ((bf16[16,192,256]{2,1,0:T(8,128)(2,1)}), bf16[16,192,256]{2,1,0:T(8,128)(2,1)S(1)}, u32[]{:S(2)}, u32[]{:S(2)}) async-start(bf16[16,192,256]{2,1,0:T(8,128)(2,1)} %pack.3.refs_0_), calls=%async_computation | async-start | bytes 3145728 | tf_op jit(solution)/shard_map/all_to_all | solution.py:412
  9.9 2.2 %ends.2 = (bf16[256,1024]{1,0:T(8,128)(2,1)}, bf16[256,1024]{1,0:T(8,128)(2,1)}) custom-call(bf16[512,1024]{1,0:T(8,128)(2,1)} %k_ref.1, bf16[16,192,256]{2,1,0:T(8,128)(2,1)} %pack.3.refs_0_), custom_call_target="tpu_custom_call" | custom-call | tf_op jit(solution)/shard_map/ends/pallas_call | solution.py:155
  12.1 1.3 collective-permute-start.1
  13.4 3.1 %collective-permute-start = (bf16[256,1024]{1,0:T(8,128)(2,1)}, bf16[256,1024]{1,0:T(8,128)(2,1)S(1)}, u32[]{:S(2)}, u32[]{:S(2)}) collective-permute-start(bf16[256,1024]{1,0:T(8,128)(2,1)} %get-tuple-element.19.refs_0_), channel_id=1, source_target_pairs={{0,2},{2,4},{4,6},{6,8},{8,10},{10,12},{12,14},{14,16},{16,18},{18... | collective-permute-start | bytes 1572872 | tf_op jit(solution)/shard_map/ppermute | solution.py:170
  16.5 2.2 %ends.3 = (bf16[256,1024]{1,0:T(8,128)(2,1)}, bf16[256,1024]{1,0:T(8,128)(2,1)}) custom-call(bf16[512,1024]{1,0:T(8,128)(2,1)} %v_ref.1, bf16[256,1024]{1,0:T(8,128)(2,1)} %get-tuple-element.19.refs_0_), custom_call_target="tpu_custom_call" | custom-call | tf_op jit(solution)/shard_map/ends/pallas_call | solution.py:155
  18.7 1.3 collective-permute-start.3
  20.0 4.2 %collective-permute-start.2 = (bf16[256,1024]{1,0:T(8,128)(2,1)}, bf16[256,1024]{1,0:T(8,128)(2,1)S(1)}, u32[]{:S(2)}, u32[]{:S(2)}) collective-permute-start(bf16[256,1024]{1,0:T(8,128)(2,1)} %get-tuple-element.21.refs_0_), channel_id=1, source_target_pairs={{0,2},{2,4},{4,6},{6,8},{8,10},{10,12},{12,14},{14,16},{16,18},{18... | collective-permute-start | bytes 1572872 | tf_op jit(solution)/shard_map/ppermute | solution.py:170
  24.2 2.2 %pack.4.refs_0_ = bf16[16,160,256]{2,1,0:T(8,128)(2,1)} custom-call(bf16[2,256,1024]{2,1,0:T(8,128)(2,1)} %bitcast.13, bf16[2,256,1024]{2,1,0:T(8,128)(2,1)} %bitcast.16, bf16[2,256,1024]{2,1,0:T(8,128)(2,1)} %bitcast.19, bf16[256,1024]{1,0:T(8,128)(2,1)} %get-tuple-element.21.refs_0_), custom_call_target="tpu_custom_call" | custom-call | tf_op jit(solution)/shard_map/pack/pallas_call | solution.py:201
  26.4 15.5 %all-to-all-done.in_ref = bf16[16,192,256]{2,1,0:T(8,128)(2,1)S(1)} async-done(((bf16[16,192,256]{2,1,0:T(8,128)(2,1)}), bf16[16,192,256]{2,1,0:T(8,128)(2,1)S(1)}, u32[]{:S(2)}, u32[]{:S(2)}) %all-to-all-start) | async-done | bytes 1572896 | tf_op jit(solution)/shard_map/all_to_all | solution.py:412
  43.1 1.3 copy-done
  44.4 3.4 %column_attention.3.refs_0_ = bf16[16,160,256]{2,1,0:T(8,128)(2,1)S(1)} custom-call(bf16[16,192,256]{2,1,0:T(8,128)(2,1)} %copy-done.13, bf16[16,160,256]{2,1,0:T(8,128)(2,1)S(1)} %copy-done), custom_call_target="tpu_custom_call", output_to_operand_aliasing={{}: (1, {})} | custom-call | tf_op jit(solution)/shard_map/column_attention/pallas_call | solution.py:256
  50.1 12.6 %all-to-all-start.1 = ((bf16[16,160,256]{2,1,0:T(8,128)(2,1)}), bf16[16,160,256]{2,1,0:T(8,128)(2,1)S(1)}, u32[]{:S(2)}, u32[]{:S(2)}) async-start(bf16[16,160,256]{2,1,0:T(8,128)(2,1)} %tie.1.refs_0_), calls=%async_computation.1 | async-start | bytes 2621440 | tf_op jit(solution)/shard_map/all_to_all | solution.py:412
  62.7 2.1 %pack.5.refs_0_ = bf16[16,128,256]{2,1,0:T(8,128)(2,1)} custom-call(bf16[2,256,1024]{2,1,0:T(8,128)(2,1)} %bitcast.14, bf16[2,256,1024]{2,1,0:T(8,128)(2,1)} %bitcast.17, bf16[2,256,1024]{2,1,0:T(8,128)(2,1)} %bitcast.20, bf16[256,1024]{1,0:T(8,128)(2,1)} %get-tuple-element.21.refs_0_), custom_call_target="tpu_custom_call" | custom-call | tf_op jit(solution)/shard_map/pack/pallas_call | solution.py:201
  65.4 10.7 %band_attention.1.a_ref.refs_0_ = bf16[512,1024]{1,0:T(8,128)(2,1)} custom-call(s32[2]{0:T(128)} %pad_add_fusion.place_ref, bf16[512,1024]{1,0:T(8,128)(2,1)} %q_ref.1, bf16[512,1024]{1,0:T(8,128)(2,1)} %k_ref.1, bf16[512,1024]{1,0:T(8,128)(2,1)} %v_ref.1, bf16[256,1024]{1,0:T(8,128)(2,1)} %copy-done.5, bf16[256,1024]{1,0:T(8,128)(2,1)} %copy-done.4, ...), custom_call_target="tpu_custom_call" | custom-call | tf_op jit(solution)/shard_map/band_attention/pallas_call | solution.py:91
  76.1 9.4 %project_local.1 = f32[512,4096]{1,0:T(8,128)} custom-call(bf16[512,1024]{1,0:T(8,128)(2,1)} %band_attention.1.a_ref.refs_0_, bf16[1024,4096]{1,0:T(8,128)(2,1)} %w_ref.6, bf16[512,1024]{1,0:T(8,128)(2,1)} %band_attention.1.a_ref.refs_0_), custom_call_target="tpu_custom_call" | custom-call | tf_op jit(solution)/shard_map/project_local/pallas_call | solution.py:375
  85.6 4.5 %all-to-all-done.1.in_ref = bf16[16,160,256]{2,1,0:T(8,128)(2,1)S(1)} async-done(((bf16[16,160,256]{2,1,0:T(8,128)(2,1)}), bf16[16,160,256]{2,1,0:T(8,128)(2,1)S(1)}, u32[]{:S(2)}, u32[]{:S(2)}) %all-to-all-start.1) | async-done | bytes 1310752 | tf_op jit(solution)/shard_map/all_to_all | solution.py:412
  91.2 3.0 %column_attention.4.refs_0_ = bf16[16,128,256]{2,1,0:T(8,128)(2,1)} custom-call(bf16[16,160,256]{2,1,0:T(8,128)(2,1)} %copy-done.12, bf16[16,128,256]{2,1,0:T(8,128)(2,1)} %pack.5.refs_0_, f32[2,256,4096]{2,1,0:T(8,128)} %bitcast.6), custom_call_target="tpu_custom_call", output_to_operand_aliasing={{}: (1, {})} | custom-call | tf_op jit(solution)/shard_map/column_attention/pallas_call | solution.py:256
  94.1 8.0 %all-to-all-start.2 = ((bf16[16,128,256]{2,1,0:T(8,128)(2,1)}), bf16[16,128,256]{2,1,0:T(8,128)(2,1)S(1)}, u32[]{:S(2)}, u32[]{:S(2)}) async-start(bf16[16,128,256]{2,1,0:T(8,128)(2,1)} %column_attention.4.refs_0_), calls=%async_computation.2 | async-start | bytes 2097152 | tf_op jit(solution)/shard_map/all_to_all | solution.py:412
  102.2 8.1 %project.5 = (f32[128,4096]{1,0:T(8,128)}, bf16[128,4096]{1,0:T(8,128)(2,1)}) custom-call(s32[1]{0:T(128)} %bitcast.mine_ref, bf16[1024,4096]{1,0:T(8,128)(2,1)} %w_ref.11, f32[2,256,4096]{2,1,0:T(8,128)} %bitcast.7, bf16[16,160,256]{2,1,0:T(8,128)(2,1)} %copy-done.12, bf16[16,128,256]{2,1,0:T(8,128)(2,1)} %column_attention.4.refs_0_), custom_call_target="tpu_custom_call" | custom-call | tf_op jit(solution)/shard_map/project/pallas_call | solution.py:338
  110.2 1.6 collective-permute-start.8
  111.8 13.3 %all-to-all-done.2.in_ref = bf16[16,128,256]{2,1,0:T(8,128)(2,1)S(1)} async-done(((bf16[16,128,256]{2,1,0:T(8,128)(2,1)}), bf16[16,128,256]{2,1,0:T(8,128)(2,1)S(1)}, u32[]{:S(2)}, u32[]{:S(2)}) %all-to-all-start.2) | async-done | bytes 1048608 | tf_op jit(solution)/shard_map/all_to_all | solution.py:412
  125.1 2.1 %column_attention.5.refs_0_ = bf16[16,32,256]{2,1,0:T(8,128)(2,1)} custom-call(bf16[16,128,256]{2,1,0:T(8,128)(2,1)S(1)} %all-to-all-done.2.in_ref, bf16[128,4096]{1,0:T(8,128)(2,1)} %get-tuple-element.23.refs_0_), custom_call_target="tpu_custom_call" | custom-call | tf_op jit(solution)/shard_map/column_attention/pallas_call | solution.py:256
  127.2 6.9 %all-to-all-start.3 = ((bf16[16,32,256]{2,1,0:T(8,128)(2,1)}), bf16[16,32,256]{2,1,0:T(8,128)(2,1)S(1)}, u32[]{:S(2)}, u32[]{:S(2)}) async-start(bf16[16,32,256]{2,1,0:T(8,128)(2,1)} %column_attention.5.refs_0_), calls=%async_computation.3 | async-start | bytes 524288 | tf_op jit(solution)/shard_map/all_to_all | solution.py:412
  134.1 4.7 %project.6 = (f32[64,2048]{1,0:T(8,128)}, bf16[64,2048]{1,0:T(8,128)(2,1)}) custom-call(s32[1]{0:T(128)} %bitcast.mine_ref, bf16[1024,4096]{1,0:T(8,128)(2,1)} %w_ref.11, f32[2,256,4096]{2,1,0:T(8,128)} %bitcast.8, bf16[16,128,256]{2,1,0:T(8,128)(2,1)} %copy-done.2, bf16[16,32,256]{2,1,0:T(8,128)(2,1)} %column_attention.5.refs_0_), custom_call_target="tpu_custom_call" | custom-call | tf_op jit(solution)/shard_map/project/pallas_call | solution.py:338
  138.7 1.6 collective-permute-start.7
  140.3 4.6 %project.7 = (f32[64,2048]{1,0:T(8,128)}, bf16[64,2048]{1,0:T(8,128)(2,1)}) custom-call(s32[1]{0:T(128)} %bitcast.mine_ref, bf16[1024,4096]{1,0:T(8,128)(2,1)} %w_ref.11, f32[2,256,4096]{2,1,0:T(8,128)} %bitcast.9, bf16[16,128,256]{2,1,0:T(8,128)(2,1)} %copy-done.2, bf16[64,2048]{1,0:T(8,128)(2,1)} %get-tuple-element.24.refs_0_), custom_call_target="tpu_custom_call" | custom-call | tf_op jit(solution)/shard_map/project/pallas_call | solution.py:338
  146.3 4.6 %project.8 = (f32[64,2048]{1,0:T(8,128)}, bf16[64,2048]{1,0:T(8,128)(2,1)}) custom-call(s32[1]{0:T(128)} %bitcast.mine_ref, bf16[1024,4096]{1,0:T(8,128)(2,1)} %w_ref.11, f32[2,256,4096]{2,1,0:T(8,128)} %bitcast.10, bf16[16,32,256]{2,1,0:T(8,128)(2,1)} %copy-done.14, bf16[64,2048]{1,0:T(8,128)(2,1)} %get-tuple-element.25.refs_0_), custom_call_target="tpu_custom_call" | custom-call | tf_op jit(solution)/shard_map/project/pallas_call | solution.py:338
  150.9 1.6 collective-permute-start.5
  152.5 4.7 %project.9 = (f32[64,2048]{1,0:T(8,128)}, bf16[64,2048]{1,0:T(8,128)(2,1)}) custom-call(s32[1]{0:T(128)} %bitcast.mine_ref, bf16[1024,4096]{1,0:T(8,128)(2,1)} %w_ref.11, f32[2,256,4096]{2,1,0:T(8,128)} %bitcast.11, bf16[16,32,256]{2,1,0:T(8,128)(2,1)} %copy-done.14, bf16[64,2048]{1,0:T(8,128)(2,1)} %get-tuple-element.26.refs_0_), custom_call_target="tpu_custom_call" | custom-call | tf_op jit(solution)/shard_map/project/pallas_call | solution.py:338
  158.8 1.1 add_into.5.refs_0_
  163.0 2.3 %collective-permute-done.4.got_ref = bf16[64,2048]{1,0:T(8,128)(2,1)S(1)} collective-permute-done((bf16[64,2048]{1,0:T(8,128)(2,1)}, bf16[64,2048]{1,0:T(8,128)(2,1)S(1)}, u32[]{:S(2)}, u32[]{:S(2)}) %collective-permute-start.4) | collective-permute-done | bytes 262176 | tf_op jit(solution)/shard_map/ppermute | solution.py:30
  (46 shorter events, 11.7 us)
Async XLA Ops:
  2.5 39.4 %all-to-all-start = ((bf16[16,192,256]{2,1,0:T(8,128)(2,1)}), bf16[16,192,256]{2,1,0:T(8,128)(2,1)S(1)}, u32[]{:S(2)}, u32[]{:S(2)}) async-start(bf16[16,192,256]{2,1,0:T(8,128)(2,1)} %pack.3.refs_0_), calls=%async_computation | async-start | bytes 3145728 | tf_op jit(solution)/shard_map/all_to_all | solution.py:412
  12.1 36.8 %collective-permute-start.1 = (bf16[256,1024]{1,0:T(8,128)(2,1)}, bf16[256,1024]{1,0:T(8,128)(2,1)S(1)}, u32[]{:S(2)}, u32[]{:S(2)}) collective-permute-start(bf16[256,1024]{1,0:T(8,128)(2,1)} %get-tuple-element.20), channel_id=1, source_target_pairs={{2,0},{4,2},{6,4},{8,6},{10,8},{12,10},{14,12},{16,14},{18,16},{20... | collective-permute-start | bytes 1572872 | tf_op jit(solution)/shard_map/ppermute | solution.py:171
  13.4 35.5 %collective-permute-start = (bf16[256,1024]{1,0:T(8,128)(2,1)}, bf16[256,1024]{1,0:T(8,128)(2,1)S(1)}, u32[]{:S(2)}, u32[]{:S(2)}) collective-permute-start(bf16[256,1024]{1,0:T(8,128)(2,1)} %get-tuple-element.19.refs_0_), channel_id=1, source_target_pairs={{0,2},{2,4},{4,6},{6,8},{8,10},{10,12},{12,14},{14,16},{16,18},{18... | collective-permute-start | bytes 1572872 | tf_op jit(solution)/shard_map/ppermute | solution.py:170
  18.7 30.2 %collective-permute-start.3 = (bf16[256,1024]{1,0:T(8,128)(2,1)}, bf16[256,1024]{1,0:T(8,128)(2,1)}, u32[]{:S(2)}, u32[]{:S(2)}) collective-permute-start(bf16[256,1024]{1,0:T(8,128)(2,1)} %get-tuple-element.22), channel_id=1, source_target_pairs={{2,0},{4,2},{6,4},{8,6},{10,8},{12,10},{14,12},{16,14},{18,16},{20... | collective-permute-start | bytes 1572872 | tf_op jit(solution)/shard_map/ppermute | solution.py:171
  20.0 29.0 %collective-permute-start.2 = (bf16[256,1024]{1,0:T(8,128)(2,1)}, bf16[256,1024]{1,0:T(8,128)(2,1)S(1)}, u32[]{:S(2)}, u32[]{:S(2)}) collective-permute-start(bf16[256,1024]{1,0:T(8,128)(2,1)} %get-tuple-element.21.refs_0_), channel_id=1, source_target_pairs={{0,2},{2,4},{4,6},{6,8},{8,10},{10,12},{12,14},{14,16},{16,18},{18... | collective-permute-start | bytes 1572872 | tf_op jit(solution)/shard_map/ppermute | solution.py:170
  42.0 1.1 copy-start.13
  43.1 1.3 copy-start
  47.9 1.1 copy-start.1
  48.9 0.8 copy-start.4
  48.9 1.0 copy-start.5
  49.0 1.1 copy-start.6
  50.1 40.0 %all-to-all-start.1 = ((bf16[16,160,256]{2,1,0:T(8,128)(2,1)}), bf16[16,160,256]{2,1,0:T(8,128)(2,1)S(1)}, u32[]{:S(2)}, u32[]{:S(2)}) async-start(bf16[16,160,256]{2,1,0:T(8,128)(2,1)} %tie.1.refs_0_), calls=%async_computation.1 | async-start | bytes 2621440 | tf_op jit(solution)/shard_map/all_to_all | solution.py:412
  90.1 1.1 copy-start.12
  94.1 31.0 %all-to-all-start.2 = ((bf16[16,128,256]{2,1,0:T(8,128)(2,1)}), bf16[16,128,256]{2,1,0:T(8,128)(2,1)S(1)}, u32[]{:S(2)}, u32[]{:S(2)}) async-start(bf16[16,128,256]{2,1,0:T(8,128)(2,1)} %column_attention.4.refs_0_), calls=%async_computation.2 | async-start | bytes 2097152 | tf_op jit(solution)/shard_map/all_to_all | solution.py:412
  110.2 47.6 %collective-permute-start.8 = (bf16[128,4096]{1,0:T(8,128)(2,1)}, bf16[128,4096]{1,0:T(8,128)(2,1)S(1)}, u32[]{:S(2)}, u32[]{:S(2)}) collective-permute-start(bf16[128,4096]{1,0:T(8,128)(2,1)} %get-tuple-element.23.refs_0_), channel_id=1, source_target_pairs={{0,1},{1,0},{2,3},{3,2},{4,5},{5,4},{6,7},{7,6},{8,9},{9,8},{10,11... | collective-permute-start | bytes 3145736 | tf_op jit(solution)/shard_map/ppermute | solution.py:30
  125.1 9.0 %copy-start.2 = (bf16[16,128,256]{2,1,0:T(8,128)(2,1)}, bf16[16,128,256]{2,1,0:T(8,128)(2,1)S(1)}, u32[]{:S(2)}) copy-start(bf16[16,128,256]{2,1,0:T(8,128)(2,1)S(1)} %all-to-all-done.2.in_ref) | copy-start | bytes 3145732
  127.2 18.4 %all-to-all-start.3 = ((bf16[16,32,256]{2,1,0:T(8,128)(2,1)}), bf16[16,32,256]{2,1,0:T(8,128)(2,1)S(1)}, u32[]{:S(2)}, u32[]{:S(2)}) async-start(bf16[16,32,256]{2,1,0:T(8,128)(2,1)} %column_attention.5.refs_0_), calls=%async_computation.3 | async-start | bytes 524288 | tf_op jit(solution)/shard_map/all_to_all | solution.py:412
  138.7 21.2 %collective-permute-start.7 = (bf16[64,2048]{1,0:T(8,128)(2,1)}, bf16[64,2048]{1,0:T(8,128)(2,1)S(1)}, u32[]{:S(2)}, u32[]{:S(2)}) collective-permute-start(bf16[64,2048]{1,0:T(8,128)(2,1)} %get-tuple-element.24.refs_0_), channel_id=1, source_target_pairs={{0,1},{1,0},{2,3},{3,2},{4,5},{5,4},{6,7},{7,6},{8,9},{9,8},{10,11... | collective-permute-start | bytes 786440 | tf_op jit(solution)/shard_map/ppermute | solution.py:30
  145.0 15.7 %collective-permute-start.6 = (bf16[64,2048]{1,0:T(8,128)(2,1)}, bf16[64,2048]{1,0:T(8,128)(2,1)S(1)}, u32[]{:S(2)}, u32[]{:S(2)}) collective-permute-start(bf16[64,2048]{1,0:T(8,128)(2,1)} %get-tuple-element.25.refs_0_), channel_id=1, source_target_pairs={{0,1},{1,0},{2,3},{3,2},{4,5},{5,4},{6,7},{7,6},{8,9},{9,8},{10,11... | collective-permute-start | bytes 786440 | tf_op jit(solution)/shard_map/ppermute | solution.py:30
  145.5 0.7 copy-start.14
  150.9 6.9 %copy-start.3 = (f32[128,4096]{1,0:T(8,128)S(1)}, f32[128,4096]{1,0:T(8,128)}, u32[]{:S(2)}) copy-start(f32[128,4096]{1,0:T(8,128)} %get-tuple-element.32.keep_ref) | copy-start | bytes 6291460
  150.9 10.9 %collective-permute-start.5 = (bf16[64,2048]{1,0:T(8,128)(2,1)}, bf16[64,2048]{1,0:T(8,128)(2,1)S(1)}, u32[]{:S(2)}, u32[]{:S(2)}) collective-permute-start(bf16[64,2048]{1,0:T(8,128)(2,1)} %get-tuple-element.26.refs_0_), channel_id=1, source_target_pairs={{0,1},{1,0},{2,3},{3,2},{4,5},{5,4},{6,7},{7,6},{8,9},{9,8},{10,11... | collective-permute-start | bytes 786440 | tf_op jit(solution)/shard_map/ppermute | solution.py:30
  157.2 8.1 %collective-permute-start.4 = (bf16[64,2048]{1,0:T(8,128)(2,1)}, bf16[64,2048]{1,0:T(8,128)(2,1)S(1)}, u32[]{:S(2)}, u32[]{:S(2)}) collective-permute-start(bf16[64,2048]{1,0:T(8,128)(2,1)} %get-tuple-element.28.refs_0_), channel_id=1, source_target_pairs={{0,1},{1,0},{2,3},{3,2},{4,5},{5,4},{6,7},{7,6},{8,9},{9,8},{10,11... | collective-permute-start | bytes 786440 | tf_op jit(solution)/shard_map/ppermute | solution.py:30
  157.8 1.0 copy-start.11
  158.8 1.1 copy-start.8
  159.9 1.1 copy-start.7
  161.1 1.1 copy-start.10
  162.2 3.1 %copy-start.9 = (f32[64,2048]{1,0:T(8,128)S(1)}, f32[64,2048]{1,0:T(8,128)}, u32[]{:S(2)}) copy-start(f32[64,2048]{1,0:T(8,128)} %get-tuple-element.27.keep_ref) | copy-start | bytes 1572868

commit v6 on v5

--- a/solution.py
+++ b/solution.py
@@ -13,6 +13,7 @@
 PLANE = 4
 TILE = 8
 PIECE = 16
+BLOCK = 512
 ROUNDS = ((0, 4), (128, 2), (192, 2))
 OFF = -1e30
 SCALE = HD**-0.5
@@ -298,62 +299,83 @@
     ]
 
 
-def project_kernel(units, begin, mine_ref, w_ref, local_ref, in_ref, *refs):
-    keep_ref, send_ref, rows_ref, sum_ref, held, sems = refs[-6:]
-    stream(pl.program_id(0), w_ref, held, sems, begin)
-
-    @pl.when(pl.program_id(0) == 0)
-    def _():
-        count, _, lanes = in_ref.shape
-        planes = count // PLANE
-        columns = planes * TILE
-        chunk = units * columns
-        for u in range(units):
-            for p in range(PLANE):
-                pieces = [
-                    in_ref[z * PLANE + p, u * PIECE : (u + 1) * PIECE].astype(jnp.float32)
-                    for z in range(planes)
-                ]
-                for j in range(PIECE // TILE):
-                    part = jnp.concatenate([x[j * TILE : (j + 1) * TILE] for x in pieces])
-                    row = j * chunk + u * columns
-                    lane = slice(p * lanes, (p + 1) * lanes)
-                    rows_ref[row : row + columns, lane] = part.astype(jnp.bfloat16)
-
-    w = held[pl.program_id(0)]
-    total = jnp.dot(rows_ref[...], w, preferred_element_type=jnp.float32)
-    sum_ref[...] = total.reshape(sum_ref.shape) + local_ref[...]
+def project_kernel(units, first, begin, mine_ref, w_ref, local_ref, in_ref, *refs):
+    keep_ref, send_ref, rows_ref, got, local, held, keep, send, sems = refs[-9:]
+    count, _, lanes = got.shape
+    planes = count // PLANE
+    columns = planes * TILE
+    chunk = units * columns
+    blocks, _, width = held.shape
+
+    fetch = pltpu.make_async_copy(in_ref.at[:, pl.ds(0, units * PIECE)], got, sems.at[4 * blocks])
+    fetch.start()
+
+    def copies(n):
+        at = pl.ds(begin + n * width, width)
+        to = pl.ds(n * width, width)
+        rows = pl.ds(first, chunk)
+        pairs = (
+            (w_ref.at[:, at], held.at[n]),
+            (local_ref.at[:, rows, at], local.at[n]),
+            (keep.at[n], keep_ref.at[:, to]),
+            (send.at[n], send_ref.at[:, to]),
+        )
+        return [
+            pltpu.make_async_copy(a, b, sems.at[k * blocks + n]) for k, (a, b) in enumerate(pairs)
+        ]
+
+    for n in range(blocks):
+        for copy in copies(n)[:2]:
+            copy.start()
+    fetch.wait()
+    for u in range(units):
+        for p in range(PLANE):
+            pieces = [
+                got[z * PLANE + p, u * PIECE : (u + 1) * PIECE].astype(jnp.float32)
+                for z in range(planes)
+            ]
+            for j in range(PIECE // TILE):
+                part = jnp.concatenate([x[j * TILE : (j + 1) * TILE] for x in pieces])
+                row = j * chunk + u * columns
+                lane = slice(p * lanes, (p + 1) * lanes)
+                rows_ref[row : row + columns, lane] = part.astype(jnp.bfloat16)
     mine = mine_ref[0]
-    keep_ref[...] = sum_ref[mine]
-    send_ref[...] = sum_ref[1 - mine].astype(jnp.bfloat16)
+    for n in range(blocks):
+        for copy in copies(n)[:2]:
+            copy.wait()
+        total = jnp.dot(rows_ref[...], held[n], preferred_element_type=jnp.float32)
+        low = total[:chunk] + local[n, 0]
+        high = total[chunk:] + local[n, 1]
+        keep[n] = jnp.where(mine == 0, low, high)
+        send[n] = jnp.where(mine == 0, high, low).astype(jnp.bfloat16)
+        for copy in copies(n)[2:]:
+            copy.start()
+    for n in range(blocks):
+        for copy in copies(n)[2:]:
+            copy.wait()
 
 
 def project(mine, got, w, local, first, units, chunk, part, parts, after=()):
     depth = w.shape[0]
     width = w.shape[1] // parts
     count, _, lanes = got.shape
-    per_column = local.shape[0]
-    step = 1024
-    steps = width // step
-    return pl.pallas_call(
-        functools.partial(project_kernel, units, part * width),
-        grid=(width // step,),
-        in_specs=[
-            SMEM,
-            ANY,
-            pl.BlockSpec((per_column, chunk, step), lambda n: (0, first // chunk, part * steps + n)),
-            pl.BlockSpec((count, units * PIECE, lanes), lambda n: (0, 0, 0)),
-        ]
-        + [ANY] * len(after),
-        out_specs=[pl.BlockSpec((chunk, step), lambda n: (0, n))] * 2,
+    blocks = width // BLOCK
+    return pl.pallas_call(
+        functools.partial(project_kernel, units, first, part * width),
+        in_specs=[SMEM] + [ANY] * (3 + len(after)),
+        out_specs=[ANY, ANY],
         out_shape=[
             jax.ShapeDtypeStruct((chunk, width), jnp.float32),
             jax.ShapeDtypeStruct((chunk, width), jnp.bfloat16),
         ],
         scratch_shapes=[
             pltpu.VMEM((2 * chunk, depth), jnp.bfloat16),
-            pltpu.VMEM((2, chunk, step), jnp.float32),
-            *stream_scratch(depth, width, step),
+            pltpu.VMEM((count, units * PIECE, lanes), jnp.bfloat16),
+            pltpu.VMEM((blocks, 2, chunk, BLOCK), jnp.float32),
+            pltpu.VMEM((blocks, depth, BLOCK), jnp.bfloat16),
+            pltpu.VMEM((blocks, chunk, BLOCK), jnp.float32),
+            pltpu.VMEM((blocks, chunk, BLOCK), jnp.bfloat16),
+            pltpu.SemaphoreType.DMA((4 * blocks + 1,)),
         ],
         compiler_params=pltpu.CompilerParams(vmem_limit_bytes=58 * MIB),
         cost_estimate=FREE,

time: 167 us -> 165 us (0.988)
  Pallas kernels: 70.8 us -> 66 us
  waiting for transfers between devices: 35.6 us -> 38.8 us
    pallas_call x5, Pallas kernels: 26.7 us -> 21.9 us  [project(): pl.pallas_call(functools.partial(project_kernel, units, first, part * wid...]
  transfers between devices with their start and end apart: 13 -> 13, of which waited for: 4 -> 5; matrix products, arithmetic and copies ran while one was open for 0% -> 0% of each run, Pallas kernels for 39% -> 36%
where the time goes in v6:
time: 165 us; the launch traced here: 164 us
  Pallas kernels  66 us (40%)
  starting transfers between devices  50.6 us (31%)
  waiting for transfers between devices  38.8 us (24%)
  local copies, waits for them, and re-layouts  8.18 us (5%)
    all_to_all x4, starting transfers between devices, exchange(): return lax.all_to_all(a, 'seq', split_axis=0, concat_axis=0, tiled=True)  34.8 us
    all_to_all x4, waiting for transfers between devices, exchange(): return lax.all_to_all(a, 'seq', split_axis=0, concat_axis=0, tiled=True)  34.8 us
    pallas_call x5, Pallas kernels, project(): pl.pallas_call(functools.partial(project_kernel, units, first, part * wid...  21.9 us
    pallas_call x1, Pallas kernels, band_attention(): pl.pallas_call(band_kernel, grid=(width // HD,), in_specs=[SMEM, own, own...  10.7 us
    pallas_call x1, Pallas kernels, project_local(): pl.pallas_call(local_kernel, grid=(width // step,), in_specs=[pl.BlockSpe...  9.43 us
    pallas_call x3, Pallas kernels, column_attention(): pl.pallas_call(functools.partial(column_kernel, lo, units, ahead), in_spe...  8.45 us
    unnamed x30, local copies, waits for them, and re-layouts  8.18 us
    ppermute x2, starting transfers between devices, direct(): lax.ppermute(low, 'seq', [(i, i + 1) for i in range(count - 1)])  7.24 us
  transfers between devices with their start and end apart: 13, of which 5 were waited for; matrix products, arithmetic and copies ran while one was open for 0% of the time, Pallas kernels for 36%

profile of v6, /device:TPU:0, one launch (start us, length us, event | category | flops | bytes accessed | tf_op | source)
XLA Modules:
  0.0 164.3 jit_solution(1314309701501667176)
XLA Ops:
  0.0 2.5 %pack.3.refs_0_ = bf16[16,192,256]{2,1,0:T(8,128)(2,1)} custom-call(bf16[2,256,1024]{2,1,0:T(8,128)(2,1)} %bitcast.12, bf16[2,256,1024]{2,1,0:T(8,128)(2,1)} %bitcast.15, bf16[2,256,1024]{2,1,0:T(8,128)(2,1)} %bitcast.18), custom_call_target="tpu_custom_call" | custom-call | tf_op jit(solution)/shard_map/pack/pallas_call | solution.py:202
  2.5 7.4 %all-to-all-start = ((bf16[16,192,256]{2,1,0:T(8,128)(2,1)}), bf16[16,192,256]{2,1,0:T(8,128)(2,1)S(1)}, u32[]{:S(2)}, u32[]{:S(2)}) async-start(bf16[16,192,256]{2,1,0:T(8,128)(2,1)} %pack.3.refs_0_), calls=%async_computation | async-start | bytes 3145728 | tf_op jit(solution)/shard_map/all_to_all | solution.py:434
  9.9 2.2 %ends.2 = (bf16[256,1024]{1,0:T(8,128)(2,1)}, bf16[256,1024]{1,0:T(8,128)(2,1)}) custom-call(bf16[512,1024]{1,0:T(8,128)(2,1)} %k_ref.1, bf16[16,192,256]{2,1,0:T(8,128)(2,1)} %pack.3.refs_0_), custom_call_target="tpu_custom_call" | custom-call | tf_op jit(solution)/shard_map/ends/pallas_call | solution.py:156
  12.1 1.3 collective-permute-start.1
  13.4 3.1 %collective-permute-start = (bf16[256,1024]{1,0:T(8,128)(2,1)}, bf16[256,1024]{1,0:T(8,128)(2,1)S(1)}, u32[]{:S(2)}, u32[]{:S(2)}) collective-permute-start(bf16[256,1024]{1,0:T(8,128)(2,1)} %get-tuple-element.19.refs_0_), channel_id=1, source_target_pairs={{0,2},{2,4},{4,6},{6,8},{8,10},{10,12},{12,14},{14,16},{16,18},{18... | collective-permute-start | bytes 1572872 | tf_op jit(solution)/shard_map/ppermute | solution.py:171
  16.5 2.2 %ends.3 = (bf16[256,1024]{1,0:T(8,128)(2,1)}, bf16[256,1024]{1,0:T(8,128)(2,1)}) custom-call(bf16[512,1024]{1,0:T(8,128)(2,1)} %v_ref.1, bf16[256,1024]{1,0:T(8,128)(2,1)} %get-tuple-element.19.refs_0_), custom_call_target="tpu_custom_call" | custom-call | tf_op jit(solution)/shard_map/ends/pallas_call | solution.py:156
  18.7 1.3 collective-permute-start.3
  20.0 4.2 %collective-permute-start.2 = (bf16[256,1024]{1,0:T(8,128)(2,1)}, bf16[256,1024]{1,0:T(8,128)(2,1)S(1)}, u32[]{:S(2)}, u32[]{:S(2)}) collective-permute-start(bf16[256,1024]{1,0:T(8,128)(2,1)} %get-tuple-element.21.refs_0_), channel_id=1, source_target_pairs={{0,2},{2,4},{4,6},{6,8},{8,10},{10,12},{12,14},{14,16},{16,18},{18... | collective-permute-start | bytes 1572872 | tf_op jit(solution)/shard_map/ppermute | solution.py:171
  24.2 2.2 %pack.4.refs_0_ = bf16[16,160,256]{2,1,0:T(8,128)(2,1)} custom-call(bf16[2,256,1024]{2,1,0:T(8,128)(2,1)} %bitcast.13, bf16[2,256,1024]{2,1,0:T(8,128)(2,1)} %bitcast.16, bf16[2,256,1024]{2,1,0:T(8,128)(2,1)} %bitcast.19, bf16[256,1024]{1,0:T(8,128)(2,1)} %get-tuple-element.21.refs_0_), custom_call_target="tpu_custom_call" | custom-call | tf_op jit(solution)/shard_map/pack/pallas_call | solution.py:202
  26.4 15.5 %all-to-all-done.in_ref = bf16[16,192,256]{2,1,0:T(8,128)(2,1)S(1)} async-done(((bf16[16,192,256]{2,1,0:T(8,128)(2,1)}), bf16[16,192,256]{2,1,0:T(8,128)(2,1)S(1)}, u32[]{:S(2)}, u32[]{:S(2)}) %all-to-all-start) | async-done | bytes 1572896 | tf_op jit(solution)/shard_map/all_to_all | solution.py:434
  43.1 1.3 copy-done
  44.4 3.4 %column_attention.3.refs_0_ = bf16[16,160,256]{2,1,0:T(8,128)(2,1)S(1)} custom-call(bf16[16,192,256]{2,1,0:T(8,128)(2,1)} %copy-done.13, bf16[16,160,256]{2,1,0:T(8,128)(2,1)S(1)} %copy-done), custom_call_target="tpu_custom_call", output_to_operand_aliasing={{}: (1, {})} | custom-call | tf_op jit(solution)/shard_map/column_attention/pallas_call | solution.py:257
  50.1 12.6 %all-to-all-start.1 = ((bf16[16,160,256]{2,1,0:T(8,128)(2,1)}), bf16[16,160,256]{2,1,0:T(8,128)(2,1)S(1)}, u32[]{:S(2)}, u32[]{:S(2)}) async-start(bf16[16,160,256]{2,1,0:T(8,128)(2,1)} %tie.1.refs_0_), calls=%async_computation.1 | async-start | bytes 2621440 | tf_op jit(solution)/shard_map/all_to_all | solution.py:434
  62.7 2.1 %pack.5.refs_0_ = bf16[16,128,256]{2,1,0:T(8,128)(2,1)} custom-call(bf16[2,256,1024]{2,1,0:T(8,128)(2,1)} %bitcast.14, bf16[2,256,1024]{2,1,0:T(8,128)(2,1)} %bitcast.17, bf16[2,256,1024]{2,1,0:T(8,128)(2,1)} %bitcast.20, bf16[256,1024]{1,0:T(8,128)(2,1)} %get-tuple-element.21.refs_0_), custom_call_target="tpu_custom_call" | custom-call | tf_op jit(solution)/shard_map/pack/pallas_call | solution.py:202
  65.4 10.7 %band_attention.1.a_ref.refs_0_ = bf16[512,1024]{1,0:T(8,128)(2,1)} custom-call(s32[2]{0:T(128)} %pad_add_fusion.place_ref, bf16[512,1024]{1,0:T(8,128)(2,1)} %q_ref.1, bf16[512,1024]{1,0:T(8,128)(2,1)} %k_ref.1, bf16[512,1024]{1,0:T(8,128)(2,1)} %v_ref.1, bf16[256,1024]{1,0:T(8,128)(2,1)} %copy-done.5, bf16[256,1024]{1,0:T(8,128)(2,1)} %copy-done.4, ...), custom_call_target="tpu_custom_call" | custom-call | tf_op jit(solution)/shard_map/band_attention/pallas_call | solution.py:92
  76.1 9.4 %project_local.1 = f32[512,4096]{1,0:T(8,128)} custom-call(bf16[512,1024]{1,0:T(8,128)(2,1)} %band_attention.1.a_ref.refs_0_, bf16[1024,4096]{1,0:T(8,128)(2,1)} %w_ref.6, bf16[512,1024]{1,0:T(8,128)(2,1)} %band_attention.1.a_ref.refs_0_), custom_call_target="tpu_custom_call" | custom-call | tf_op jit(solution)/shard_map/project_local/pallas_call | solution.py:397
  85.6 4.5 %all-to-all-done.1.in_ref = bf16[16,160,256]{2,1,0:T(8,128)(2,1)S(1)} async-done(((bf16[16,160,256]{2,1,0:T(8,128)(2,1)}), bf16[16,160,256]{2,1,0:T(8,128)(2,1)S(1)}, u32[]{:S(2)}, u32[]{:S(2)}) %all-to-all-start.1) | async-done | bytes 1310752 | tf_op jit(solution)/shard_map/all_to_all | solution.py:434
  91.2 3.0 %column_attention.4.refs_0_ = bf16[16,128,256]{2,1,0:T(8,128)(2,1)} custom-call(bf16[16,160,256]{2,1,0:T(8,128)(2,1)} %copy-done.12, bf16[16,128,256]{2,1,0:T(8,128)(2,1)} %pack.5.refs_0_, f32[2,256,4096]{2,1,0:T(8,128)} %bitcast.6), custom_call_target="tpu_custom_call", output_to_operand_aliasing={{}: (1, {})} | custom-call | tf_op jit(solution)/shard_map/column_attention/pallas_call | solution.py:257
  94.1 8.0 %all-to-all-start.2 = ((bf16[16,128,256]{2,1,0:T(8,128)(2,1)}), bf16[16,128,256]{2,1,0:T(8,128)(2,1)S(1)}, u32[]{:S(2)}, u32[]{:S(2)}) async-start(bf16[16,128,256]{2,1,0:T(8,128)(2,1)} %column_attention.4.refs_0_), calls=%async_computation.2 | async-start | bytes 2097152 | tf_op jit(solution)/shard_map/all_to_all | solution.py:434
  102.2 7.0 %project.5 = (f32[128,4096]{1,0:T(8,128)}, bf16[128,4096]{1,0:T(8,128)(2,1)}) custom-call(s32[1]{0:T(128)} %bitcast.mine_ref, bf16[1024,4096]{1,0:T(8,128)(2,1)} %w_ref.11, f32[2,256,4096]{2,1,0:T(8,128)} %bitcast.7, bf16[16,160,256]{2,1,0:T(8,128)(2,1)} %copy-done.12, bf16[16,128,256]{2,1,0:T(8,128)(2,1)} %column_attention.4.refs_0_), custom_call_target="tpu_custom_call" | custom-call | tf_op jit(solution)/shard_map/project/pallas_call | solution.py:363
  109.2 1.6 collective-permute-start.8
  110.7 14.4 %all-to-all-done.2.in_ref = bf16[16,128,256]{2,1,0:T(8,128)(2,1)S(1)} async-done(((bf16[16,128,256]{2,1,0:T(8,128)(2,1)}), bf16[16,128,256]{2,1,0:T(8,128)(2,1)S(1)}, u32[]{:S(2)}, u32[]{:S(2)}) %all-to-all-start.2) | async-done | bytes 1048608 | tf_op jit(solution)/shard_map/all_to_all | solution.py:434
  125.1 2.1 %column_attention.5.refs_0_ = bf16[16,32,256]{2,1,0:T(8,128)(2,1)} custom-call(bf16[16,128,256]{2,1,0:T(8,128)(2,1)S(1)} %all-to-all-done.2.in_ref, bf16[128,4096]{1,0:T(8,128)(2,1)} %get-tuple-element.23.refs_0_), custom_call_target="tpu_custom_call" | custom-call | tf_op jit(solution)/shard_map/column_attention/pallas_call | solution.py:257
  127.2 6.9 %all-to-all-start.3 = ((bf16[16,32,256]{2,1,0:T(8,128)(2,1)}), bf16[16,32,256]{2,1,0:T(8,128)(2,1)S(1)}, u32[]{:S(2)}, u32[]{:S(2)}) async-start(bf16[16,32,256]{2,1,0:T(8,128)(2,1)} %column_attention.5.refs_0_), calls=%async_computation.3 | async-start | bytes 524288 | tf_op jit(solution)/shard_map/all_to_all | solution.py:434
  134.1 3.7 %project.6 = (f32[64,2048]{1,0:T(8,128)}, bf16[64,2048]{1,0:T(8,128)(2,1)}) custom-call(s32[1]{0:T(128)} %bitcast.mine_ref, bf16[1024,4096]{1,0:T(8,128)(2,1)} %w_ref.11, f32[2,256,4096]{2,1,0:T(8,128)} %bitcast.8, bf16[16,128,256]{2,1,0:T(8,128)(2,1)} %copy-done.2, bf16[16,32,256]{2,1,0:T(8,128)(2,1)} %column_attention.5.refs_0_), custom_call_target="tpu_custom_call" | custom-call | tf_op jit(solution)/shard_map/project/pallas_call | solution.py:363
  137.8 1.6 collective-permute-start.7
  139.4 3.7 %project.7 = (f32[64,2048]{1,0:T(8,128)}, bf16[64,2048]{1,0:T(8,128)(2,1)}) custom-call(s32[1]{0:T(128)} %bitcast.mine_ref, bf16[1024,4096]{1,0:T(8,128)(2,1)} %w_ref.11, f32[2,256,4096]{2,1,0:T(8,128)} %bitcast.9, bf16[16,128,256]{2,1,0:T(8,128)(2,1)} %copy-done.2, bf16[64,2048]{1,0:T(8,128)(2,1)} %get-tuple-element.24.refs_0_), custom_call_target="tpu_custom_call" | custom-call | tf_op jit(solution)/shard_map/project/pallas_call | solution.py:363
  144.8 3.7 %project.8 = (f32[64,2048]{1,0:T(8,128)}, bf16[64,2048]{1,0:T(8,128)(2,1)}) custom-call(s32[1]{0:T(128)} %bitcast.mine_ref, bf16[1024,4096]{1,0:T(8,128)(2,1)} %w_ref.11, f32[2,256,4096]{2,1,0:T(8,128)} %bitcast.10, bf16[16,32,256]{2,1,0:T(8,128)(2,1)} %copy-done.14, bf16[64,2048]{1,0:T(8,128)(2,1)} %get-tuple-element.25.refs_0_), custom_call_target="tpu_custom_call" | custom-call | tf_op jit(solution)/shard_map/project/pallas_call | solution.py:363
  148.6 1.6 collective-permute-start.5
  150.2 3.7 %project.9 = (f32[64,2048]{1,0:T(8,128)}, bf16[64,2048]{1,0:T(8,128)(2,1)}) custom-call(s32[1]{0:T(128)} %bitcast.mine_ref, bf16[1024,4096]{1,0:T(8,128)(2,1)} %w_ref.11, f32[2,256,4096]{2,1,0:T(8,128)} %bitcast.11, bf16[16,32,256]{2,1,0:T(8,128)(2,1)} %copy-done.14, bf16[64,2048]{1,0:T(8,128)(2,1)} %get-tuple-element.26.refs_0_), custom_call_target="tpu_custom_call" | custom-call | tf_op jit(solution)/shard_map/project/pallas_call | solution.py:363
  155.5 1.1 add_into.5.refs_0_
  159.7 3.9 %collective-permute-done.4.got_ref = bf16[64,2048]{1,0:T(8,128)(2,1)S(1)} collective-permute-done((bf16[64,2048]{1,0:T(8,128)(2,1)}, bf16[64,2048]{1,0:T(8,128)(2,1)S(1)}, u32[]{:S(2)}, u32[]{:S(2)}) %collective-permute-start.4) | collective-permute-done | bytes 262176 | tf_op jit(solution)/shard_map/ppermute | solution.py:31
  (46 shorter events, 12.1 us)
Async XLA Ops:
  2.5 39.4 %all-to-all-start = ((bf16[16,192,256]{2,1,0:T(8,128)(2,1)}), bf16[16,192,256]{2,1,0:T(8,128)(2,1)S(1)}, u32[]{:S(2)}, u32[]{:S(2)}) async-start(bf16[16,192,256]{2,1,0:T(8,128)(2,1)} %pack.3.refs_0_), calls=%async_computation | async-start | bytes 3145728 | tf_op jit(solution)/shard_map/all_to_all | solution.py:434
  12.1 36.8 %collective-permute-start.1 = (bf16[256,1024]{1,0:T(8,128)(2,1)}, bf16[256,1024]{1,0:T(8,128)(2,1)S(1)}, u32[]{:S(2)}, u32[]{:S(2)}) collective-permute-start(bf16[256,1024]{1,0:T(8,128)(2,1)} %get-tuple-element.20), channel_id=1, source_target_pairs={{2,0},{4,2},{6,4},{8,6},{10,8},{12,10},{14,12},{16,14},{18,16},{20... | collective-permute-start | bytes 1572872 | tf_op jit(solution)/shard_map/ppermute | solution.py:172
  13.4 35.5 %collective-permute-start = (bf16[256,1024]{1,0:T(8,128)(2,1)}, bf16[256,1024]{1,0:T(8,128)(2,1)S(1)}, u32[]{:S(2)}, u32[]{:S(2)}) collective-permute-start(bf16[256,1024]{1,0:T(8,128)(2,1)} %get-tuple-element.19.refs_0_), channel_id=1, source_target_pairs={{0,2},{2,4},{4,6},{6,8},{8,10},{10,12},{12,14},{14,16},{16,18},{18... | collective-permute-start | bytes 1572872 | tf_op jit(solution)/shard_map/ppermute | solution.py:171
  18.7 30.2 %collective-permute-start.3 = (bf16[256,1024]{1,0:T(8,128)(2,1)}, bf16[256,1024]{1,0:T(8,128)(2,1)}, u32[]{:S(2)}, u32[]{:S(2)}) collective-permute-start(bf16[256,1024]{1,0:T(8,128)(2,1)} %get-tuple-element.22), channel_id=1, source_target_pairs={{2,0},{4,2},{6,4},{8,6},{10,8},{12,10},{14,12},{16,14},{18,16},{20... | collective-permute-start | bytes 1572872 | tf_op jit(solution)/shard_map/ppermute | solution.py:172
  20.0 28.9 %collective-permute-start.2 = (bf16[256,1024]{1,0:T(8,128)(2,1)}, bf16[256,1024]{1,0:T(8,128)(2,1)S(1)}, u32[]{:S(2)}, u32[]{:S(2)}) collective-permute-start(bf16[256,1024]{1,0:T(8,128)(2,1)} %get-tuple-element.21.refs_0_), channel_id=1, source_target_pairs={{0,2},{2,4},{4,6},{6,8},{8,10},{10,12},{12,14},{14,16},{16,18},{18... | collective-permute-start | bytes 1572872 | tf_op jit(solution)/shard_map/ppermute | solution.py:171
  42.0 1.1 copy-start.13
  43.1 1.3 copy-start
  47.9 1.1 copy-start.1
  48.9 0.8 copy-start.4
  48.9 1.0 copy-start.5
  49.0 1.1 copy-start.6
  50.1 40.0 %all-to-all-start.1 = ((bf16[16,160,256]{2,1,0:T(8,128)(2,1)}), bf16[16,160,256]{2,1,0:T(8,128)(2,1)S(1)}, u32[]{:S(2)}, u32[]{:S(2)}) async-start(bf16[16,160,256]{2,1,0:T(8,128)(2,1)} %tie.1.refs_0_), calls=%async_computation.1 | async-start | bytes 2621440 | tf_op jit(solution)/shard_map/all_to_all | solution.py:434
  90.1 1.1 copy-start.12
  94.1 31.0 %all-to-all-start.2 = ((bf16[16,128,256]{2,1,0:T(8,128)(2,1)}), bf16[16,128,256]{2,1,0:T(8,128)(2,1)S(1)}, u32[]{:S(2)}, u32[]{:S(2)}) async-start(bf16[16,128,256]{2,1,0:T(8,128)(2,1)} %column_attention.4.refs_0_), calls=%async_computation.2 | async-start | bytes 2097152 | tf_op jit(solution)/shard_map/all_to_all | solution.py:434
  109.2 45.4 %collective-permute-start.8 = (bf16[128,4096]{1,0:T(8,128)(2,1)}, bf16[128,4096]{1,0:T(8,128)(2,1)S(1)}, u32[]{:S(2)}, u32[]{:S(2)}) collective-permute-start(bf16[128,4096]{1,0:T(8,128)(2,1)} %get-tuple-element.23.refs_0_), channel_id=1, source_target_pairs={{0,1},{1,0},{2,3},{3,2},{4,5},{5,4},{6,7},{7,6},{8,9},{9,8},{10,11... | collective-permute-start | bytes 3145736 | tf_op jit(solution)/shard_map/ppermute | solution.py:31
  125.1 9.0 %copy-start.2 = (bf16[16,128,256]{2,1,0:T(8,128)(2,1)}, bf16[16,128,256]{2,1,0:T(8,128)(2,1)S(1)}, u32[]{:S(2)}) copy-start(bf16[16,128,256]{2,1,0:T(8,128)(2,1)S(1)} %all-to-all-done.2.in_ref) | copy-start | bytes 3145732
  127.2 16.9 %all-to-all-start.3 = ((bf16[16,32,256]{2,1,0:T(8,128)(2,1)}), bf16[16,32,256]{2,1,0:T(8,128)(2,1)S(1)}, u32[]{:S(2)}, u32[]{:S(2)}) async-start(bf16[16,32,256]{2,1,0:T(8,128)(2,1)} %column_attention.5.refs_0_), calls=%async_computation.3 | async-start | bytes 524288 | tf_op jit(solution)/shard_map/all_to_all | solution.py:434
  137.8 18.8 %collective-permute-start.7 = (bf16[64,2048]{1,0:T(8,128)(2,1)}, bf16[64,2048]{1,0:T(8,128)(2,1)S(1)}, u32[]{:S(2)}, u32[]{:S(2)}) collective-permute-start(bf16[64,2048]{1,0:T(8,128)(2,1)} %get-tuple-element.24.refs_0_), channel_id=1, source_target_pairs={{0,1},{1,0},{2,3},{3,2},{4,5},{5,4},{6,7},{7,6},{8,9},{9,8},{10,11... | collective-permute-start | bytes 786440 | tf_op jit(solution)/shard_map/ppermute | solution.py:31
  143.1 14.3 %collective-permute-start.6 = (bf16[64,2048]{1,0:T(8,128)(2,1)}, bf16[64,2048]{1,0:T(8,128)(2,1)S(1)}, u32[]{:S(2)}, u32[]{:S(2)}) collective-permute-start(bf16[64,2048]{1,0:T(8,128)(2,1)} %get-tuple-element.25.refs_0_), channel_id=1, source_target_pairs={{0,1},{1,0},{2,3},{3,2},{4,5},{5,4},{6,7},{7,6},{8,9},{9,8},{10,11... | collective-permute-start | bytes 786440 | tf_op jit(solution)/shard_map/ppermute | solution.py:31
  144.1 0.7 copy-start.14
  148.6 5.9 %copy-start.3 = (f32[128,4096]{1,0:T(8,128)S(1)}, f32[128,4096]{1,0:T(8,128)}, u32[]{:S(2)}) copy-start(f32[128,4096]{1,0:T(8,128)} %get-tuple-element.32.keep_ref) | copy-start | bytes 6291460
  148.6 10.0 %collective-permute-start.5 = (bf16[64,2048]{1,0:T(8,128)(2,1)}, bf16[64,2048]{1,0:T(8,128)(2,1)S(1)}, u32[]{:S(2)}, u32[]{:S(2)}) collective-permute-start(bf16[64,2048]{1,0:T(8,128)(2,1)} %get-tuple-element.26.refs_0_), channel_id=1, source_target_pairs={{0,1},{1,0},{2,3},{3,2},{4,5},{5,4},{6,7},{7,6},{8,9},{9,8},{10,11... | collective-permute-start | bytes 786440 | tf_op jit(solution)/shard_map/ppermute | solution.py:31
  153.9 9.7 %collective-permute-start.4 = (bf16[64,2048]{1,0:T(8,128)(2,1)}, bf16[64,2048]{1,0:T(8,128)(2,1)S(1)}, u32[]{:S(2)}, u32[]{:S(2)}) collective-permute-start(bf16[64,2048]{1,0:T(8,128)(2,1)} %get-tuple-element.28.refs_0_), channel_id=1, source_target_pairs={{0,1},{1,0},{2,3},{3,2},{4,5},{5,4},{6,7},{7,6},{8,9},{9,8},{10,11... | collective-permute-start | bytes 786440 | tf_op jit(solution)/shard_map/ppermute | solution.py:31
  154.5 1.0 copy-start.11
  155.5 1.1 copy-start.8
  156.6 1.1 copy-start.7
  157.8 1.1 copy-start.10
  158.9 4.7 %copy-start.9 = (f32[64,2048]{1,0:T(8,128)S(1)}, f32[64,2048]{1,0:T(8,128)}, u32[]{:S(2)}) copy-start(f32[64,2048]{1,0:T(8,128)} %get-tuple-element.27.keep_ref) | copy-start | bytes 1572868
